TPU v7x, 32 devices: a whole 2x2x4 slice. The times are simulated.
32 devices in a mesh: seq: 4 (over z), ctx: 8 (over y, x, core).
Axes of the slice: x: 2, y: 2, z: 4, core: 2. Of those that a mesh axis runs over, the one named last changes fastest.
Arguments:
- tokens: bfloat16 [6144, 2048], P(('seq', 'ctx')), may hold values from -6 to 6
- segments: int32 [4, 1536], P('seq', 'ctx'), may hold values from 0 to 7, as said below
- cotangent: bfloat16 [6144, 2048], P(('seq', 'ctx')), may hold values from -6 to 6
- attention_gain: bfloat16 [2048], P(('seq', 'ctx')), may hold values from 0.5 to 1.5
- query_weight: bfloat16 [2048, 2048], P(('seq', 'ctx')), may hold values from -0.1875 to 0.1875
- key_weight: bfloat16 [2048, 256], P(('seq', 'ctx')), may hold values from -0.1875 to 0.1875
- value_weight: bfloat16 [2048, 256], P(('seq', 'ctx')), may hold values from -0.125 to 0.125
- projection: bfloat16 [2048, 2048], P(('seq', 'ctx')), may hold values from -0.5 to 0.5
- feedforward_gain: bfloat16 [2048], P(('seq', 'ctx')), may hold values from 0.5 to 1.5
- gate_weight: bfloat16 [2048, 5632], P(('seq', 'ctx')), may hold values from -0.125 to 0.125
- up_weight: bfloat16 [2048, 5632], P(('seq', 'ctx')), may hold values from -0.125 to 0.125
- down_weight: bfloat16 [5632, 2048], P(('seq', 'ctx')), may hold values from -0.078125 to 0.078125
Outputs:
- block_out: bfloat16 [6144, 2048], P(('seq', 'ctx'))
- grad_tokens: float32 [6144, 2048], P(('seq', 'ctx'))
- grad_attention: float32 [2048], P(('seq', 'ctx'))
- grad_query: float32 [2048, 2048], P(('seq', 'ctx'))
- grad_key: float32 [2048, 256], P(('seq', 'ctx'))
- grad_value: float32 [2048, 256], P(('seq', 'ctx'))
- grad_projection: float32 [2048, 2048], P(('seq', 'ctx'))
- grad_feedforward: float32 [2048], P(('seq', 'ctx'))
- grad_gate: float32 [2048, 5632], P(('seq', 'ctx'))
- grad_up: float32 [2048, 5632], P(('seq', 'ctx'))
- grad_down: float32 [5632, 2048], P(('seq', 'ctx'))
Inputs may be any that keep to these rules, and one draw needn't show every extreme that they name: `segments`: segment numbers count documents from 0 along each sequence. One sequence, chosen by the seed, is a single document. Another, also chosen by the seed, is packed with documents of exactly 200 tokens. In the others the documents have 200 to 2000 tokens. In every sequence the last document may be shorter.
All inputs are finite; a program needn't handle non-finite values.
Results may differ from a plain program's by a relative error of at most 0.017.
Values may be sent and summed in bfloat16 or wider, within the bound.
No kernel may reach another device: no remote copies, remote signals or barrier semaphores. Data moves between devices by JAX's collectives and lax.ppermute only.
A program may use at most 384 MiB of HBM per device.

v0:
```python
import jax
import jax.numpy as jnp
from jax import lax
from jax.sharding import PartitionSpec as P

H = 32
KV = 4
HD = 64


EPSILON = 1e-05
MASKED = -1e30


def normalize_rows(values, scaling):
    factor = lax.rsqrt(jnp.mean(values * values, axis=-1, keepdims=True) + EPSILON)
    return (values * factor * scaling, factor)


def normalize_back(values, factor, scaling, upstream):
    shaped = upstream * scaling
    grad_scaling = jnp.sum(upstream * values * factor, axis=0)
    inner_mean = jnp.mean(shaped * values, axis=-1, keepdims=True)
    return (factor * shaped - values * factor * factor * factor * inner_mean, grad_scaling)


def rotate_heads(source, cosine, sine_part, head_count):
    row_count = source.shape[0]
    halves = source.reshape(row_count, head_count, 2, HD // 2)
    first_half = halves[:, :, 0]
    second_half = halves[:, :, 1]
    cos_part = cosine[:, None, :]
    sin_part = sine_part[:, None, :]
    turned = jnp.stack(
        [
            first_half * cos_part - second_half * sin_part,
            second_half * cos_part + first_half * sin_part,
        ],
        axis=2,
    )
    return turned.reshape(row_count, head_count * HD)


def local_dot(left, right):
    return jnp.dot(left, right, preferred_element_type=jnp.float32)


def outer_sum(left, right):
    return jnp.einsum("ti,to->io", left, right, preferred_element_type=jnp.float32)


def back_dot(left, right):
    return jnp.einsum("to,io->ti", left, right, preferred_element_type=jnp.float32)


def arrange_queries(source):
    row_count = source.shape[0]
    return (
        source.reshape(row_count, KV, H // KV, HD)
        .transpose(1, 2, 0, 3)
        .reshape(KV, H // KV * row_count, HD)
    )


def restore_queries(source, row_count):
    return (
        source.reshape(KV, H // KV, row_count, HD).transpose(2, 0, 1, 3).reshape(row_count, H * HD)
    )


def arrange_keys(source, block_size):
    return source.reshape(source.shape[0] // block_size, block_size, KV, HD).transpose(0, 2, 1, 3)


def restore_keys(source):
    return source.transpose(0, 2, 1, 3).reshape(source.shape[0] * source.shape[2], KV * HD)


def allowed_block(query_place, query_segment, key_place, key_segment):
    allowed = (key_segment[None, :] == query_segment[:, None]) & (
        key_place[None, :] <= query_place[:, None]
    )
    return jnp.tile(allowed, (H // KV, 1))


def block_scores(arranged, key_block, allowed):
    scores = jnp.einsum(
        "gre,gke->grk", arranged, key_block, preferred_element_type=jnp.float32
    ) * HD ** (-0.5)
    return jnp.where(allowed[None], scores, MASKED)


def body(
    tokens,
    segments,
    cotangent,
    attention_gain,
    query_weight,
    key_weight,
    value_weight,
    projection,
    feedforward_gain,
    gate_weight,
    up_weight,
    down_weight,
):
    local_count = tokens.shape[0]
    length = local_count * lax.axis_size("ctx")
    block_size = 256
    block_count = length // block_size
    offset = lax.axis_index("ctx") * local_count
    seg_all = lax.all_gather(segments, "ctx", axis=1, tiled=True)[0]
    place_all = jnp.arange(length, dtype=jnp.int32)
    starts = jnp.concatenate([jnp.ones((1,), dtype=jnp.bool_), seg_all[1:] != seg_all[:-1]])
    positions = place_all - lax.cummax(jnp.where(starts, place_all, 0), axis=0)
    local_pos = lax.dynamic_slice_in_dim(positions, offset, local_count)
    local_seg = lax.dynamic_slice_in_dim(seg_all, offset, local_count)
    query_place = offset + jnp.arange(local_count, dtype=jnp.int32)
    freqs = jnp.power(10000.0, -jnp.arange(HD // 2, dtype=jnp.float32) * (2.0 / HD))
    angles = local_pos.astype(jnp.float32)[:, None] * freqs[None, :]
    cosine = jnp.cos(angles)
    sine_part = jnp.sin(angles)
    key_places = place_all.reshape(block_count, block_size)
    key_segs = seg_all.reshape(block_count, block_size)
    gain_one, wide_query, wide_key, wide_value, wide_projection = (
        lax.all_gather(attention_gain, ("seq", "ctx"), axis=0, tiled=True),
        lax.all_gather(query_weight, ("seq", "ctx"), axis=0, tiled=True),
        lax.all_gather(key_weight, ("seq", "ctx"), axis=0, tiled=True),
        lax.all_gather(value_weight, ("seq", "ctx"), axis=0, tiled=True),
        lax.all_gather(projection, ("seq", "ctx"), axis=0, tiled=True),
    )
    inputs = tokens.astype(jnp.float32)
    gain_first = gain_one.astype(jnp.float32)
    normed_float, factor_first = normalize_rows(inputs, gain_first)
    normed = normed_float.astype(jnp.bfloat16)
    query_low = rotate_heads(local_dot(normed, wide_query), cosine, sine_part, H).astype(
        jnp.bfloat16
    )
    key_low = rotate_heads(local_dot(normed, wide_key), cosine, sine_part, KV).astype(jnp.bfloat16)
    value_low = local_dot(normed, wide_value).astype(jnp.bfloat16)
    all_keys, all_values = (
        lax.all_gather(key_low, "ctx", axis=0, tiled=True),
        lax.all_gather(value_low, "ctx", axis=0, tiled=True),
    )
    arranged = arrange_queries(query_low)
    row_total = H // KV * local_count
    key_blocks = arrange_keys(all_keys, block_size)
    value_blocks = arrange_keys(all_values, block_size)

    def max_step(carry, pieces):
        running_max, running_sum = carry
        key_block, place_block, seg_block = pieces
        scores = block_scores(
            arranged, key_block, allowed_block(query_place, local_seg, place_block, seg_block)
        )
        new_max = jnp.maximum(running_max, jnp.max(scores, axis=-1))
        new_sum = running_sum * jnp.exp(running_max - new_max) + jnp.sum(
            jnp.exp(scores - new_max[..., None]), axis=-1
        )
        return ((new_max, new_sum), None)

    start_max = jnp.full((KV, row_total), MASKED, jnp.float32)
    start_sum = jnp.zeros((KV, row_total), jnp.float32)
    (row_max, row_sum), unused = lax.scan(
        max_step, (start_max, start_sum), (key_blocks, key_places, key_segs)
    )

    def mix_step(total, pieces):
        key_block, value_block, place_block, seg_block = pieces
        scores = block_scores(
            arranged, key_block, allowed_block(query_place, local_seg, place_block, seg_block)
        )
        probs = (jnp.exp(scores - row_max[..., None]) / row_sum[..., None]).astype(jnp.bfloat16)
        return (
            total
            + jnp.einsum("grk,gke->gre", probs, value_block, preferred_element_type=jnp.float32),
            None,
        )

    attended_full, unused = lax.scan(
        mix_step,
        jnp.zeros((KV, row_total, HD), jnp.float32),
        (key_blocks, value_blocks, key_places, key_segs),
    )
    attended_low = restore_queries(attended_full, local_count).astype(jnp.bfloat16)
    hidden = inputs + local_dot(attended_low, wide_projection)
    gain_two, wide_gate, wide_up, wide_down = (
        lax.all_gather(feedforward_gain, ("seq", "ctx"), axis=0, tiled=True),
        lax.all_gather(gate_weight, ("seq", "ctx"), axis=0, tiled=True),
        lax.all_gather(up_weight, ("seq", "ctx"), axis=0, tiled=True),
        lax.all_gather(down_weight, ("seq", "ctx"), axis=0, tiled=True),
    )
    gain_second = gain_two.astype(jnp.float32)
    normed_two_float, factor_second = normalize_rows(hidden, gain_second)
    normed_two = normed_two_float.astype(jnp.bfloat16)
    gate = local_dot(normed_two, wide_gate)
    upward = local_dot(normed_two, wide_up)
    sigmoid_gate = jax.nn.sigmoid(gate)
    swished = gate * sigmoid_gate
    activated = (swished * upward).astype(jnp.bfloat16)
    block_out = (hidden + local_dot(activated, wide_down)).astype(jnp.bfloat16)
    wide_gate, wide_up, wide_down = (
        lax.all_gather(gate_weight, ("seq", "ctx"), axis=0, tiled=True),
        lax.all_gather(up_weight, ("seq", "ctx"), axis=0, tiled=True),
        lax.all_gather(down_weight, ("seq", "ctx"), axis=0, tiled=True),
    )
    upstream = cotangent.astype(jnp.float32)
    grad_down_part = outer_sum(activated, cotangent)
    grad_act = back_dot(cotangent, wide_down)
    grad_gate_in = (grad_act * upward * sigmoid_gate * (1.0 + gate * (1.0 - sigmoid_gate))).astype(
        jnp.bfloat16
    )
    grad_up_in = (grad_act * swished).astype(jnp.bfloat16)
    grad_normed_two = back_dot(grad_gate_in, wide_gate) + back_dot(grad_up_in, wide_up)
    grad_hidden_norm, grad_gain_two = normalize_back(
        hidden, factor_second, gain_second, grad_normed_two
    )
    grad_hidden = upstream + grad_hidden_norm
    grad_gate_part = outer_sum(normed_two, grad_gate_in)
    grad_up_part = outer_sum(normed_two, grad_up_in)
    grad_feedforward, grad_gate, grad_up, grad_down = (
        lax.psum_scatter(grad_gain_two, ("seq", "ctx"), scatter_dimension=0, tiled=True),
        lax.psum_scatter(grad_gate_part, ("seq", "ctx"), scatter_dimension=0, tiled=True),
        lax.psum_scatter(grad_up_part, ("seq", "ctx"), scatter_dimension=0, tiled=True),
        lax.psum_scatter(grad_down_part, ("seq", "ctx"), scatter_dimension=0, tiled=True),
    )
    wide_query, wide_key, wide_value, wide_projection = (
        lax.all_gather(query_weight, ("seq", "ctx"), axis=0, tiled=True),
        lax.all_gather(key_weight, ("seq", "ctx"), axis=0, tiled=True),
        lax.all_gather(value_weight, ("seq", "ctx"), axis=0, tiled=True),
        lax.all_gather(projection, ("seq", "ctx"), axis=0, tiled=True),
    )
    grad_branch = grad_hidden.astype(jnp.bfloat16)
    grad_projection = outer_sum(attended_low, grad_branch)
    grad_attended = back_dot(grad_branch, wide_projection).astype(jnp.bfloat16)
    arranged_grad = arrange_queries(grad_attended)
    delta = jnp.sum(arranged_grad.astype(jnp.float32) * attended_full, axis=-1)

    def back_step(grad_rows, pieces):
        key_block, value_block, place_block, seg_block = pieces
        scores = block_scores(
            arranged, key_block, allowed_block(query_place, local_seg, place_block, seg_block)
        )
        probs = jnp.exp(scores - row_max[..., None]) / row_sum[..., None]
        grad_value_block = jnp.einsum(
            "grk,gre->gke",
            probs.astype(jnp.bfloat16),
            arranged_grad,
            preferred_element_type=jnp.float32,
        )
        grad_probs = jnp.einsum(
            "gre,gke->grk", arranged_grad, value_block, preferred_element_type=jnp.float32
        )
        grad_scores = (probs * (grad_probs - delta[..., None])).astype(jnp.bfloat16)
        grad_rows = grad_rows + jnp.einsum(
            "grk,gke->gre", grad_scores, key_block, preferred_element_type=jnp.float32
        ) * HD ** (-0.5)
        grad_key_block = jnp.einsum(
            "grk,gre->gke", grad_scores, arranged, preferred_element_type=jnp.float32
        ) * HD ** (-0.5)
        return (grad_rows, (grad_key_block, grad_value_block))

    grad_query_rows, (key_parts, value_parts) = lax.scan(
        back_step,
        jnp.zeros((KV, row_total, HD), jnp.float32),
        (key_blocks, value_blocks, key_places, key_segs),
    )
    grad_key_local, grad_value_local = (
        lax.psum_scatter(
            restore_keys(key_parts).astype(jnp.bfloat16), "ctx", scatter_dimension=0, tiled=True
        ).astype(jnp.float32),
        lax.psum_scatter(
            restore_keys(value_parts).astype(jnp.bfloat16), "ctx", scatter_dimension=0, tiled=True
        ).astype(jnp.float32),
    )
    grad_query_in = rotate_heads(
        restore_queries(grad_query_rows, local_count), cosine, -sine_part, H
    ).astype(jnp.bfloat16)
    grad_key_in = rotate_heads(grad_key_local, cosine, -sine_part, KV).astype(jnp.bfloat16)
    grad_value_in = grad_value_local.astype(jnp.bfloat16)
    grad_normed = (
        back_dot(grad_query_in, wide_query)
        + back_dot(grad_key_in, wide_key)
        + back_dot(grad_value_in, wide_value)
    )
    grad_input_norm, grad_gain_one = normalize_back(inputs, factor_first, gain_first, grad_normed)
    grad_tokens = grad_hidden + grad_input_norm
    grad_attention, grad_query, grad_key, grad_value, grad_projection = (
        lax.psum_scatter(grad_gain_one, ("seq", "ctx"), scatter_dimension=0, tiled=True),
        lax.psum_scatter(
            outer_sum(normed, grad_query_in), ("seq", "ctx"), scatter_dimension=0, tiled=True
        ),
        lax.psum_scatter(
            outer_sum(normed, grad_key_in), ("seq", "ctx"), scatter_dimension=0, tiled=True
        ),
        lax.psum_scatter(
            outer_sum(normed, grad_value_in), ("seq", "ctx"), scatter_dimension=0, tiled=True
        ),
        lax.psum_scatter(grad_projection, ("seq", "ctx"), scatter_dimension=0, tiled=True),
    )
    return (
        block_out,
        grad_tokens,
        grad_attention,
        grad_query,
        grad_key,
        grad_value,
        grad_projection,
        grad_feedforward,
        grad_gate,
        grad_up,
        grad_down,
    )


def solution(mesh):
    in_specs = (
        P(("seq", "ctx"), None),
        P("seq", "ctx"),
        P(("seq", "ctx"), None),
        P(("seq", "ctx")),
        P(("seq", "ctx"), None),
        P(("seq", "ctx"), None),
        P(("seq", "ctx"), None),
        P(("seq", "ctx"), None),
        P(("seq", "ctx")),
        P(("seq", "ctx"), None),
        P(("seq", "ctx"), None),
        P(("seq", "ctx"), None),
    )
    out_specs = (
        P(("seq", "ctx"), None),
        P(("seq", "ctx"), None),
        P(("seq", "ctx")),
        P(("seq", "ctx"), None),
        P(("seq", "ctx"), None),
        P(("seq", "ctx"), None),
        P(("seq", "ctx"), None),
        P(("seq", "ctx")),
        P(("seq", "ctx"), None),
        P(("seq", "ctx"), None),
        P(("seq", "ctx"), None),
    )
    return jax.shard_map(body, mesh=mesh, in_specs=in_specs, out_specs=out_specs, check_vma=False)
```

profile of v0, /device:TPU:0, one launch (start us, length us, event | category | flops | bytes accessed | tf_op | source)
XLA Modules:
  0.0 3087.3 jit_solution(11206587899117896703)
XLA Ops:
  13.6 9.6 all-reduce
  23.7 39.7 %all-reduce.6 = (bf16[2048]{0:T(1024)(128)(2,1)S(1)}, bf16[2048]{0:T(1024)(128)(2,1)S(1)}) all-reduce(bf16[2048]{0:T(1024)(128)(2,1)S(1)} %dynamic-update-slice.1, bf16[2048]{0:T(1024)(128)(2,1)S(1)} %dynamic-update-slice.2), channel_id=1, replica_groups=mesh['seq'=4,'ctx'=8] {'seq','ctx'}, use_global_device_ids=true, to_apply=%add.1 | all-reduce | flops 4096 | bytes 16384
  69.5 10.3 all_gather.46
  81.1 41.9 %all-gather.12.cloned.1.call-done = bf16[2048,256]{1,0:T(8,128)(2,1)} async-done(((bf16[64,256]{1,0:T(8,128)(2,1)}), bf16[2048,256]{1,0:T(8,128)(2,1)}) %all-gather.12.cloned.1.call-update) | async-done | bytes 1048592 | tf_op jit(solution)/shard_map/all_gather | solution.py:129
  124.7 10.5 all_gather.49
  139.4 63.0 %all-gather.10.cloned.1.call-done = bf16[2048,2048]{1,0:T(8,128)(2,1)} async-done(((bf16[64,2048]{1,0:T(8,128)(2,1)}), bf16[2048,2048]{1,0:T(8,128)(2,1)}) %all-gather.10.cloned.1.call-update) | async-done | bytes 8388624 | tf_op jit(solution)/shard_map/all_gather | solution.py:127
  213.3 53.8 %while.39 = (s32[]{:T(128)}, f32[4,1536]{1,0:T(4,128)S(1)}, f32[4,1536]{1,0:T(4,128)S(1)}, s32[6,256]{1,0:T(8,128)S(1)}, s32[192]{0:T(256)S(1)}, /*index=5*/s32[...) while((s32[]{:T(128)}, f32[4,1536]{1,0:T(4,128)S(1)}, ...), condition=%wide.region_6.7_spmd.clone, body=%wide.region_3.6_spmd.clone.sunk | while | flops 212515008 | bytes 15892876 | solution.py:164
  267.1 34.6 %while.40 = (s32[]{:T(128)}, f32[4,1536,64]{1,2,0:T(8,128)}, s32[6,256]{1,0:T(8,128)S(1)}, s32[192]{0:T(256)S(1)}, s32[6,256]{1,0:T(8,128)S(1)}, /*index=5*/bf16...) while((s32[]{:T(128)}, f32[4,1536,64]{1,2,0:T(8,128)}, ...), condition=%wide.region_8.9_spmd.clone, body=%wide.region_7.8_spmd.clone.sunk | while | flops 411451584 | bytes 5924758 | solution.py:180
  315.5 111.6 %all-gather.16.cloned.1.call-done = bf16[2048,5632]{1,0:T(8,128)(2,1)} async-done(((bf16[64,5632]{1,0:T(8,128)(2,1)}), bf16[2048,5632]{1,0:T(8,128)(2,1)}) %all-gather.16.cloned.1.call-update) | async-done | bytes 23068688 | tf_op jit(solution)/shard_map/all_gather | solution.py:189
  427.1 12.0 fusion.79
  439.1 133.5 %all-gather.18.cloned.1.call-done = bf16[2048,5632]{1,0:T(8,128)(2,1)} async-done(((bf16[64,5632]{1,0:T(8,128)(2,1)}), bf16[2048,5632]{1,0:T(8,128)(2,1)}) %all-gather.18.cloned.1.call-update) | async-done | bytes 23068688 | tf_op jit(solution)/shard_map/all_gather | solution.py:190
  572.6 12.0 fusion.80
  584.6 133.6 %all-gather.20.cloned.1.call-done = bf16[5632,2048]{1,0:T(8,128)(2,1)} async-done(((bf16[176,2048]{1,0:T(8,128)(2,1)}), bf16[5632,2048]{1,0:T(8,128)(2,1)}) %all-gather.20.cloned.1.call-update) | async-done | bytes 23068688 | tf_op jit(solution)/shard_map/all_gather | solution.py:191
  718.3 16.2 multiply_convert_fusion
  734.4 14.0 fusion.81
  748.4 14.6 multiply_reduce_fusion
  778.9 100.7 %while.41 = (s32[]{:T(128)}, f32[4,1536,64]{1,2,0:T(8,128)}, bf16[6,4,256,64]{2,3,1,0:T(8,128)(2,1)}, bf16[6,4,256,64]{2,3,1,0:T(8,128)(2,1)}, s32[6,256]{1,0:T(...) while((s32[]{:T(128)}, f32[4,1536,64]{1,2,0:T(8,128)}, ...), condition=%wide.region_13.14_spmd.clone, body=%wide.region_12.13_spmd.clone.sunk | while | flops 1020608704 | bytes 100188792 | solution.py:263
  886.7 30.4 reduce-scatter.28.cloned.1.call-done
  920.3 35.6 %reduce-scatter.30.cloned.1.call-done = bf16[192,256]{1,0:T(8,128)(2,1)} async-done(((bf16[1536,256]{1,0:T(8,128)(2,1)}), bf16[192,256]{1,0:T(8,128)(2,1)}) %reduce-scatter.30.cloned.1.call-update) | async-done | bytes 98320
  964.8 8.3 fusion.72
  974.8 8.1 fusion.63
  984.0 19.5 fusion.83
  1003.9 19.6 fusion.84
  1024.5 19.5 fusion.85
  1051.8 11.4 fusion.51
  1066.3 39.6 %all-reduce.5 = (f32[2048]{0:T(1024)S(1)}, f32[2048]{0:T(1024)S(1)}) all-reduce(f32[2048]{0:T(1024)S(1)} %get-tuple-element.477, f32[2048]{0:T(1024)S(1)} %copy-done.41), channel_id=4, replica_groups=mesh['seq'=4,'ctx'=8] {'seq','ctx'}, use_global_device_ids=true, to_apply=%region_18.19.clone | all-reduce | flops 4096 | bytes 32768
  1110.1 120.3 %reduce-scatter.18.cloned.1.call-done = f32[64,256]{1,0:T(8,128)} async-done(((f32[2048,256]{1,0:T(8,128)}), f32[64,256]{1,0:T(8,128)}) %reduce-scatter.18.cloned.1.call-update) | async-done | bytes 65552 | tf_op jit(solution)/shard_map/reduce_scatter | solution.py:296
  1230.4 181.7 %reduce-scatter.14.cloned.1.call-done = f32[64,2048]{1,0:T(8,128)} async-done(((f32[2048,2048]{1,0:T(8,128)}), f32[64,2048]{1,0:T(8,128)}) %reduce-scatter.14.cloned.1.call-update) | async-done | bytes 524304 | tf_op jit(solution)/shard_map/reduce_scatter | solution.py:290
  1412.1 187.3 %reduce-scatter.20.cloned.1.call-done = f32[64,2048]{1,0:T(8,128)} async-done(((f32[2048,2048]{1,0:T(8,128)}), f32[64,2048]{1,0:T(8,128)}) %reduce-scatter.20.cloned.1.call-update) | async-done | bytes 524304 | tf_op jit(solution)/shard_map/reduce_scatter | solution.py:299
  1599.3 489.4 %reduce-scatter.22.cloned.1.call-done = f32[64,5632]{1,0:T(8,128)} async-done(((f32[2048,5632]{1,0:T(8,128)}), f32[64,5632]{1,0:T(8,128)}) %reduce-scatter.22.cloned.1.call-update) | async-done | bytes 1441808 | tf_op jit(solution)/shard_map/reduce_scatter | solution.py:223
  2088.7 495.8 %reduce-scatter.24.cloned.1.call-done = f32[64,5632]{1,0:T(8,128)} async-done(((f32[2048,5632]{1,0:T(8,128)}), f32[64,5632]{1,0:T(8,128)}) %reduce-scatter.24.cloned.1.call-update) | async-done | bytes 1441808 | tf_op jit(solution)/shard_map/reduce_scatter | solution.py:224
  2584.5 495.8 %reduce-scatter.26.cloned.1.call-done = f32[176,2048]{1,0:T(8,128)} async-done(((f32[5632,2048]{1,0:T(8,128)}), f32[176,2048]{1,0:T(8,128)}) %reduce-scatter.26.cloned.1.call-update) | async-done | bytes 1441808 | tf_op jit(solution)/shard_map/reduce_scatter | solution.py:225
  (424 shorter events, 285.6 us)
Async XLA Ops:
  7.2 16.1 copy-start.43
  7.2 16.3 copy-start.44
  7.2 57.1 %copy-start.7 = (bf16[192,2048]{1,0:T(8,128)(2,1)S(1)}, bf16[192,2048]{1,0:T(8,128)(2,1)}, u32[]{:S(2)}) copy-start(bf16[192,2048]{1,0:T(8,128)(2,1)} %param.18) | copy-start | bytes 2359300
  7.2 60.3 %all-gather.8.cloned.1.call-start = ((), (), s32[]{:S(2)}) async-start(), calls=%async_computation.9 | async-start | bytes 1081344 | tf_op jit(solution)/shard_map/all_gather | solution.py:128
  8.0 115.1 %all-gather.12.cloned.1.call-start = ((), (), s32[]{:S(2)}) async-start(), calls=%async_computation.11 | async-start | bytes 1081344 | tf_op jit(solution)/shard_map/all_gather | solution.py:129
  8.7 193.6 %all-gather.10.cloned.1.call-start = ((), (), s32[]{:S(2)}) async-start(), calls=%async_computation.10 | async-start | bytes 8650752 | tf_op jit(solution)/shard_map/all_gather | solution.py:127
  9.5 300.1 %all-gather.14.cloned.1.call-start = ((), (), s32[]{:S(2)}) async-start(), calls=%async_computation.12 | async-start | bytes 8650752 | tf_op jit(solution)/shard_map/all_gather | solution.py:130
  10.0 417.1 %all-gather.16.cloned.1.call-start = ((), (), s32[]{:S(2)}) async-start(), calls=%async_computation.13 | async-start | bytes 23789568 | tf_op jit(solution)/shard_map/all_gather | solution.py:189
  10.6 562.0 %all-gather.18.cloned.1.call-start = ((), (), s32[]{:S(2)}) async-start(), calls=%async_computation.14 | async-start | bytes 23789568 | tf_op jit(solution)/shard_map/all_gather | solution.py:190
  11.2 707.1 %all-gather.20.cloned.1.call-start = ((), (), s32[]{:S(2)}) async-start(), calls=%async_computation.15 | async-start | bytes 23789568 | tf_op jit(solution)/shard_map/all_gather | solution.py:191
  11.9 905.2 %reduce-scatter.28.cloned.1.call-start = ((), (), s32[]{:S(2)}) async-start(), calls=%async_computation.23 | async-start | bytes 884736
  63.4 139.0 %copy-start.33 = (f32[2048]{0:T(1024)}, f32[2048]{0:T(1024)S(1)}, u32[]{:S(2)}) copy-start(f32[2048]{0:T(1024)S(1)} %convert_element_type.105) | copy-start | bytes 24580
  64.5 137.8 %copy-start.39 = (f32[192]{0:T(256)}, f32[192]{0:T(256)S(1)}, u32[]{:S(2)}) copy-start(f32[192]{0:T(256)S(1)} %add_rsqrt_fusion.1) | copy-start | bytes 2308
  65.3 143.8 %copy-start.28 = (f32[192,32]{0,1:T(8,128)}, f32[192,32]{0,1:T(8,128)S(1)}, u32[]{:S(2)}) copy-start(f32[192,32]{0,1:T(8,128)S(1)} %get-tuple-element.574) | copy-start | bytes 73732
  315.2 447.8 %copy-start.9 = (f32[192,2048]{1,0:T(8,128)}, f32[192,2048]{1,0:T(8,128)S(1)}, u32[]{:S(2)}) copy-start(f32[192,2048]{1,0:T(8,128)S(1)} %get-tuple-element.576) | copy-start | bytes 4718596
  315.5 257.1 %copy-start.14 = (bf16[192,2048]{1,0:T(8,128)(2,1)}, bf16[192,2048]{1,0:T(8,128)(2,1)S(1)}, u32[]{:S(2)}) copy-start(bf16[192,2048]{1,0:T(8,128)(2,1)S(1)} %multiply_convert_fusion.3) | copy-start | bytes 2359300
  734.4 14.0 copy-start.25
  748.4 14.6 copy-start.21
  883.8 72.1 %reduce-scatter.30.cloned.1.call-start = ((), (), s32[]{:S(2)}) async-start(), calls=%async_computation.24 | async-start | bytes 884736
  884.9 33.3 %copy-start.29 = (f32[192,32]{0,1:T(8,128)S(1)}, f32[192,32]{0,1:T(8,128)}, u32[]{:S(2)}) copy-start(f32[192,32]{0,1:T(8,128)} %copy-done.28) | copy-start | bytes 73732
  884.9 33.3 %copy-start.36 = (f32[192,32]{0,1:T(8,128)S(1)}, f32[192,32]{0,1:T(8,128)}, u32[]{:S(2)}) copy-start(f32[192,32]{0,1:T(8,128)} %get-tuple-element.572) | copy-start | bytes 73732
  884.9 33.4 %copy-start.8 = (bf16[192,2048]{1,0:T(8,128)(2,1)S(1)}, bf16[192,2048]{1,0:T(8,128)(2,1)}, u32[]{:S(2)}) copy-start(bf16[192,2048]{1,0:T(8,128)(2,1)} %param.18) | copy-start | bytes 2359300
  884.9 33.4 %copy-start.34 = (f32[2048]{0:T(1024)S(1)}, f32[2048]{0:T(1024)}, u32[]{:S(2)}) copy-start(f32[2048]{0:T(1024)} %copy-done.33) | copy-start | bytes 24580
  884.9 33.4 %copy-start.40 = (f32[192]{0:T(256)S(1)}, f32[192]{0:T(256)}, u32[]{:S(2)}) copy-start(f32[192]{0:T(256)} %copy-done.39) | copy-start | bytes 2308
  886.7 223.4 %reduce-scatter.16.cloned.1.call-start = ((), (), s32[]{:S(2)}) async-start(), calls=%async_computation.17 | async-start | bytes 2162688 | tf_op jit(solution)/shard_map/reduce_scatter | solution.py:293
  920.2 38.8 %copy-start.6 = (f32[4,1536,64]{1,2,0:T(8,128)S(1)}, f32[4,1536,64]{1,2,0:T(8,128)}, u32[]{:S(2)}) copy-start(f32[4,1536,64]{1,2,0:T(8,128)} %get-tuple-element.198) | copy-start | bytes 4718596
  920.2 310.1 %reduce-scatter.18.cloned.1.call-start = ((), (), s32[]{:S(2)}) async-start(), calls=%async_computation.18 | async-start | bytes 2162688 | tf_op jit(solution)/shard_map/reduce_scatter | solution.py:296
  958.7 453.3 %reduce-scatter.14.cloned.1.call-start = ((), (), s32[]{:S(2)}) async-start(), calls=%async_computation.16 | async-start | bytes 17301504 | tf_op jit(solution)/shard_map/reduce_scatter | solution.py:290
  973.1 626.2 %reduce-scatter.20.cloned.1.call-start = ((), (), s32[]{:S(2)}) async-start(), calls=%async_computation.19 | async-start | bytes 17301504 | tf_op jit(solution)/shard_map/reduce_scatter | solution.py:299
  982.9 1105.8 %reduce-scatter.22.cloned.1.call-start = ((), (), s32[]{:S(2)}) async-start(), calls=%async_computation.20 | async-start | bytes 47579136 | tf_op jit(solution)/shard_map/reduce_scatter | solution.py:223
  1003.6 1581.0 %reduce-scatter.24.cloned.1.call-start = ((), (), s32[]{:S(2)}) async-start(), calls=%async_computation.21 | async-start | bytes 47579136 | tf_op jit(solution)/shard_map/reduce_scatter | solution.py:224
  1023.4 2056.9 %reduce-scatter.26.cloned.1.call-start = ((), (), s32[]{:S(2)}) async-start(), calls=%async_computation.22 | async-start | bytes 47579136 | tf_op jit(solution)/shard_map/reduce_scatter | solution.py:225
  (60 other events, 231.7 us)
Sparse Core Ops, SparseCore 0:
  10.9 56.5 all-gather.7
  70.4 52.6 all-gather.11
  125.9 76.4 all-gather.9
  205.1 76.0 all-gather.13
  283.9 143.1 all-gather.15
  429.8 142.7 all-gather.17
  575.4 142.7 all-gather.19
  883.9 33.1 reduce-scatter.27
  920.8 35.0 reduce-scatter.29
  958.6 136.5 reduce-scatter.15
  1098.1 132.2 reduce-scatter.17
  1233.1 178.9 reduce-scatter.13
  1414.9 184.3 reduce-scatter.19
  1602.1 486.5 reduce-scatter.21
  2091.4 493.0 reduce-scatter.23
  2587.3 493.0 reduce-scatter.25
where the time goes:
time: 3100 us; the launch traced here: 3090 us
  waiting for transfers between devices  2530 us (82%)
  matrix products  334 us (11%)
  blocking collectives  110 us (4%)
  local copies, waits for them, and re-layouts  60.2 us (2%)
  other arithmetic  38.6 us (1%)
    reduce_scatter x1, waiting for transfers between devices, body(): lax.psum_scatter(grad_up_part, ('seq', 'ctx'), scatter_dimension=0, tiled...  496 us
    reduce_scatter x1, waiting for transfers between devices, body(): lax.psum_scatter(grad_down_part, ('seq', 'ctx'), scatter_dimension=0, til...  496 us
    reduce_scatter x1, waiting for transfers between devices, body(): lax.psum_scatter(grad_gate_part, ('seq', 'ctx'), scatter_dimension=0, til...  489 us
    reduce_scatter x1, waiting for transfers between devices, body(): lax.psum_scatter(grad_projection, ('seq', 'ctx'), scatter_dimension=0, ti...  187 us
    reduce_scatter x1, waiting for transfers between devices, body(): lax.psum_scatter(outer_sum(normed, grad_query_in), ('seq', 'ctx'), scatte...  182 us
    all_gather x1, waiting for transfers between devices, body(): lax.all_gather(down_weight, ('seq', 'ctx'), axis=0, tiled=True)  134 us
    all_gather x1, waiting for transfers between devices, body(): lax.all_gather(up_weight, ('seq', 'ctx'), axis=0, tiled=True)  134 us
    reduce_scatter x1, waiting for transfers between devices, body(): lax.psum_scatter(outer_sum(normed, grad_value_in), ('seq', 'ctx'), scatte...  120 us
  transfers between devices with their start and end apart: 16, of which 14 were waited for; matrix products, arithmetic and copies ran while one was open for 8% of the time, Pallas kernels for 0%

commit v1 on v0

v1 whole, which is shorter than its diff:
```python
import functools

import jax
import jax.numpy as jnp
from jax import lax
from jax.experimental import pallas as pl
from jax.experimental.pallas import tpu as pltpu
from jax.sharding import PartitionSpec as P

H = 32
KV = 4
HD = 64
HALF = HD // 2

EPSILON = 1e-05
MASKED = -1e30
BOTH = ("seq", "ctx")
f32 = jnp.float32
bf16 = jnp.bfloat16


def dot(left, right, contract, out=f32):
    return lax.dot_general(left, right, (contract, ((), ())), preferred_element_type=f32).astype(out)


def after(value, *others):
    return lax.optimization_barrier((value, *others))[0]


def swap(value, step, count):
    return lax.ppermute(value, "ctx", [(i, i ^ step) for i in range(count)])


def blank(shape, dtype):
    return pl.pallas_call(
        lambda out_ref: None,
        out_shape=jax.ShapeDtypeStruct(shape, dtype),
        out_specs=pl.BlockSpec(memory_space=pl.ANY),
        name="blank",
    )()


def chip_bits():
    me = lax.axis_index("ctx")
    count = lax.axis_size("ctx")
    bits = [1 << at for at in range(1, count.bit_length() - 1)]
    return [(step, (me // step) % 2) for step in bits]


def gather_ctx(value):
    count = lax.axis_size("ctx")
    core = lax.axis_index("ctx") % 2
    bits = chip_bits()
    half, depth = value.shape[0] // 2, value.shape[1]
    shape = (2,) * len(bits) + (2, 2, half, depth)
    whole = blank(shape, value.dtype)

    def put(whole, part, at):
        place = [0] * len(shape)
        for axis, index in at:
            place[axis] = index
        return lax.dynamic_update_slice(whole, part, place)

    for which in range(2):
        current = value[which * half : (which + 1) * half].reshape((1,) * len(bits) + (half, depth))
        order = range(len(bits)) if which == 0 else range(len(bits) - 1, -1, -1)
        for at in order:
            step, bit = bits[at]
            axis = len(bits) - 1 - at
            arrived = swap(current, step, count)
            if at == order[-1]:
                break
            current = jnp.where(
                bit == 0,
                jnp.concatenate([current, arrived], axis),
                jnp.concatenate([arrived, current], axis),
            )
        for part, index in ((current, bit), (arrived, 1 - bit)):
            for there in range(2):
                piece = swap(part, 1, count) if there else part
                owner = 1 - core if there else core
                spots = ((axis, index), (len(bits), owner), (len(bits) + 1, which))
                piece = piece.reshape(piece.shape[:-2] + (1, 1, half, depth))
                whole = put(whole, piece, spots)
    return whole.reshape(count * value.shape[0], depth)


def of_core(value, core):
    count = lax.axis_size("ctx")
    blocks = value.reshape(count // 2, 2, value.shape[0] // count, value.shape[1])
    return lax.dynamic_index_in_dim(blocks, core, 1, keepdims=False).reshape(-1, value.shape[1])


def pair_up(left, right, contract, wait=()):
    count = lax.axis_size("ctx")
    core = lax.axis_index("ctx") % 2
    away = dot(of_core(left, 1 - core), right, contract, bf16)
    arrived = swap(away, 1, count)
    stay = of_core(left, core)
    stay = after(stay, away, *wait)
    pairs = (dot(stay, right, contract) + arrived.astype(f32)).astype(bf16)
    return pairs.reshape(count // 2, -1, pairs.shape[1])


def scatter_pairs(pairs):
    count = lax.axis_size("ctx")
    bits = chip_bits()
    half, depth = pairs.shape[1] // 2, pairs.shape[2]
    pairs = pairs.reshape((2,) * len(bits) + (2, half, depth))
    sums = []
    for which in range(2):
        current = pairs[..., which, :, :]
        order = range(len(bits)) if which == 0 else range(len(bits) - 1, -1, -1)
        for at in order:
            step, bit = bits[at]
            axis = len(bits) - 1 - at
            away = lax.dynamic_slice_in_dim(current, 1 - bit, 1, axis).astype(bf16)
            stay = lax.dynamic_slice_in_dim(current, bit, 1, axis).astype(f32)
            current = stay + swap(away, step, count).astype(f32)
        sums.append(current.reshape(half, depth))
    return jnp.concatenate(sums)


def gather_seq(value):
    return lax.all_gather(value, "seq", axis=0, tiled=True)


def scatter_seq(value):
    return lax.psum_scatter(value, "seq", scatter_dimension=0, tiled=True)


def exchange_ctx(value):
    return lax.all_to_all(value, "ctx", 0, 0)


def gather_small(gains, segments):
    seqs, ranks = lax.axis_size("seq"), lax.axis_size("ctx")
    line = jnp.concatenate([part.astype(f32) for part in gains] + [segments[0].astype(f32)])
    spread = jnp.broadcast_to(line[None, None], (seqs * ranks, 1, line.shape[0]))
    table = lax.all_to_all(spread, BOTH, 0, 0)[:, 0]
    width = gains[0].shape[0]
    own = lax.dynamic_slice_in_dim(table, lax.axis_index("seq") * ranks, ranks, 0)
    return (
        table[:, :width].reshape(1, -1),
        table[:, width : 2 * width].reshape(1, -1),
        own[:, 2 * width :].reshape(1, -1),
    )


def split_kernel(seqs, ranks, units, gate_ref, up_ref, out_ref):
    for rank in range(ranks):
        for at, ref in enumerate((gate_ref, up_ref)):
            for seq in range(seqs):
                first = (seq * ranks + rank) * units
                to = (at * seqs + seq) * units
                out_ref[rank, :, to : to + units] = ref[:, first : first + units]


def split_units(gate, up, units):
    seqs, ranks = lax.axis_size("seq"), lax.axis_size("ctx")
    return pl.pallas_call(
        functools.partial(split_kernel, seqs, ranks, units),
        out_shape=jax.ShapeDtypeStruct((ranks, gate.shape[0], 2 * seqs * units), gate.dtype),
        compiler_params=pltpu.CompilerParams(vmem_limit_bytes=48 * 1024 * 1024),
        name="split_units",
    )(gate, up)


def join_kernel(
    seqs, ranks, units, grad_ref, gate_ref, up_ref, grad_gate_ref, grad_up_ref, sum_ref
):
    for at, ref in enumerate((grad_gate_ref, grad_up_ref)):
        for rank in range(ranks):
            for seq in range(seqs):
                first = (seq * ranks + rank) * units
                to = (at * seqs + seq) * units
                ref[:, first : first + units] = grad_ref[rank, :, to : to + units].astype(f32)
    terms = grad_gate_ref[...] * gate_ref[...].astype(f32)
    terms = terms + grad_up_ref[...] * up_ref[...].astype(f32)
    sum_ref[...] = jnp.sum(terms, axis=1, keepdims=True)


def join_units(grad, gate, up, units):
    seqs, ranks = lax.axis_size("seq"), lax.axis_size("ctx")
    whole = jax.ShapeDtypeStruct(gate.shape, f32)
    return pl.pallas_call(
        functools.partial(join_kernel, seqs, ranks, units),
        out_shape=[whole, whole, jax.ShapeDtypeStruct((gate.shape[0], 1), f32)],
        compiler_params=pltpu.CompilerParams(vmem_limit_bytes=48 * 1024 * 1024),
        name="join_units",
    )(grad, gate, up)


def forward_kernel(block, heads, key_ref, value_ref, query_ref, start_ref, out_ref, out_n_ref, lse_ref):
    at = pl.program_id(0)
    start = start_ref[...]
    rows = lax.broadcasted_iota(jnp.int32, (block, block), 0)
    columns = lax.broadcasted_iota(jnp.int32, (block, block), 1)

    out_ref[...] = jnp.zeros_like(out_ref)

    def step(j, carry, diagonal):
        first = pl.multiple_of(j * block, block)
        keys = key_ref[pl.ds(first, block), :]
        values = value_ref[:, pl.ds(first, block)]
        allowed = rows >= start - first
        if diagonal:
            allowed = allowed & (rows <= columns)
        fresh = []
        for head in range(heads):
            top, mass = carry[head]
            span = slice(head * HD, (head + 1) * HD)
            scores = dot(keys, query_ref[span, :], ((1,), (0,)))
            scores = jnp.where(allowed, scores, MASKED)
            high = jnp.maximum(top, jnp.max(scores, axis=0, keepdims=True))
            weights = jnp.exp(scores - high)
            fade = jnp.exp(top - high)
            mass = mass * fade + jnp.sum(weights, axis=0, keepdims=True)
            mixed = dot(values, weights.astype(bf16), ((1,), (0,)))
            out_ref[span, :] = out_ref[span, :] * fade + mixed
            fresh.append((high, mass))
        return tuple(fresh)

    begin = tuple(
        (jnp.full((1, block), MASKED, f32), jnp.zeros((1, block), f32)) for _ in range(heads)
    )
    carry = lax.fori_loop(0, at, lambda j, c: step(j, c, False), begin)
    carry = step(at, carry, True)
    for head in range(heads):
        top, mass = carry[head]
        span = slice(head * HD, (head + 1) * HD)
        out = out_ref[span, :] / mass
        out_ref[span, :] = out
        out_n_ref[:, span] = out.T.astype(bf16)
        lse_ref[head : head + 1, :] = top + jnp.log(mass)


def attention_forward(query_t, key_n, value_t, start, block):
    width, length = query_t.shape
    heads = width // HD
    return pl.pallas_call(
        functools.partial(forward_kernel, block, heads),
        grid=(length // block,),
        in_specs=[
            pl.BlockSpec((length, HD), lambda i: (0, 0)),
            pl.BlockSpec((HD, length), lambda i: (0, 0)),
            pl.BlockSpec((width, block), lambda i: (0, i)),
            pl.BlockSpec((1, block), lambda i: (0, i)),
        ],
        out_specs=[
            pl.BlockSpec((width, block), lambda i: (0, i)),
            pl.BlockSpec((block, width), lambda i: (i, 0)),
            pl.BlockSpec((heads, block), lambda i: (0, i)),
        ],
        out_shape=[
            jax.ShapeDtypeStruct((width, length), f32),
            jax.ShapeDtypeStruct((length, width), bf16),
            jax.ShapeDtypeStruct((heads, length), f32),
        ],
        compiler_params=pltpu.CompilerParams(vmem_limit_bytes=48 * 1024 * 1024),
        name="attention_forward",
    )(key_n, value_t, query_t, start)


def backward_kernel(
    block,
    heads,
    count,
    key_ref,
    key_t_ref,
    value_ref,
    query_ref,
    grad_ref,
    out_ref,
    lse_ref,
    start_ref,
    grad_query_ref,
    grad_key_ref,
    grad_value_ref,
    query_n,
    grad_n,
    delta,
    key_sum,
    value_sum,
):
    at = pl.program_id(0)
    rows = lax.broadcasted_iota(jnp.int32, (block, block), 0)
    columns = lax.broadcasted_iota(jnp.int32, (block, block), 1)

    @pl.when(at == 0)
    def _():
        grad_query_ref[...] = jnp.zeros_like(grad_query_ref)

        def turn(i, unused):
            part = pl.ds(pl.multiple_of(i * block, block), block)
            for head in range(heads):
                span = slice(head * HD, (head + 1) * HD)
                grads = grad_ref[span, part].astype(f32)
                query_n[head, part, :] = query_ref[span, part].astype(f32).T.astype(bf16)
                grad_n[head, part, :] = grads.T.astype(bf16)
                delta[head : head + 1, part] = jnp.sum(
                    grads * out_ref[span, part], axis=0, keepdims=True
                )
            return unused

        lax.fori_loop(0, count, turn, 0)

    key_sum[...] = jnp.zeros_like(key_sum)
    value_sum[...] = jnp.zeros_like(value_sum)
    keys = key_ref[...]
    keys_t = key_t_ref[...]
    values = value_ref[...]

    def step(i, diagonal):
        part = pl.ds(pl.multiple_of(i * block, block), block)
        allowed = rows >= start_ref[:, part] - at * block
        if diagonal:
            allowed = allowed & (rows <= columns)
        for head in range(heads):
            span = slice(head * HD, (head + 1) * HD)
            scores = dot(keys, query_ref[span, part], ((1,), (0,)))
            scores = jnp.where(allowed, scores, MASKED)
            probs = jnp.exp(scores - lse_ref[head : head + 1, part])
            value_sum[...] += dot(probs.astype(bf16), grad_n[head, part, :], ((1,), (0,)))
            grad_probs = dot(values, grad_ref[span, part], ((1,), (0,)))
            grad_scores = (probs * (grad_probs - delta[head : head + 1, part])).astype(bf16)
            key_sum[...] += dot(grad_scores, query_n[head, part, :], ((1,), (0,)))
            grad_query_ref[span, part] += dot(keys_t, grad_scores, ((1,), (0,)))

    step(at, True)

    def loop(i, unused):
        step(i, False)
        return unused

    lax.fori_loop(at + 1, count, loop, 0)
    grad_key_ref[...] = key_sum[...].T
    grad_value_ref[...] = value_sum[...].T


def attention_backward(query_t, key_n, key_t, value_n, grad_t, out_t, lse, start, block):
    width, length = query_t.shape
    heads = width // HD
    count = length // block
    whole = lambda j: (0, 0)
    return pl.pallas_call(
        functools.partial(backward_kernel, block, heads, count),
        grid=(count,),
        in_specs=[
            pl.BlockSpec((block, HD), lambda j: (j, 0)),
            pl.BlockSpec((HD, block), lambda j: (0, j)),
            pl.BlockSpec((block, HD), lambda j: (j, 0)),
            pl.BlockSpec((width, length), whole),
            pl.BlockSpec((width, length), whole),
            pl.BlockSpec((width, length), whole),
            pl.BlockSpec((heads, length), whole),
            pl.BlockSpec((1, length), whole),
        ],
        out_specs=[
            pl.BlockSpec((width, length), whole),
            pl.BlockSpec((HD, block), lambda j: (0, j)),
            pl.BlockSpec((HD, block), lambda j: (0, j)),
        ],
        out_shape=[
            jax.ShapeDtypeStruct((width, length), f32),
            jax.ShapeDtypeStruct((HD, length), f32),
            jax.ShapeDtypeStruct((HD, length), f32),
        ],
        scratch_shapes=[
            pltpu.VMEM((heads, length, HD), bf16),
            pltpu.VMEM((heads, length, HD), bf16),
            pltpu.VMEM((heads, length), f32),
            pltpu.VMEM((block, HD), f32),
            pltpu.VMEM((block, HD), f32),
        ],
        compiler_params=pltpu.CompilerParams(vmem_limit_bytes=48 * 1024 * 1024),
        name="attention_backward",
    )(key_n, key_t, value_n, query_t, grad_t, out_t, lse, start)


def rotate(source, cosine, sine_part):
    halves = source.reshape(-1, 2, HALF, source.shape[1])
    first, second = halves[:, 0], halves[:, 1]
    turned = jnp.stack(
        [first * cosine - second * sine_part, second * cosine + first * sine_part], axis=1
    )
    return turned.reshape(source.shape)


def body(
    tokens,
    segments,
    cotangent,
    attention_gain,
    query_weight,
    key_weight,
    value_weight,
    projection,
    feedforward_gain,
    gate_weight,
    up_weight,
    down_weight,
):
    seqs, ranks = lax.axis_size("seq"), lax.axis_size("ctx")
    rows = query_weight.shape[0]
    depth = tokens.shape[1]
    units = down_weight.shape[0]
    local_count = tokens.shape[0]
    length = local_count * ranks
    block = 256 if length % 256 == 0 else local_count
    width = H * HD // ranks

    def row_factor(values):
        return lax.rsqrt(jnp.mean(values * values, axis=-1, keepdims=True) + EPSILON)

    gain_one_row, gain_two_row, seg_row = gather_small(
        (attention_gain, feedforward_gain), segments
    )
    inputs = tokens.astype(f32)
    factor_one = row_factor(inputs)
    normed = (inputs * factor_one * gain_one_row).astype(bf16)

    def split_heads(weight):
        return jnp.repeat(weight.reshape(rows, KV, HD), ranks // KV, axis=1)

    mix = jnp.concatenate(
        [
            query_weight.reshape(rows, ranks, width),
            split_heads(key_weight),
            split_heads(value_weight),
        ],
        axis=2,
    ).transpose(1, 0, 2)
    mix = exchange_ctx(after(mix, seg_row)).reshape(ranks * rows, -1)
    mix_wide = gather_seq(mix)
    normed_all = gather_ctx(normed)
    index = [(i, (i % seqs) * ranks + i // seqs) for i in range(seqs * ranks)]
    proj_wide = gather_seq(after(lax.ppermute(projection, BOTH, index), mix))
    pair = split_units(after(gate_weight, mix), up_weight, units)
    pair = exchange_ctx(pair).reshape(ranks * rows, -1)
    pair_wide = gather_seq(after(pair, proj_wide))
    down_wide = gather_seq(after(down_weight, pair))
    hidden_units = units * seqs

    start = jnp.sum((seg_row < seg_row.T).astype(jnp.int32), axis=1)
    positions = jnp.arange(length, dtype=jnp.int32) - start
    freqs = jnp.power(10000.0, -jnp.arange(HALF, dtype=f32) * (2.0 / HD))
    angles = freqs[:, None] * positions.astype(f32)[None, :]
    cosine, sine_part = jnp.cos(angles), jnp.sin(angles)
    start_row = start[None, :]

    mixed = dot(mix_wide, normed_all, ((0,), (1,)))
    query_t = rotate(mixed[:width], cosine, sine_part).astype(bf16) * bf16(HD**-0.5)
    key_t = rotate(mixed[width : width + HD], cosine, sine_part).astype(bf16)
    value_t = mixed[width + HD :].astype(bf16)
    query_t = after(query_t, pair)
    key_n, value_n = key_t.T, value_t.T
    out_t, out_low, lse = attention_forward(query_t, key_n, value_t, start_row, block)
    cotangent_all = gather_ctx(after(cotangent, query_t))
    rows_by = ((1,), (0,))
    hidden = inputs + scatter_pairs(pair_up(out_low, proj_wide, rows_by))

    factor_two = row_factor(hidden)
    normed_two = (hidden * factor_two * gain_two_row).astype(bf16)
    normed_two_all = gather_ctx(normed_two)
    both = dot(normed_two_all, pair_wide, ((1,), (0,)))
    gate, upward = both[:, :hidden_units], both[:, hidden_units:]
    sigmoid_gate = jax.nn.sigmoid(gate)
    swished = gate * sigmoid_gate
    activated = (swished * upward).astype(bf16)
    grad_down = dot(activated, cotangent_all, ((0,), (0,)), bf16)
    grad_act = dot(cotangent_all, down_wide, ((1,), (1,)))
    grad_pair_in = jnp.concatenate(
        [
            (grad_act * upward * sigmoid_gate * (1.0 + gate * (1.0 - sigmoid_gate))).astype(bf16),
            (grad_act * swished).astype(bf16),
        ],
        axis=1,
    )
    grad_pair_in = after(grad_pair_in, grad_down)
    grad_down = scatter_seq(grad_down).astype(f32)
    columns_by = ((1,), (1,))
    shaped_two = scatter_pairs(pair_up(grad_pair_in, pair_wide, columns_by)) * gain_two_row
    grad_pair = dot(normed_two_all, grad_pair_in, ((0,), (0,)), bf16)
    shaped_two = after(shaped_two, grad_pair)
    grad_pair = scatter_seq(grad_pair)
    mean_two = jnp.mean(shaped_two * hidden, axis=-1, keepdims=True)
    grad_hidden = (
        cotangent.astype(f32)
        + factor_two * shaped_two
        - hidden * (factor_two * factor_two * factor_two * mean_two)
    )

    branch_all = gather_ctx(grad_hidden.astype(bf16))
    grad_out_t = dot(proj_wide, branch_all, columns_by, bf16)
    grad_proj = dot(out_low, branch_all, ((0,), (0,)), bf16)
    out_pairs = pair_up(after(activated, grad_out_t), down_wide, rows_by)
    grad_out_t = after(grad_out_t, grad_proj, out_pairs, grad_down)
    grad_query_t, grad_key_t, grad_value_t = attention_backward(
        query_t, key_n, key_t, value_n, grad_out_t, out_t, lse, start_row, block
    )
    grad_mixed = jnp.concatenate(
        [
            rotate(grad_query_t * HD**-0.5, cosine, -sine_part),
            rotate(grad_key_t, cosine, -sine_part),
            grad_value_t,
        ],
        axis=0,
    ).astype(bf16)
    grad_projection = lax.ppermute(
        scatter_seq(after(grad_proj, grad_pair)), BOTH, [(b, a) for a, b in index]
    ).astype(f32)
    block_out = (hidden + scatter_pairs(after(out_pairs, grad_out_t))).astype(bf16)
    grad_mix = dot(normed_all, grad_mixed, ((0,), (1,)), bf16)
    grad_pair = exchange_ctx(after(grad_pair, grad_mixed).reshape(ranks, rows, -1))
    mixed_n = after(grad_mixed.T, grad_mix)
    shaped_one = pair_up(mixed_n, mix_wide, columns_by)
    grad_mix = scatter_seq(grad_mix)
    grad_gate, grad_up, grad_feedforward = join_units(grad_pair, gate_weight, up_weight, units)
    shaped_one = after(scatter_pairs(shaped_one), grad_gate, block_out)
    shaped_one = shaped_one * gain_one_row
    mean_one = jnp.mean(shaped_one * inputs, axis=-1, keepdims=True)
    grad_tokens = (
        grad_hidden
        + factor_one * shaped_one
        - inputs * (factor_one * factor_one * factor_one * mean_one)
    )

    def join_heads(part):
        part = part.reshape(KV, ranks // KV, rows, HD).astype(f32).sum(axis=1)
        return part.transpose(1, 0, 2).reshape(rows, -1)

    def row_sum(grad, weight):
        return jnp.sum(grad * weight.astype(f32), axis=1)

    grad_feedforward = grad_feedforward[:, 0] / feedforward_gain.astype(f32)

    grad_mix = exchange_ctx(grad_mix.reshape(ranks, rows, -1))
    grad_query = grad_mix[:, :, :width].transpose(1, 0, 2).reshape(rows, -1).astype(f32)
    grad_key = join_heads(grad_mix[:, :, width : width + HD])
    grad_value = join_heads(grad_mix[:, :, width + HD :])
    grad_attention = (
        row_sum(grad_query, query_weight)
        + row_sum(grad_key, key_weight)
        + row_sum(grad_value, value_weight)
    ) / attention_gain.astype(f32)
    return (
        block_out,
        grad_tokens,
        grad_attention,
        grad_query,
        grad_key,
        grad_value,
        grad_projection,
        grad_feedforward,
        grad_gate,
        grad_up,
        grad_down,
    )


def solution(mesh):
    rows, plain = P(BOTH, None), P(BOTH)
    return jax.shard_map(
        body,
        mesh=mesh,
        in_specs=(rows, P("seq", "ctx"), rows, plain, rows, rows, rows, rows, plain, rows, rows, rows),
        out_specs=(rows, rows, plain, rows, rows, rows, rows, plain, rows, rows, rows),
        check_vma=False,
    )
```

time: 3100 us -> 631 us (0.20)
  waiting for transfers between devices: 2530 us -> 227 us
  matrix products: 334 us -> 115 us
  blocking collectives: 110 us -> 0 us
  starting transfers between devices: 1.1 us -> 75.8 us
  Pallas kernels: 0 us -> 59.2 us
    reduce_scatter x7 -> x4, waiting for transfers between devices: 1970 us -> 0.01 us  [scatter_seq(): return lax.psum_scatter(value, 'seq', scatter_dimension=0, tiled=True)]
    all_gather x7 -> x4, waiting for transfers between devices: 486 us -> 0.01 us  [gather_seq(): return lax.all_gather(value, 'seq', axis=0, tiled=True)]
    dot_general x63 -> x16, matrix products: 334 us -> 115 us  [dot(): lax.dot_general(left, right, (contract, ((), ())), preferred_element_type...]
    ppermute x0 -> x54, waiting for transfers between devices: none -> 191 us  [the longest x52 191 us: swap(): return lax.ppermute(value, 'ctx', [(i, i ^ step) for i in range(count)])]
    unnamed x3 -> x0, blocking collectives: 88.8 us -> none
    unnamed x18 -> x8, waiting for transfers between devices: 70.5 us -> 1.23 us
    pallas_call x0 -> x8, Pallas kernels: none -> 59.2 us  [the longest x1 29.1 us: attention_backward(): pl.pallas_call(functools.partial(backward_kernel, block, heads, count), g...]
    ppermute x0 -> x54, starting transfers between devices: none -> 44.7 us  [the longest x52 42.4 us: swap(): return lax.ppermute(value, 'ctx', [(i, i ^ step) for i in range(count)])]
  transfers between devices with their start and end apart: 16 -> 67, of which waited for: 14 -> 31; matrix products, arithmetic and copies ran while one was open for 8% -> 29% of each run, Pallas kernels for 0% -> 9%
where the time goes in v1:
time: 631 us; the launch traced here: 625 us
  waiting for transfers between devices  227 us (36%)
  matrix products  115 us (18%)
  local copies, waits for them, and re-layouts  85.2 us (14%)
  starting transfers between devices  75.8 us (12%)
  Pallas kernels  59.2 us (9%)
  other arithmetic  47.3 us (7%)
  between operations  16.1 us (3%)
    ppermute x52, waiting for transfers between devices, swap(): return lax.ppermute(value, 'ctx', [(i, i ^ step) for i in range(count)])  191 us
    dot_general x16, matrix products, dot(): lax.dot_general(left, right, (contract, ((), ())), preferred_element_type...  115 us
    ppermute x52, starting transfers between devices, swap(): return lax.ppermute(value, 'ctx', [(i, i ^ step) for i in range(count)])  42.4 us
    dynamic_update_slice x24, local copies, waits for them, and re-layouts, put(): return lax.dynamic_update_slice(whole, part, place)  32.5 us
    pallas_call x1, Pallas kernels, attention_backward(): pl.pallas_call(functools.partial(backward_kernel, block, heads, count), g...  29.1 us
    all_to_all x4, waiting for transfers between devices, exchange_ctx(): return lax.all_to_all(value, 'ctx', 0, 0)  27.6 us
    pallas_call x1, Pallas kernels, attention_forward(): pl.pallas_call(functools.partial(forward_kernel, block, heads), grid=(len...  26.3 us
    all_to_all x4, starting transfers between devices, exchange_ctx(): return lax.all_to_all(value, 'ctx', 0, 0)  15.8 us
  transfers between devices with their start and end apart: 67, of which 31 were waited for; matrix products, arithmetic and copies ran while one was open for 29% of the time, Pallas kernels for 9%

profile of v1, /device:TPU:0, one launch (start us, length us, event | category | flops | bytes accessed | tf_op | source)
XLA Modules:
  0.0 625.0 jit_solution(8377700084157828465)
XLA Ops:
  17.0 7.6 %all-to-all-done = bf16[8,64,384]{2,1,0:T(8,128)(2,1)S(1)} async-done(((bf16[8,64,384]{2,1,0:T(8,128)(2,1)}), bf16[8,64,384]{2,1,0:T(8,128)(2,1)S(1)}, u32[]{:S(2)}, u32[]{:S(2)}) %all-to-all-start) | async-done | bytes 393248 | tf_op jit(solution)/shard_map/all_to_all | solution.py:133
  25.5 14.4 %all-to-all-start.1 = ((f32[32,1,320]{2,1,0:T(1,128)}), f32[32,1,320]{2,1,0:T(1,128)S(1)}, u32[]{:S(2)}, u32[]{:S(2)}) async-start(f32[32,1,320]{2,1,0:T(1,128)} %broadcast_in_dim.8), calls=%async_computation.1 | async-start | bytes 98304 | tf_op jit(solution)/shard_map/all_to_all | solution.py:140
  40.8 6.5 %all-to-all-done.1 = f32[32,1,320]{2,1,0:T(1,128)S(1)} async-done(((f32[32,1,320]{2,1,0:T(1,128)}), f32[32,1,320]{2,1,0:T(1,128)S(1)}, u32[]{:S(2)}, u32[]{:S(2)}) %all-to-all-start.1) | async-done | bytes 40992 | tf_op jit(solution)/shard_map/all_to_all | solution.py:140
  58.8 21.4 %collective-permute-done = bf16[1,1,96,2048]{3,2,1,0:T(8,128)(2,1)S(1)} collective-permute-done((bf16[1,1,96,2048]{3,2,1,0:T(8,128)(2,1)}, bf16[1,1,96,2048]{3,2,1,0:T(8,128)(2,1)S(1)}, u32[]{:S(2)}, u32[]{:S(2)}) %collective-permute-start) | collective-permute-done | bytes 393248 | tf_op jit(solution)/shard_map/ppermute | solution.py:31
  89.3 13.3 %collective-permute-done.2 = bf16[1,2,96,2048]{3,2,1,0:T(8,128)(2,1)} collective-permute-done((bf16[1,2,96,2048]{3,2,1,0:T(8,128)(2,1)}, bf16[1,2,96,2048]{3,2,1,0:T(8,128)(2,1)}, u32[]{:S(2)}, u32[]{:S(2)}) %collective-permute-start.2) | collective-permute-done | bytes 786464 | tf_op jit(solution)/shard_map/ppermute | solution.py:31
  115.2 5.3 fusion.42
  124.7 26.3 %attention_forward.1 = (f32[256,1536]{1,0:T(8,128)S(1)}, bf16[1536,256]{1,0:T(8,128)(2,1)S(1)}, f32[4,1536]{1,0:T(4,128)S(1)}) custom-call(bf16[1536,64]{1,0:T(8,128)(2,1)S(1)} %copy.229.key_ref, bf16[64,1536]{1,0:T(8,128)(2,1)S(1)} %copy.230.value_ref, bf16[256,1536]{1,0:T(8,128)(2,1)S(1)} %bitcast.322, s32[1,1536]{1,0:T(1,128)S(1)} %reduce_sum.94.start_ref), custom_call_target="tpu_custom_call" | custom-call | tf_op jit(solution)/shard_map/attention_forward/pallas_call | solution.py:241
  156.3 10.0 %collective-permute-done.22 = bf16[1,1,96,2048]{3,2,1,0:T(8,128)(2,1)S(1)} collective-permute-done((bf16[1,1,96,2048]{3,2,1,0:T(8,128)(2,1)S(1)}, bf16[1,1,96,2048]{3,2,1,0:T(8,128)(2,1)S(1)}, u32[]{:S(2)}, u32[]{:S(2)}) %collective-permute-start.22) | collective-permute-done | bytes 393248 | tf_op jit(solution)/shard_map/ppermute | solution.py:31
  172.7 13.6 %collective-permute-done.24 = bf16[1,2,96,2048]{3,2,1,0:T(8,128)(2,1)} collective-permute-done((bf16[1,2,96,2048]{3,2,1,0:T(8,128)(2,1)}, bf16[1,2,96,2048]{3,2,1,0:T(8,128)(2,1)}, u32[]{:S(2)}, u32[]{:S(2)}) %collective-permute-start.24) | collective-permute-done | bytes 786464 | tf_op jit(solution)/shard_map/ppermute | solution.py:31
  200.9 15.4 %collective-permute-done.10 = bf16[2,1,96,2048]{3,2,1,0:T(8,128)(2,1)S(1)} collective-permute-done((bf16[2,1,96,2048]{3,2,1,0:T(8,128)(2,1)S(1)}, bf16[2,1,96,2048]{3,2,1,0:T(8,128)(2,1)S(1)}, u32[]{:S(2)}, u32[]{:S(2)}) %collective-permute-start.10) | collective-permute-done | bytes 786464 | tf_op jit(solution)/shard_map/ppermute | solution.py:31
  219.6 7.8 %collective-permute-done.11 = bf16[1,1,96,2048]{3,2,1,0:T(8,128)(2,1)S(1)} collective-permute-done((bf16[1,1,96,2048]{3,2,1,0:T(8,128)(2,1)S(1)}, bf16[1,1,96,2048]{3,2,1,0:T(8,128)(2,1)S(1)}, u32[]{:S(2)}, u32[]{:S(2)}) %collective-permute-start.11) | collective-permute-done | bytes 393248 | tf_op jit(solution)/shard_map/ppermute | solution.py:31
  234.9 5.7 collective-permute-done.14
  246.0 14.8 %collective-permute-done.16 = bf16[1,2,96,2048]{3,2,1,0:T(8,128)(2,1)S(1)} collective-permute-done((bf16[1,2,96,2048]{3,2,1,0:T(8,128)(2,1)S(1)}, bf16[1,2,96,2048]{3,2,1,0:T(8,128)(2,1)S(1)}, u32[]{:S(2)}, u32[]{:S(2)}) %collective-permute-start.16) | collective-permute-done | bytes 786464 | tf_op jit(solution)/shard_map/ppermute | solution.py:31
  268.4 15.6 %fusion.43 = f32[1536,1408]{0,1:T(8,128)} fusion(bf16[1536,2048]{1,0:T(8,128)(2,1)} %bitcast.58, bf16[2048,1408]{1,0:T(8,128)(2,1)} %all-gather.9.cloned.1.call-done), kind=kOutput, calls=%fused_computation.203 | convolution fusion | flops 8858370048 | bytes 20709376 | tf_op jit(solution)/shard_map/dot_general | solution.py:23
  284.0 14.3 %multiply_convert_fusion.1 = (bf16[1536,704]{0,1:T(8,128)(2,1)}, bf16[1536,704]{0,1:T(8,128)(2,1)}, bf16[1536,704]{0,1:T(8,128)(2,1)S(1)}) fusion(f32[1536,1408]{0,1:T(8,128)} %fusion.43, bf16[1536,2048]{1,0:T(8,128)(2,1)} %bitcast.340, bf16[704,2048]{1,0:T(8,128)(2,1)} %all-gather.11.cloned.1.call-done), kind=kOutput, calls=%fused_computation.8 | convolution fusion | flops 4445405184 | bytes 24313856 | tf_op jit(solution)/shard_map/dot_general | solution.py:23
  299.6 8.9 %convolution_convert_fusion.5 = bf16[704,2048]{1,0:T(8,128)(2,1)} fusion(bf16[1536,704]{0,1:T(8,128)(2,1)S(1)} %get-tuple-element.50, bf16[1536,2048]{1,0:T(8,128)(2,1)} %bitcast.341), kind=kOutput, calls=%fused_computation.16 | convolution fusion | flops 4430626816 | bytes 11337728 | tf_op jit(solution)/shard_map/dot_general | solution.py:23
  313.1 6.5 %copy.245 = bf16[1536,1408]{1,0:T(8,128)(2,1)} copy(bf16[1536,1408]{0,1:T(8,128)(2,1)} %pad_maximum_fusion) | data formatting | bytes 8650752 | tf_op jit(solution)/shard_map/optimization_barrier | solution.py:27
  323.5 9.1 %convolution_convert_fusion.4 = bf16[768,2048]{1,0:T(8,128)(2,1)} fusion(bf16[768,1408]{1,0:T(8,128)(2,1)S(1)} %bitcast.353, bf16[2048,1408]{1,0:T(8,128)(2,1)} %all-gather.9.cloned.1.call-done), kind=kOutput, calls=%fused_computation.15 | convolution fusion | flops 4430757888 | bytes 11075584 | tf_op jit(solution)/shard_map/dot_general | solution.py:23
  333.1 5.6 collective-permute-done.30
  338.7 8.3 %add_convert_fusion.2 = bf16[768,2048]{1,0:T(8,128)(2,1)S(1)} fusion(bf16[768,2048]{1,0:T(8,128)(2,1)} %collective-permute-done.30, bf16[768,1408]{1,0:T(8,128)(2,1)} %bitcast.352, bf16[2048,1408]{1,0:T(8,128)(2,1)} %all-gather.9.cloned.1.call-done), kind=kOutput, calls=%fused_computation.4 | convolution fusion | flops 4433903616 | bytes 14221312 | tf_op jit(solution)/shard_map/dot_general | solution.py:23
  352.2 13.8 %convolution_convert_fusion = bf16[2048,1408]{1,0:T(8,128)(2,1)} fusion(bf16[1536,2048]{1,0:T(8,128)(2,1)} %bitcast.58, bf16[1536,1408]{0,1:T(8,128)(2,1)S(1)} %bitcast.332), kind=kOutput, calls=%fused_computation.1 | convolution fusion | flops 8861253632 | bytes 16384000 | tf_op jit(solution)/shard_map/dot_general | solution.py:23
  374.5 6.3 %collective-permute-done.32 = bf16[1,1,96,2048]{3,2,1,0:T(8,128)(2,1)S(1)} collective-permute-done((bf16[1,1,96,2048]{3,2,1,0:T(8,128)(2,1)S(1)}, bf16[1,1,96,2048]{3,2,1,0:T(8,128)(2,1)S(1)}, u32[]{:S(2)}, u32[]{:S(2)}) %collective-permute-start.32) | collective-permute-done | bytes 393248 | tf_op jit(solution)/shard_map/ppermute | solution.py:31
  389.9 7.2 %collective-permute-done.35 = bf16[1,1,96,2048]{3,2,1,0:T(8,128)(2,1)S(1)} collective-permute-done((bf16[1,1,96,2048]{3,2,1,0:T(8,128)(2,1)S(1)}, bf16[1,1,96,2048]{3,2,1,0:T(8,128)(2,1)S(1)}, u32[]{:S(2)}, u32[]{:S(2)}) %collective-permute-start.35) | collective-permute-done | bytes 393248 | tf_op jit(solution)/shard_map/ppermute | solution.py:31
  403.8 11.9 %collective-permute-done.37 = bf16[1,2,96,2048]{3,2,1,0:T(8,128)(2,1)} collective-permute-done((bf16[1,2,96,2048]{3,2,1,0:T(8,128)(2,1)}, bf16[1,2,96,2048]{3,2,1,0:T(8,128)(2,1)}, u32[]{:S(2)}, u32[]{:S(2)}) %collective-permute-start.37) | collective-permute-done | bytes 786464 | tf_op jit(solution)/shard_map/ppermute | solution.py:31
  445.8 5.6 convolution_convert_fusion.7
  451.4 7.5 %add_convert_fusion.1 = bf16[768,2048]{1,0:T(8,128)(2,1)} fusion(bf16[768,2048]{1,0:T(8,128)(2,1)} %collective-permute-done.43, bf16[768,704]{1,0:T(8,128)(2,1)} %bitcast.367, bf16[704,2048]{1,0:T(8,128)(2,1)} %all-gather.11.cloned.1.call-done), kind=kOutput, calls=%fused_computation.3 | convolution fusion | flops 2219311104 | bytes 10256384 | tf_op jit(solution)/shard_map/dot_general | solution.py:23
  458.9 29.1 %attention_backward.1 = (f32[256,1536]{1,0:T(8,128)S(1)}, f32[64,1536]{1,0:T(8,128)S(1)}, f32[64,1536]{1,0:T(8,128)S(1)}) custom-call(bf16[1536,64]{1,0:T(8,128)(2,1)S(1)} %copy.229.key_ref, bf16[64,1536]{1,0:T(8,128)(2,1)S(1)} %bitcast.327, bf16[1536,64]{1,0:T(8,128)(2,1)S(1)} %bitcast.325, bf16[256,1536]{1,0:T(8,128)(2,1)S(1)} %bitcast.323, ...), custom_call_target="tpu_custom_call" | custom-call | tf_op jit(solution)/shard_map/attention_backward/pallas_call | solution.py:346
  505.7 12.9 %collective-permute-done.44 = bf16[2,1,96,2048]{3,2,1,0:T(8,128)(2,1)S(1)} collective-permute-done((bf16[2,1,96,2048]{3,2,1,0:T(8,128)(2,1)S(1)}, bf16[2,1,96,2048]{3,2,1,0:T(8,128)(2,1)S(1)}, u32[]{:S(2)}, u32[]{:S(2)}) %collective-permute-start.44) | collective-permute-done | bytes 786464 | tf_op jit(solution)/shard_map/ppermute | solution.py:31
  526.2 6.4 %collective-permute-done.45 = bf16[1,1,96,2048]{3,2,1,0:T(8,128)(2,1)S(1)} collective-permute-done((bf16[1,1,96,2048]{3,2,1,0:T(8,128)(2,1)S(1)}, bf16[1,1,96,2048]{3,2,1,0:T(8,128)(2,1)S(1)}, u32[]{:S(2)}, u32[]{:S(2)}) %collective-permute-start.45) | collective-permute-done | bytes 393248 | tf_op jit(solution)/shard_map/ppermute | solution.py:31
  550.9 9.5 %all-to-all-done.3.grad_ref = bf16[8,64,1408]{2,1,0:T(8,128)(2,1)S(1)} async-done(((bf16[8,64,1408]{2,1,0:T(8,128)(2,1)}), bf16[8,64,1408]{2,1,0:T(8,128)(2,1)S(1)}, u32[]{:S(2)}, u32[]{:S(2)}) %all-to-all-start.3) | async-done | bytes 1441824 | tf_op jit(solution)/shard_map/all_to_all | solution.py:133
  570.5 10.5 %all-to-all-done.4 = bf16[8,64,384]{2,1,0:T(8,128)(2,1)S(1)} async-done(((bf16[8,64,384]{2,1,0:T(8,128)(2,1)}), bf16[8,64,384]{2,1,0:T(8,128)(2,1)S(1)}, u32[]{:S(2)}, u32[]{:S(2)}) %all-to-all-start.4) | async-done | bytes 393248 | tf_op jit(solution)/shard_map/all_to_all | solution.py:133
  596.6 14.8 %collective-permute-done.52 = bf16[1,1,96,2048]{3,2,1,0:T(8,128)(2,1)} collective-permute-done((bf16[1,1,96,2048]{3,2,1,0:T(8,128)(2,1)}, bf16[1,1,96,2048]{3,2,1,0:T(8,128)(2,1)}, u32[]{:S(2)}, u32[]{:S(2)}) %collective-permute-start.52) | collective-permute-done | bytes 393248 | tf_op jit(solution)/shard_map/ppermute | solution.py:31
  (446 shorter events, 243.1 us)
Async XLA Ops:
  16.3 69.1 %all-gather.7.cloned.1.call-start = ((), (), s32[]{:S(2)}) async-start(), calls=%async_computation.10 | async-start | bytes 1310720 | tf_op jit(solution)/shard_map/all_gather | solution.py:125
  25.5 21.7 %all-to-all-start.1 = ((f32[32,1,320]{2,1,0:T(1,128)}), f32[32,1,320]{2,1,0:T(1,128)S(1)}, u32[]{:S(2)}, u32[]{:S(2)}) async-start(f32[32,1,320]{2,1,0:T(1,128)} %broadcast_in_dim.8), calls=%async_computation.1 | async-start | bytes 98304 | tf_op jit(solution)/shard_map/all_to_all | solution.py:140
  39.9 75.3 %all-gather.5.cloned.1.call-start = ((), (), s32[]{:S(2)}) async-start(), calls=%async_computation.9 | async-start | bytes 1966080 | tf_op jit(solution)/shard_map/all_gather | solution.py:125
  49.4 35.9 %all-to-all-start.2 = ((bf16[8,64,1408]{2,1,0:T(8,128)(2,1)}), bf16[8,64,1408]{2,1,0:T(8,128)(2,1)S(1)}, u32[]{:S(2)}, u32[]{:S(2)}) async-start(bf16[8,64,1408]{2,1,0:T(8,128)(2,1)} %split_units.1), calls=%async_computation.2 | async-start | bytes 2883584 | tf_op jit(solution)/shard_map/all_to_all | solution.py:133
  53.0 215.4 %all-gather.9.cloned.1.call-start = ((), (), s32[]{:S(2)}) async-start(), calls=%async_computation.11 | async-start | bytes 7208960 | tf_op jit(solution)/shard_map/all_gather | solution.py:125
  54.0 26.1 %collective-permute-start = (bf16[1,1,96,2048]{3,2,1,0:T(8,128)(2,1)}, bf16[1,1,96,2048]{3,2,1,0:T(8,128)(2,1)S(1)}, u32[]{:S(2)}, u32[]{:S(2)}) collective-permute-start(bf16[1,1,96,2048]{3,2,1,0:T(8,128)(2,1)} %get-tuple-element.105), channel_id=1, source_target_pairs={{0,2},{1,3},{2,0},{3,1},{4,6},{5,7},{6,4},{7,5},{8,10},{9,11},{10,... | collective-permute-start | bytes 1179656 | tf_op jit(solution)/shard_map/ppermute | solution.py:31
  56.0 27.8 %collective-permute-start.4 = (bf16[1,1,96,2048]{3,2,1,0:T(8,128)(2,1)S(1)}, bf16[1,1,96,2048]{3,2,1,0:T(8,128)(2,1)S(1)}, u32[]{:S(2)}, u32[]{:S(2)}) collective-permute-start(bf16[1,1,96,2048]{3,2,1,0:T(8,128)(2,1)S(1)} %get-tuple-element.106), channel_id=1, source_target_pairs={{0,4},{1,5},{2,6},{3,7},{4,0},{5,1},{6,2},{7,3},{8,12},{9,13},{10,... | collective-permute-start | bytes 1179656 | tf_op jit(solution)/shard_map/ppermute | solution.py:31
  82.3 22.5 %collective-permute-start.1 = (bf16[1,2,96,2048]{3,2,1,0:T(8,128)(2,1)}, bf16[1,2,96,2048]{3,2,1,0:T(8,128)(2,1)}, u32[]{:S(2)}, u32[]{:S(2)}) collective-permute-start(bf16[1,2,96,2048]{3,2,1,0:T(8,128)(2,1)} %maximum_select_fusion.1), channel_id=1, source_target_pairs={{0,1},{1,0},{2,3},{3,2},{4,5},{5,4},{6,7},{7,6},{8,9},{9,8},{10,11... | collective-permute-start | bytes 2359304 | tf_op jit(solution)/shard_map/ppermute | solution.py:31
  82.3 20.3 %collective-permute-start.2 = (bf16[1,2,96,2048]{3,2,1,0:T(8,128)(2,1)}, bf16[1,2,96,2048]{3,2,1,0:T(8,128)(2,1)}, u32[]{:S(2)}, u32[]{:S(2)}) collective-permute-start(bf16[1,2,96,2048]{3,2,1,0:T(8,128)(2,1)} %maximum_select_fusion.1), channel_id=1, source_target_pairs={{0,4},{1,5},{2,6},{3,7},{4,0},{5,1},{6,2},{7,3},{8,12},{9,13},{10,... | collective-permute-start | bytes 2359304 | tf_op jit(solution)/shard_map/ppermute | solution.py:31
  86.5 197.5 %all-gather.11.cloned.1.call-start = ((), (), s32[]{:S(2)}) async-start(), calls=%async_computation.12 | async-start | bytes 3604480 | tf_op jit(solution)/shard_map/all_gather | solution.py:125
  88.2 22.9 %collective-permute-start.5 = (bf16[2,1,96,2048]{3,2,1,0:T(8,128)(2,1)}, bf16[2,1,96,2048]{3,2,1,0:T(8,128)(2,1)S(1)}, u32[]{:S(2)}, u32[]{:S(2)}) collective-permute-start(bf16[2,1,96,2048]{3,2,1,0:T(8,128)(2,1)} %maximum_select_fusion.3), channel_id=1, source_target_pairs={{0,1},{1,0},{2,3},{3,2},{4,5},{5,4},{6,7},{7,6},{8,9},{9,8},{10,11... | collective-permute-start | bytes 2359304 | tf_op jit(solution)/shard_map/ppermute | solution.py:31
  154.5 38.4 %collective-permute-start.9 = (bf16[768,2048]{1,0:T(8,128)(2,1)}, bf16[768,2048]{1,0:T(8,128)(2,1)}, u32[]{:S(2)}, u32[]{:S(2)}) collective-permute-start(bf16[768,2048]{1,0:T(8,128)(2,1)} %convolution_convert_fusion.3), channel_id=1, source_target_pairs={{0,1},{1,0},{2,3},{3,2},{4,5},{5,4},{6,7},{7,6},{8,9},{9,8},{10,11... | collective-permute-start | bytes 9437192 | tf_op jit(solution)/shard_map/ppermute | solution.py:31
  169.5 273.9 %reduce-scatter.5.cloned.1.call-start = ((), (), s32[]{:S(2)}) async-start(), calls=%async_computation.13 | async-start | bytes 3604480 | tf_op jit(solution)/shard_map/reduce_scatter | solution.py:129
  169.8 30.1 %collective-permute-start.27 = (bf16[2,1,96,2048]{3,2,0,1:T(8,128)(2,1)}, bf16[2,1,96,2048]{3,2,0,1:T(8,128)(2,1)S(1)}, u32[]{:S(2)}, u32[]{:S(2)}) collective-permute-start(bf16[2,1,96,2048]{3,2,0,1:T(8,128)(2,1)} %bitcast_select_fusion), channel_id=1, source_target_pairs={{0,1},{1,0},{2,3},{3,2},{4,5},{5,4},{6,7},{7,6},{8,9},{9,8},{10,11... | collective-permute-start | bytes 2359304 | tf_op jit(solution)/shard_map/ppermute | solution.py:31
  187.6 54.8 %collective-permute-start.29 = (bf16[2,1,96,2048]{3,2,0,1:T(8,128)(2,1)}, bf16[2,1,96,2048]{3,2,0,1:T(8,128)(2,1)S(1)}, u32[]{:S(2)}, u32[]{:S(2)}) collective-permute-start(bf16[2,1,96,2048]{3,2,0,1:T(8,128)(2,1)} %collective-permute-done.28), channel_id=1, source_target_pairs={{0,1},{1,0},{2,3},{3,2},{4,5},{5,4},{6,7},{7,6},{8,9},{9,8},{10,11... | collective-permute-start | bytes 2359304 | tf_op jit(solution)/shard_map/ppermute | solution.py:31
  196.3 20.0 %collective-permute-start.10 = (bf16[2,1,96,2048]{3,2,1,0:T(8,128)(2,1)S(1)}, bf16[2,1,96,2048]{3,2,1,0:T(8,128)(2,1)S(1)}, u32[]{:S(2)}, u32[]{:S(2)}) collective-permute-start(bf16[2,1,96,2048]{3,2,1,0:T(8,128)(2,1)S(1)} %dynamic-slice_bitcast_fusion.7), channel_id=1, source_target_pairs={{0,2},{1,3},{2,0},{3,1},{4,6},{5,7},{6,4},{7,5},{8,10},{9,11},{10,... | collective-permute-start | bytes 2359304 | tf_op jit(solution)/shard_map/ppermute | solution.py:31
  240.8 20.0 %collective-permute-start.15 = (bf16[1,2,96,2048]{3,2,1,0:T(8,128)(2,1)S(1)}, bf16[1,2,96,2048]{3,2,1,0:T(8,128)(2,1)S(1)}, u32[]{:S(2)}, u32[]{:S(2)}) collective-permute-start(bf16[1,2,96,2048]{3,2,1,0:T(8,128)(2,1)S(1)} %maximum_select_fusion.5), channel_id=1, source_target_pairs={{0,1},{1,0},{2,3},{3,2},{4,5},{5,4},{6,7},{7,6},{8,9},{9,8},{10,11... | collective-permute-start | bytes 2359304 | tf_op jit(solution)/shard_map/ppermute | solution.py:31
  243.5 22.1 %collective-permute-start.19 = (bf16[2,1,96,2048]{3,2,1,0:T(8,128)(2,1)S(1)}, bf16[2,1,96,2048]{3,2,1,0:T(8,128)(2,1)S(1)}, u32[]{:S(2)}, u32[]{:S(2)}) collective-permute-start(bf16[2,1,96,2048]{3,2,1,0:T(8,128)(2,1)S(1)} %maximum_select_fusion.7), channel_id=1, source_target_pairs={{0,1},{1,0},{2,3},{3,2},{4,5},{5,4},{6,7},{7,6},{8,9},{9,8},{10,11... | collective-permute-start | bytes 2359304 | tf_op jit(solution)/shard_map/ppermute | solution.py:31
  333.1 203.6 %reduce-scatter.7.cloned.1.call-start = ((), (), s32[]{:S(2)}) async-start(), calls=%async_computation.14 | async-start | bytes 7208960 | tf_op jit(solution)/shard_map/reduce_scatter | solution.py:129
  348.4 20.1 %collective-permute-start.31 = (bf16[2,1,96,2048]{3,2,1,0:T(8,128)(2,1)}, bf16[2,1,96,2048]{3,2,1,0:T(8,128)(2,1)}, u32[]{:S(2)}, u32[]{:S(2)}) collective-permute-start(bf16[2,1,96,2048]{3,2,1,0:T(8,128)(2,1)} %dynamic-slice_bitcast_fusion.5), channel_id=1, source_target_pairs={{0,2},{1,3},{2,0},{3,1},{4,6},{5,7},{6,4},{7,5},{8,10},{9,11},{10,... | collective-permute-start | bytes 2359304 | tf_op jit(solution)/shard_map/ppermute | solution.py:31
  350.6 20.6 %collective-permute-start.33 = (bf16[1,2,96,2048]{3,2,1,0:T(8,128)(2,1)}, bf16[1,2,96,2048]{3,2,1,0:T(8,128)(2,1)}, u32[]{:S(2)}, u32[]{:S(2)}) collective-permute-start(bf16[1,2,96,2048]{3,2,1,0:T(8,128)(2,1)} %dynamic-slice_bitcast_fusion.4), channel_id=1, source_target_pairs={{0,4},{1,5},{2,6},{3,7},{4,0},{5,1},{6,2},{7,3},{8,12},{9,13},{10,... | collective-permute-start | bytes 2359304 | tf_op jit(solution)/shard_map/ppermute | solution.py:31
  399.1 151.8 %reduce-scatter.9.cloned.1.call-start = ((), (), s32[]{:S(2)}) async-start(), calls=%async_computation.15 | async-start | bytes 1966080 | tf_op jit(solution)/shard_map/reduce_scatter | solution.py:129
  400.9 23.4 %collective-permute-start.40 = (bf16[2,1,96,2048]{3,2,1,0:T(8,128)(2,1)S(1)}, bf16[2,1,96,2048]{3,2,1,0:T(8,128)(2,1)S(1)}, u32[]{:S(2)}, u32[]{:S(2)}) collective-permute-start(bf16[2,1,96,2048]{3,2,1,0:T(8,128)(2,1)S(1)} %maximum_select_fusion.14), channel_id=1, source_target_pairs={{0,1},{1,0},{2,3},{3,2},{4,5},{5,4},{6,7},{7,6},{8,9},{9,8},{10,11... | collective-permute-start | bytes 2359304 | tf_op jit(solution)/shard_map/ppermute | solution.py:31
  504.1 37.0 %collective-permute-start.48 = (bf16[768,2048]{1,0:T(8,128)(2,1)}, bf16[768,2048]{1,0:T(8,128)(2,1)}, u32[]{:S(2)}, u32[]{:S(2)}) collective-permute-start(bf16[768,2048]{1,0:T(8,128)(2,1)} %convolution_convert_fusion.1), channel_id=1, source_target_pairs={{0,1},{1,0},{2,3},{3,2},{4,5},{5,4},{6,7},{7,6},{8,9},{9,8},{10,11... | collective-permute-start | bytes 9437192 | tf_op jit(solution)/shard_map/ppermute | solution.py:31
  504.1 20.4 %collective-permute-start.46 = (bf16[1,2,96,2048]{3,2,1,0:T(8,128)(2,1)S(1)}, bf16[1,2,96,2048]{3,2,1,0:T(8,128)(2,1)S(1)}, u32[]{:S(2)}, u32[]{:S(2)}) collective-permute-start(bf16[1,2,96,2048]{3,2,1,0:T(8,128)(2,1)S(1)} %dynamic-slice_bitcast_fusion.2), channel_id=1, source_target_pairs={{0,4},{1,5},{2,6},{3,7},{4,0},{5,1},{6,2},{7,3},{8,12},{9,13},{10,... | collective-permute-start | bytes 2359304 | tf_op jit(solution)/shard_map/ppermute | solution.py:31
  536.7 23.6 %all-to-all-start.3 = ((bf16[8,64,1408]{2,1,0:T(8,128)(2,1)}), bf16[8,64,1408]{2,1,0:T(8,128)(2,1)S(1)}, u32[]{:S(2)}, u32[]{:S(2)}) async-start(bf16[8,64,1408]{2,1,0:T(8,128)(2,1)} %bitcast.366), calls=%async_computation.5 | async-start | bytes 2883584 | tf_op jit(solution)/shard_map/all_to_all | solution.py:133
  540.3 52.5 %reduce-scatter.11.cloned.1.call-start = ((), (), s32[]{:S(2)}) async-start(), calls=%async_computation.16 | async-start | bytes 1310720 | tf_op jit(solution)/shard_map/reduce_scatter | solution.py:129
  548.9 33.8 %collective-permute-start.49 = (bf16[2,1,96,2048]{3,2,1,0:T(8,128)(2,1)}, bf16[2,1,96,2048]{3,2,1,0:T(8,128)(2,1)}, u32[]{:S(2)}, u32[]{:S(2)}) collective-permute-start(bf16[2,1,96,2048]{3,2,1,0:T(8,128)(2,1)} %dynamic-slice_bitcast_fusion.1), channel_id=1, source_target_pairs={{0,2},{1,3},{2,0},{3,1},{4,6},{5,7},{6,4},{7,5},{8,10},{9,11},{10,... | collective-permute-start | bytes 2359304 | tf_op jit(solution)/shard_map/ppermute | solution.py:31
  560.3 20.7 %all-to-all-start.4 = ((bf16[8,64,384]{2,1,0:T(8,128)(2,1)}), bf16[8,64,384]{2,1,0:T(8,128)(2,1)S(1)}, u32[]{:S(2)}, u32[]{:S(2)}) async-start(bf16[8,64,384]{2,1,0:T(8,128)(2,1)} %bitcast.379), calls=%async_computation.7 | async-start | bytes 786432 | tf_op jit(solution)/shard_map/all_to_all | solution.py:133
  565.9 22.8 %collective-permute-start.51 = (bf16[1,2,96,2048]{3,2,1,0:T(8,128)(2,1)}, bf16[1,2,96,2048]{3,2,1,0:T(8,128)(2,1)}, u32[]{:S(2)}, u32[]{:S(2)}) collective-permute-start(bf16[1,2,96,2048]{3,2,1,0:T(8,128)(2,1)} %dynamic-slice_bitcast_fusion), channel_id=1, source_target_pairs={{0,4},{1,5},{2,6},{3,7},{4,0},{5,1},{6,2},{7,3},{8,12},{9,13},{10,... | collective-permute-start | bytes 2359304 | tf_op jit(solution)/shard_map/ppermute | solution.py:31
  590.8 20.6 %collective-permute-start.52 = (bf16[1,1,96,2048]{3,2,1,0:T(8,128)(2,1)}, bf16[1,1,96,2048]{3,2,1,0:T(8,128)(2,1)}, u32[]{:S(2)}, u32[]{:S(2)}) collective-permute-start(bf16[1,1,96,2048]{3,2,1,0:T(8,128)(2,1)} %dynamic-slice_convert_fusion), channel_id=1, source_target_pairs={{0,2},{1,3},{2,0},{3,1},{4,6},{5,7},{6,4},{7,5},{8,10},{9,11},{10,... | collective-permute-start | bytes 1179656 | tf_op jit(solution)/shard_map/ppermute | solution.py:31
  592.8 24.1 %collective-permute-start.53 = (bf16[64,2048]{1,0:T(8,128)(2,1)}, bf16[64,2048]{1,0:T(8,128)(2,1)S(1)}, u32[]{:S(2)}, u32[]{:S(2)}) collective-permute-start(bf16[64,2048]{1,0:T(8,128)(2,1)} %reduce-scatter.11.cloned.1.call-done), channel_id=1, source_target_pairs={{0,0},{8,1},{16,2},{24,3},{1,4},{9,5},{17,6},{25,7},{2,8},{10,9},{... | collective-permute-start | bytes 786440 | tf_op jit(solution)/shard_map/ppermute | solution.py:510
  (111 other events, 1100.6 us)
Sparse Core Ops, SparseCore 0:
  24.8 37.7 all-gather.6
  64.8 36.5 all-gather.4
  103.5 105.5 all-gather.8
  210.6 57.4 all-gather.10
  333.2 54.7 reduce-scatter.4
  399.2 101.5 reduce-scatter.6
  503.1 35.7 reduce-scatter.8
  543.5 26.7 reduce-scatter.10

commit v2 on v1

v2 whole, which is shorter than its diff:
```python
import functools

import jax
import jax.numpy as jnp
from jax import lax
from jax.experimental import pallas as pl
from jax.experimental.pallas import tpu as pltpu
from jax.sharding import PartitionSpec as P

H = 32
KV = 4
HD = 64
HALF = HD // 2

EPSILON = 1e-05
MASKED = -1e30
BOTH = ("seq", "ctx")
f32 = jnp.float32
bf16 = jnp.bfloat16
LIGHT = pl.CostEstimate(flops=0, transcendentals=0, bytes_accessed=0)


def dot(left, right, contract, out=f32):
    return lax.dot_general(left, right, (contract, ((), ())), preferred_element_type=f32).astype(out)


def after(value, *others):
    return lax.optimization_barrier((value, *others))[0]


def swap(value, step, count):
    return lax.ppermute(value, "ctx", [(i, i ^ step) for i in range(count)])


def blank(shape, dtype):
    return pl.pallas_call(
        lambda out_ref: None,
        out_shape=jax.ShapeDtypeStruct(shape, dtype),
        out_specs=pl.BlockSpec(memory_space=pl.ANY),
        name="blank",
    )()


def chip_bits():
    me = lax.axis_index("ctx")
    count = lax.axis_size("ctx")
    bits = [1 << at for at in range(1, count.bit_length() - 1)]
    return [(step, (me // step) % 2) for step in bits]


def gather_first(value):
    count = lax.axis_size("ctx")
    bits = chip_bits()
    half = value.shape[0] // 2
    steps = (bits[0][0], bits[-1][0])
    parts = [value[:half], value[half:]]
    return [(part, swap(part, step, count)) for part, step in zip(parts, steps)]


def gather_second(first):
    count = lax.axis_size("ctx")
    bits = chip_bits()
    parts = []
    for which, (current, arrived) in enumerate(first):
        half, depth = current.shape
        order = list(range(len(bits)))
        if which:
            order.reverse()
        current = current.reshape((1,) * len(bits) + (half, depth))
        arrived = arrived.reshape(current.shape)
        for at in order:
            step, bit = bits[at]
            axis = len(bits) - 1 - at
            if at != order[0]:
                arrived = swap(current, step, count)
            if at != order[-1]:
                current = jnp.where(
                    bit == 0,
                    jnp.concatenate([current, arrived], axis),
                    jnp.concatenate([arrived, current], axis),
                )
        parts.append((current, arrived))
    return parts


def place_kernel(bits, steps, natural, change, *refs):
    parts = 4 * 2
    given, gains = refs[:parts], refs[parts:-4]
    whole, held, ready, done = refs[-4:]
    me = lax.axis_index("ctx")
    core = lax.rem(me, 2)
    arrivals = [pltpu.make_async_copy(ref, held.at[i], ready.at[i]) for i, ref in enumerate(given)]
    copies = []
    for arrival in arrivals:
        arrival.start()
    for number, arrival in enumerate(arrivals):
        which, late, there = number // 4, number // 2 % 2, number % 2
        at = 0 if which else bits - 1
        axis = bits - 1 - at
        index = lax.rem(me // steps[at], 2)
        index = 1 - index if late else index
        owner = 1 - core if there else core
        spot = [slice(None)] * bits
        spot[axis] = index
        arrival.wait()
        if change is not None:
            held[number] = change(held[number], *[ref[...] for ref in gains])
        place = (*spot, owner, which) if natural else (there, *spot, which)
        copy = pltpu.make_async_copy(held.at[number], whole.at[place], done.at[number])
        copy.start()
        copies.append(copy)
    for copy in copies:
        copy.wait()


def gather_place(parts, natural=True, change=None, gains=()):
    count = lax.axis_size("ctx")
    steps = tuple(step for step, _ in chip_bits())
    half, depth = parts[0][0].shape[-2:]
    pieces = []
    for pair in parts:
        for part in pair:
            pieces += [part, swap(part, 1, count)]
    pieces = [piece.reshape((2,) * (len(steps) - 1) + (half, depth)) for piece in pieces]
    anywhere = pl.BlockSpec(memory_space=pl.ANY)
    dtype = pieces[0].dtype
    whole = pl.pallas_call(
        functools.partial(place_kernel, len(steps), steps, natural, change),
        in_specs=[anywhere] * len(pieces) + [pl.BlockSpec(memory_space=pltpu.VMEM)] * len(gains),
        out_specs=anywhere,
        out_shape=jax.ShapeDtypeStruct((2,) * len(steps) + (2, 2, half, depth), dtype),
        scratch_shapes=[
            pltpu.VMEM((len(pieces),) + pieces[0].shape, dtype),
            pltpu.SemaphoreType.DMA((len(pieces),)),
            pltpu.SemaphoreType.DMA((len(pieces),)),
        ],
        compiler_params=pltpu.CompilerParams(vmem_limit_bytes=48 * 1024 * 1024),
        cost_estimate=LIGHT,
        name="place",
    )(*pieces, *gains)
    return whole.reshape(2 * count * half, depth)


def send_chips(value):
    count = lax.axis_size("ctx")
    return {step: swap(value, step, count) if step else value for step in range(0, count, 2)}


def place_chips(pieces, natural=True):
    count = lax.axis_size("ctx")
    me = lax.axis_index("ctx")
    whole = blank((count,) + pieces[0].shape, pieces[0].dtype)
    for step, piece in pieces.items():
        for there in range(2):
            spot = me ^ step ^ there if natural else there * (count // 2) + (me ^ step) // 2
            piece = swap(piece, 1, count) if there else piece
            whole = lax.dynamic_update_index_in_dim(whole, piece, spot, 0)
    return whole.reshape((-1,) + pieces[0].shape[1:])


def double(value, step):
    seqs = lax.axis_size("seq")
    bit = (lax.axis_index("seq") // step) % 2
    other = lax.ppermute(value, "seq", [(i, i ^ step) for i in range(seqs)])
    whole = jnp.where(bit == 0, jnp.concatenate([value, other]), jnp.concatenate([other, value]))
    return whole, other


def double_to(value, end):
    step, other = 1, value
    while step < end:
        value, other = double(value, step)
        step *= 2
    return value, other


def head_order():
    seqs, ranks = lax.axis_size("seq"), lax.axis_size("ctx")
    return [(i, (i % seqs) * ranks + i // seqs) for i in range(seqs * ranks)]


def of_core(value, core):
    count = lax.axis_size("ctx")
    blocks = value.reshape(count // 2, 2, value.shape[0] // count, value.shape[1])
    return lax.dynamic_index_in_dim(blocks, core, 1, keepdims=False).reshape(-1, value.shape[1])


def blocks_of(pairs):
    return pairs.reshape(lax.axis_size("ctx") // 2, -1, pairs.shape[1])


def pair_up(left, right, contract):
    core = lax.axis_index("ctx") % 2
    away = dot(of_core(left, 1 - core), right, contract, bf16)
    arrived = swap(away, 1, lax.axis_size("ctx"))
    stay = after(of_core(left, core), away)
    return blocks_of((dot(stay, right, contract) + arrived.astype(f32)).astype(bf16))


def scatter_step(current, at):
    step, bit = chip_bits()[at]
    axis = current.ndim - 3 - at
    away = lax.dynamic_slice_in_dim(current, 1 - bit, 1, axis).astype(bf16)
    stay = lax.dynamic_slice_in_dim(current, bit, 1, axis).astype(f32)
    return stay, swap(away, step, lax.axis_size("ctx"))


def scatter_first(pairs):
    bits = len(chip_bits())
    half, depth = pairs.shape[1] // 2, pairs.shape[2]
    pairs = pairs.reshape((2,) * bits + (2, half, depth))
    return scatter_step(pairs[..., 0, :, :], 0), scatter_step(pairs[..., 1, :, :], bits - 1)


def scatter_rest(first):
    bits = len(chip_bits())
    low, high = first
    for at in range(1, bits):
        low = scatter_step(low[0] + low[1].astype(f32), at)
        high = scatter_step(high[0] + high[1].astype(f32), bits - 1 - at)
    sums = [stay + arrived.astype(f32) for stay, arrived in (low, high)]
    return jnp.concatenate([part.reshape(part.shape[-2:]) for part in sums])


def scatter_pairs(pairs):
    return scatter_rest(scatter_first(pairs))


def gather_seq(value):
    return lax.all_gather(value, "seq", axis=0, tiled=True)


def scatter_seq(value):
    return lax.psum_scatter(value, "seq", scatter_dimension=0, tiled=True)


def exchange_ctx(value):
    return lax.all_to_all(value, "ctx", 0, 0)


def gather_small(spread, segments):
    seqs, ranks = lax.axis_size("seq"), lax.axis_size("ctx")
    me = lax.axis_index("ctx")
    line = jnp.concatenate([spread.reshape(1, -1), segments.astype(f32)], axis=1)
    chips = send_chips(line)
    others = {step: swap(piece, 1, ranks) for step, piece in chips.items()}
    table = jnp.zeros((ranks, line.shape[1]), f32)
    for step, piece in chips.items():
        table = lax.dynamic_update_slice_in_dim(table, piece, me ^ step, 0)
        table = lax.dynamic_update_slice_in_dim(table, others[step], me ^ step ^ 1, 0)
    width = spread.size
    gains = table[:, :width].reshape(ranks, seqs, 2, -1).transpose(2, 1, 0, 3).reshape(2, -1)
    return gains[:1], gains[1:], table[:, width:].reshape(1, -1), list(others.values())


def unit_pieces(seqs, ranks, units):
    wide = seqs * units
    main = wide // 128 * 128
    for rank in range(ranks):
        for which in range(2):
            for seq in range(seqs):
                first, at, end = (seq * ranks + rank) * units, seq * units, (seq + 1) * units
                if at < main:
                    yield rank, which, first, which * main + at, min(end, main) - at
                if end > main:
                    cut = max(at, main)
                    to = 2 * main + which * (wide - main) + cut - main
                    yield rank, which, first + cut - at, to, end - cut


def split_kernel(pieces, gate_ref, up_ref, out_ref):
    refs = (gate_ref, up_ref)
    for rank, which, first, to, size in pieces:
        out_ref[rank, :, to : to + size] = refs[which][:, first : first + size]


def split_units(gate, up, units):
    seqs, ranks = lax.axis_size("seq"), lax.axis_size("ctx")
    return pl.pallas_call(
        functools.partial(split_kernel, tuple(unit_pieces(seqs, ranks, units))),
        out_shape=jax.ShapeDtypeStruct((ranks, gate.shape[0], 2 * seqs * units), gate.dtype),
        compiler_params=pltpu.CompilerParams(vmem_limit_bytes=48 * 1024 * 1024),
        name="split_units",
    )(gate, up)


def join_kernel(pieces, grad_ref, gate_ref, up_ref, grad_gate_ref, grad_up_ref, sum_ref):
    refs = (grad_gate_ref, grad_up_ref)
    for rank, which, first, to, size in pieces:
        refs[which][:, first : first + size] = grad_ref[rank, :, to : to + size].astype(f32)
    terms = grad_gate_ref[...] * gate_ref[...].astype(f32)
    terms = terms + grad_up_ref[...] * up_ref[...].astype(f32)
    sum_ref[...] = jnp.sum(terms, axis=1, keepdims=True)


def join_units(grad, gate, up, units):
    seqs, ranks = lax.axis_size("seq"), lax.axis_size("ctx")
    whole = jax.ShapeDtypeStruct(gate.shape, f32)
    return pl.pallas_call(
        functools.partial(join_kernel, tuple(unit_pieces(seqs, ranks, units))),
        out_shape=[whole, whole, jax.ShapeDtypeStruct((gate.shape[0], 1), f32)],
        compiler_params=pltpu.CompilerParams(vmem_limit_bytes=48 * 1024 * 1024),
        name="join_units",
    )(grad, gate, up)


def spans_of(hidden):
    main = hidden // 128 * 128
    return [(0, main)] + ([(main, hidden - main)] if main < hidden else [])


def units_kernel(hidden, row_ref, weight_ref, out_ref, slope_ref, swished_ref):
    both = dot(row_ref[...], weight_ref[...], ((1,), (0,)))
    for first, size in spans_of(hidden):
        span = slice(first, first + size)
        gate = both[:, 2 * first : 2 * first + size]
        upward = both[:, 2 * first + size : 2 * first + 2 * size]
        sigmoid_gate = jax.nn.sigmoid(gate)
        swished = gate * sigmoid_gate
        out_ref[:, span] = (swished * upward).astype(bf16)
        slope_ref[:, span] = (upward * sigmoid_gate * (1.0 + gate * (1.0 - sigmoid_gate))).astype(bf16)
        swished_ref[:, span] = swished.astype(bf16)


def units_back_kernel(hidden, grad_ref, down_ref, slope_ref, swished_ref, weight_ref, *refs):
    *given, out_ref, product_ref = refs
    grads = dot(grad_ref[...], down_ref[...], ((1,), (1,)))
    for first, size in spans_of(hidden):
        span = slice(first, first + size)
        grad = grads[:, span]
        out_ref[:, 2 * first : 2 * first + size] = (grad * slope_ref[:, span].astype(f32)).astype(bf16)
        out_ref[:, 2 * first + size : 2 * first + 2 * size] = (
            grad * swished_ref[:, span].astype(f32)
        ).astype(bf16)
    product = dot(out_ref[...], weight_ref[...], ((1,), (1,)))
    for ref in given:
        product = product + ref[...].astype(f32)
    product_ref[...] = product.astype(bf16)


def product_kernel(contract, row_ref, weight_ref, *refs):
    out = dot(row_ref[...], weight_ref[...], contract)
    for ref in refs[:-1]:
        out = out + ref[...].astype(f32)
    refs[-1][...] = out.astype(bf16)


def by_rows(kernel, rows, weight, widths, name, part=None, also=None):
    number, parts = part or (0, 1)
    count = rows[0].shape[0] // parts
    block = 256 if count % 256 == 0 else count

    def spec(array):
        first = number * (count // block) if array.shape[0] != count else 0
        return pl.BlockSpec((block, array.shape[1]), lambda i: (i + first, 0))

    arrays = list(rows)
    specs = [spec(array) for array in rows]
    for place, whole in ((1, weight), also or (0, None)):
        if whole is not None:
            arrays.insert(place, whole)
            specs.insert(place, pl.BlockSpec(whole.shape, lambda i: (0, 0)))
    return pl.pallas_call(
        kernel,
        grid=(count // block,),
        in_specs=specs,
        out_specs=[pl.BlockSpec((block, width), lambda i: (i, 0)) for width in widths],
        out_shape=[jax.ShapeDtypeStruct((count, width), bf16) for width in widths],
        compiler_params=pltpu.CompilerParams(vmem_limit_bytes=56 * 1024 * 1024),
        cost_estimate=LIGHT,
        name=name,
    )(*arrays)


def product(rows, weight, contract, part, name):
    kernel = functools.partial(product_kernel, contract)
    width = weight.shape[1 - contract[1][0]]
    return by_rows(kernel, rows, weight, [width], name, part)[0]


def attention_block(length):
    return 512 if length % 512 == 0 else length


def forward_kernel(
    block, heads, count, key_ref, value_ref, query_ref, start_ref, out_ref, out_n_ref, lse_ref
):
    def queries(at):
        end = (at + 1) * block
        rows = lax.broadcasted_iota(jnp.int32, (end, block), 0)
        columns = lax.broadcasted_iota(jnp.int32, (end, block), 1) + at * block
        allowed = (rows >= start_ref[...]) & (rows <= columns)
        for head in range(heads):
            span = slice(head * HD, (head + 1) * HD)
            scores = dot(key_ref[:end, :], query_ref[span, :], ((1,), (0,)))
            scores = jnp.where(allowed, scores, MASKED)
            top = jnp.max(scores, axis=0, keepdims=True)
            weights = jnp.exp(scores - top)
            mass = jnp.sum(weights, axis=0, keepdims=True)
            out = dot(value_ref[:, :end], weights.astype(bf16), ((1,), (0,))) / mass
            out_ref[span, :] = out
            out_n_ref[:, span] = out.T.astype(bf16)
            lse_ref[head : head + 1, :] = top + jnp.log(mass)

    for at in range(count):
        pl.when(pl.program_id(0) == at)(functools.partial(queries, at))


def attention_forward(query_t, key_n, value_t, start):
    width, length = query_t.shape
    heads = width // HD
    block = attention_block(length)
    return pl.pallas_call(
        functools.partial(forward_kernel, block, heads, length // block),
        grid=(length // block,),
        in_specs=[
            pl.BlockSpec((length, HD), lambda i: (0, 0)),
            pl.BlockSpec((HD, length), lambda i: (0, 0)),
            pl.BlockSpec((width, block), lambda i: (0, i)),
            pl.BlockSpec((1, block), lambda i: (0, i)),
        ],
        out_specs=[
            pl.BlockSpec((width, block), lambda i: (0, i)),
            pl.BlockSpec((block, width), lambda i: (i, 0)),
            pl.BlockSpec((heads, block), lambda i: (0, i)),
        ],
        out_shape=[
            jax.ShapeDtypeStruct((width, length), f32),
            jax.ShapeDtypeStruct((length, width), bf16),
            jax.ShapeDtypeStruct((heads, length), f32),
        ],
        compiler_params=pltpu.CompilerParams(vmem_limit_bytes=56 * 1024 * 1024),
        cost_estimate=LIGHT,
        name="attention_forward",
    )(key_n, value_t, query_t, start)


def backward_kernel(
    block,
    heads,
    count,
    key_ref,
    key_t_ref,
    value_ref,
    query_ref,
    grad_ref,
    out_ref,
    lse_ref,
    start_ref,
    grad_query_ref,
    grad_key_ref,
    grad_value_ref,
    query_n,
    grad_n,
    delta,
):
    spans = [slice(head * HD, (head + 1) * HD) for head in range(heads)]

    @pl.when(pl.program_id(0) == 0)
    def _():
        grad_query_ref[...] = jnp.zeros_like(grad_query_ref)
        for head, span in enumerate(spans):
            grads = grad_ref[span, :].astype(f32)
            query_n[head] = query_ref[span, :].astype(f32).T.astype(bf16)
            grad_n[head] = grads.T.astype(bf16)
            delta[head : head + 1, :] = jnp.sum(grads * out_ref[span, :], axis=0, keepdims=True)

    def keys(at):
        low = at * block
        shape = (block, (count - at) * block)
        rows = lax.broadcasted_iota(jnp.int32, shape, 0) + low
        columns = lax.broadcasted_iota(jnp.int32, shape, 1) + low
        allowed = (rows >= start_ref[:, low:]) & (rows <= columns)
        key_sum = jnp.zeros((block, HD), f32)
        value_sum = jnp.zeros((block, HD), f32)
        for head, span in enumerate(spans):
            scores = dot(key_ref[...], query_ref[span, low:], ((1,), (0,)))
            scores = jnp.where(allowed, scores, MASKED)
            probs = jnp.exp(scores - lse_ref[head : head + 1, low:])
            value_sum += dot(probs.astype(bf16), grad_n[head, low:, :], ((1,), (0,)))
            grad_probs = dot(value_ref[...], grad_ref[span, low:], ((1,), (0,)))
            grad_scores = (probs * (grad_probs - delta[head : head + 1, low:])).astype(bf16)
            key_sum += dot(grad_scores, query_n[head, low:, :], ((1,), (0,)))
            grad_query_ref[span, low:] += dot(key_t_ref[...], grad_scores, ((1,), (0,)))
        grad_key_ref[...] = key_sum.T
        grad_value_ref[...] = value_sum.T

    for at in range(count):
        pl.when(pl.program_id(0) == at)(functools.partial(keys, at))


def attention_backward(query_t, key_n, key_t, value_n, grad_t, out_t, lse, start):
    width, length = query_t.shape
    heads = width // HD
    block = attention_block(length)
    count = length // block

    def whole(j):
        return 0, 0

    return pl.pallas_call(
        functools.partial(backward_kernel, block, heads, count),
        grid=(count,),
        in_specs=[
            pl.BlockSpec((block, HD), lambda j: (j, 0)),
            pl.BlockSpec((HD, block), lambda j: (0, j)),
            pl.BlockSpec((block, HD), lambda j: (j, 0)),
            pl.BlockSpec((width, length), whole),
            pl.BlockSpec((width, length), whole),
            pl.BlockSpec((width, length), whole),
            pl.BlockSpec((heads, length), whole),
            pl.BlockSpec((1, length), whole),
        ],
        out_specs=[
            pl.BlockSpec((width, length), whole),
            pl.BlockSpec((HD, block), lambda j: (0, j)),
            pl.BlockSpec((HD, block), lambda j: (0, j)),
        ],
        out_shape=[
            jax.ShapeDtypeStruct((width, length), f32),
            jax.ShapeDtypeStruct((HD, length), f32),
            jax.ShapeDtypeStruct((HD, length), f32),
        ],
        scratch_shapes=[
            pltpu.VMEM((heads, length, HD), bf16),
            pltpu.VMEM((heads, length, HD), bf16),
            pltpu.VMEM((heads, length), f32),
        ],
        cost_estimate=pl.CostEstimate(flops=25_000_000_000, transcendentals=0, bytes_accessed=0),
        compiler_params=pltpu.CompilerParams(vmem_limit_bytes=56 * 1024 * 1024),
        name="attention_backward",
    )(key_n, key_t, value_n, query_t, grad_t, out_t, lse, start)


def rotate(source, cosine, sine_part):
    halves = source.reshape(-1, 2, HALF, source.shape[1])
    first, second = halves[:, 0], halves[:, 1]
    turned = jnp.stack(
        [first * cosine - second * sine_part, second * cosine + first * sine_part], axis=1
    )
    return turned.reshape(source.shape)


def body(
    tokens,
    segments,
    cotangent,
    attention_gain,
    query_weight,
    key_weight,
    value_weight,
    projection,
    feedforward_gain,
    gate_weight,
    up_weight,
    down_weight,
):
    seqs, ranks = lax.axis_size("seq"), lax.axis_size("ctx")
    rows = query_weight.shape[0]
    depth = tokens.shape[1]
    units = down_weight.shape[0]
    hidden_units = units * seqs
    local_count = tokens.shape[0]
    length = local_count * ranks
    width = H * HD // ranks

    def row_factor(values):
        return lax.rsqrt(jnp.mean(values * values, axis=-1, keepdims=True) + EPSILON)

    inputs = tokens.astype(f32)
    factor_one = row_factor(inputs)
    own_gains = jnp.concatenate([attention_gain, feedforward_gain]).astype(f32)[None]
    spread, last = double_to(own_gains, seqs)
    tokens_first = gather_first(tokens)

    def split_heads(weight):
        return jnp.repeat(weight.reshape(rows, KV, HD), ranks // KV, axis=1)

    mix = jnp.concatenate(
        [
            query_weight.reshape(rows, ranks, width),
            split_heads(key_weight),
            split_heads(value_weight),
        ],
        axis=2,
    ).transpose(1, 0, 2)
    gain_one_row, gain_two_row, seg_row, small = gather_small(spread, segments)
    mix = exchange_ctx(after(mix, last)).reshape(ranks * rows, -1)
    mix_wide = gather_seq(mix)
    tokens_second = gather_second(lax.optimization_barrier((tokens_first, mix))[0])
    pair = split_units(after(gate_weight, mix, *small), up_weight, units)
    pair = exchange_ctx(pair).reshape(ranks * rows, -1)
    proj = lax.ppermute(after(projection, mix), BOTH, head_order())
    proj_wide = gather_seq(proj)

    start = jnp.sum((seg_row < seg_row.T).astype(jnp.int32), axis=1)
    positions = jnp.arange(length, dtype=jnp.int32) - start
    freqs = jnp.power(10000.0, -jnp.arange(HALF, dtype=f32) * (2.0 / HD))
    angles = freqs[:, None] * positions.astype(f32)[None, :]
    cosine, sine_part = jnp.cos(angles), jnp.sin(angles)
    start_row = start[None, :]

    def normalize(piece, gain):
        piece = piece.astype(f32)
        return (piece * row_factor(piece) * gain).astype(bf16)

    normed_all = gather_place(tokens_second, True, normalize, (gain_one_row,))
    pair = after(pair, normed_all)
    pair_wide = gather_seq(pair)
    mixed = dot(mix_wide, normed_all, ((0,), (1,)))
    query_t = rotate(mixed[:width], cosine, sine_part).astype(bf16) * bf16(HD**-0.5)
    key_t = rotate(mixed[width : width + HD], cosine, sine_part).astype(bf16)
    value_t = mixed[width + HD :].astype(bf16)
    query_t = after(query_t, pair)
    key_n, value_n = key_t.T, value_t.T
    cotangent_pieces = send_chips(after(cotangent, normed_all))
    out_t, out_low, lse = attention_forward(query_t, key_n, value_t, start_row)
    out_low, cotangent_pieces = lax.optimization_barrier((out_low, cotangent_pieces))
    down_wide = gather_seq(after(down_weight, out_low))
    rows_by = ((1,), (0,))
    hidden = inputs + scatter_pairs(pair_up(out_low, proj_wide, rows_by))

    factor_two = row_factor(hidden)
    normed_two = (hidden * factor_two * gain_two_row).astype(bf16)
    cotangent_pieces, normed_two = lax.optimization_barrier((cotangent_pieces, normed_two))
    normed_two_first = gather_first(normed_two)
    cotangent_all = place_chips(cotangent_pieces, natural=False)
    columns_by = ((1,), (1,))
    normed_two_all = gather_place(gather_second(normed_two_first), natural=False)
    activated, slope, swished = by_rows(
        functools.partial(units_kernel, hidden_units),
        [normed_two_all],
        pair_wide,
        [hidden_units] * 3,
        "hidden_layer",
    )

    grad_down = dot(activated, cotangent_all, ((0,), (0,)), bf16)
    back = functools.partial(units_back_kernel, hidden_units)
    given = [after(cotangent_all, grad_down), slope, swished]
    wide = [2 * hidden_units, depth]
    both = (4, pair_wide)
    back_away, away = by_rows(back, given, down_wide, wide, "hidden_back_away", (1, 2), both)
    given[0] = after(given[0], away)
    given.append(swap(away, 1, ranks))
    back_stay, two_pairs = by_rows(back, given, down_wide, wide, "hidden_back_stay", (0, 2), both)
    two_pairs = blocks_of(two_pairs)
    grad_pair_in = jnp.concatenate([back_stay, back_away])
    grad_down = scatter_seq(grad_down).astype(f32)
    shaped_two = scatter_pairs(two_pairs) * gain_two_row
    grad_pair = dot(normed_two_all, grad_pair_in, ((0,), (0,)), bf16)
    shaped_two = after(shaped_two, grad_pair)
    grad_pair = scatter_seq(grad_pair)
    mean_two = jnp.mean(shaped_two * hidden, axis=-1, keepdims=True)
    grad_hidden = (
        cotangent.astype(f32)
        + factor_two * shaped_two
        - hidden * (factor_two * factor_two * factor_two * mean_two)
    )

    branch_first = gather_first(grad_hidden.astype(bf16))
    branch_second = gather_second(branch_first)
    activated = after(activated, shaped_two)
    away = product([activated], down_wide, rows_by, (1, 2), "out_away")
    given = [after(activated, away), swap(away, 1, ranks)]
    out_pairs = blocks_of(product(given, down_wide, rows_by, (0, 2), "out_stay"))
    branch_second, out_pairs = lax.optimization_barrier((branch_second, out_pairs))
    out_first = scatter_first(out_pairs)
    branch_all = gather_place(branch_second)
    grad_proj = dot(out_low, branch_all, ((0,), (0,)), bf16)
    grad_out_t = dot(proj_wide, branch_all, columns_by, bf16)
    grad_out_t, out_first, grad_down, grad_proj = lax.optimization_barrier(
        (grad_out_t, out_first, grad_down, grad_proj)
    )
    grad_out_t = after(grad_out_t, grad_pair)
    grad_proj = scatter_seq(grad_proj)
    out_sum = scatter_rest(out_first)
    grad_query_t, grad_key_t, grad_value_t = attention_backward(
        query_t, key_n, key_t, value_n, grad_out_t, out_t, lse, start_row
    )
    grad_mixed = jnp.concatenate(
        [
            rotate(grad_query_t * HD**-0.5, cosine, -sine_part),
            rotate(grad_key_t, cosine, -sine_part),
            grad_value_t,
        ],
        axis=0,
    ).astype(bf16)
    grad_pair = exchange_ctx(grad_pair.reshape(ranks, rows, -1))
    grad_mixed = after(grad_mixed, out_sum, grad_proj, grad_pair)
    block_out = (hidden + out_sum).astype(bf16)
    grad_mix = dot(normed_all, grad_mixed, ((0,), (1,)), bf16)
    mixed_n = after(grad_mixed.T, grad_mix)
    grad_mix = scatter_seq(grad_mix)
    shaped_one = pair_up(mixed_n, mix_wide, columns_by)
    grad_gate, grad_up, grad_feedforward = join_units(grad_pair, gate_weight, up_weight, units)
    shaped_first = scatter_first(shaped_one)
    arrived = [part for _, part in shaped_first]
    shaped_first, grad_gate, block_out = lax.optimization_barrier(
        (shaped_first, grad_gate, block_out)
    )
    shaped_one = scatter_rest(shaped_first)
    shaped_one = shaped_one * gain_one_row
    mean_one = jnp.mean(shaped_one * inputs, axis=-1, keepdims=True)
    grad_tokens = (
        grad_hidden
        + factor_one * shaped_one
        - inputs * (factor_one * factor_one * factor_one * mean_one)
    )

    def join_heads(part):
        part = part.reshape(KV, ranks // KV, rows, HD).astype(f32).sum(axis=1)
        return part.transpose(1, 0, 2).reshape(rows, -1)

    def row_sum(grad, weight):
        return jnp.sum(grad * weight.astype(f32), axis=1)

    grad_feedforward = grad_feedforward[:, 0] / feedforward_gain.astype(f32)

    grad_mix = exchange_ctx(after(grad_mix, *arrived).reshape(ranks, rows, -1))
    grad_query = grad_mix[:, :, :width].transpose(1, 0, 2).reshape(rows, -1).astype(f32)
    grad_key = join_heads(grad_mix[:, :, width : width + HD])
    grad_value = join_heads(grad_mix[:, :, width + HD :])
    grad_attention = (
        row_sum(grad_query, query_weight)
        + row_sum(grad_key, key_weight)
        + row_sum(grad_value, value_weight)
    ) / attention_gain.astype(f32)
    back_order = [(b, a) for a, b in head_order()]
    grad_projection = lax.ppermute(grad_proj, BOTH, back_order).astype(f32)
    return (
        block_out,
        grad_tokens,
        grad_attention,
        grad_query,
        grad_key,
        grad_value,
        grad_projection,
        grad_feedforward,
        grad_gate,
        grad_up,
        grad_down,
    )


def solution(mesh):
    rows, plain = P(BOTH, None), P(BOTH)
    return jax.shard_map(
        body,
        mesh=mesh,
        in_specs=(rows, P("seq", "ctx"), rows, plain, rows, rows, rows, rows, plain, rows, rows, rows),
        out_specs=(rows, rows, plain, rows, rows, rows, rows, plain, rows, rows, rows),
        check_vma=False,
    )
```

time: 631 us -> 578 us (0.916)
  matrix products: 115 us -> 59.1 us
  Pallas kernels: 59.2 us -> 111 us
  local copies, waits for them, and re-layouts: 85.2 us -> 36.1 us
  waiting for transfers between devices: 227 us -> 208 us
  blocking collectives: 0 us -> 12 us
  starting transfers between devices: 75.8 us -> 87.6 us
    pallas_call x3 -> x11, Pallas kernels: 30 us -> 90 us  [the longest x5 61.8 us: by_rows(): pl.pallas_call(kernel, grid=(count // block,), in_specs=specs, out_specs=...]
    dot_general x16 -> x10, matrix products: 115 us -> 59.1 us  [dot(): lax.dot_general(left, right, (contract, ((), ())), preferred_element_type...]
    ppermute x52 -> x58, waiting for transfers between devices: 191 us -> 147 us  [swap(): return lax.ppermute(value, 'ctx', [(i, i ^ step) for i in range(count)])]
    reduce_scatter x4, waiting for transfers between devices: 0.01 us -> 33 us  [scatter_seq(): return lax.psum_scatter(value, 'seq', scatter_dimension=0, tiled=True)]
    dynamic_update_slice x24 -> x16, local copies, waits for them, and re-layouts: 32.5 us -> 2.4 us  [the longest x8 1.71 us: place_chips(): whole = lax.dynamic_update_index_in_dim(whole, piece, spot, 0)]
    ppermute x52 -> x58, starting transfers between devices: 42.4 us -> 61.5 us  [swap(): return lax.ppermute(value, 'ctx', [(i, i ^ step) for i in range(count)])]
    all_to_all x4 -> x3, waiting for transfers between devices: 27.6 us -> 9.69 us  [exchange_ctx(): return lax.all_to_all(value, 'ctx', 0, 0)]
    all_gather x4, waiting for transfers between devices: 0.01 us -> 16 us  [gather_seq(): return lax.all_gather(value, 'seq', axis=0, tiled=True)]
  transfers between devices with their start and end apart: 67 -> 73, of which waited for: 31 -> 36; matrix products, arithmetic and copies ran while one was open for 29% -> 19% of each run, Pallas kernels for 9% -> 19%
where the time goes in v2:
time: 578 us; the launch traced here: 571 us
  waiting for transfers between devices  208 us (36%)
  Pallas kernels  111 us (19%)
  starting transfers between devices  87.6 us (15%)
  matrix products  59.1 us (10%)
  other arithmetic  41.7 us (7%)
  local copies, waits for them, and re-layouts  36.1 us (6%)
  between operations  16 us (3%)
  blocking collectives  12 us (2%)
    ppermute x58, waiting for transfers between devices, swap(): return lax.ppermute(value, 'ctx', [(i, i ^ step) for i in range(count)])  147 us
    pallas_call x5, Pallas kernels, by_rows(): pl.pallas_call(kernel, grid=(count // block,), in_specs=specs, out_specs=...  61.8 us
    ppermute x58, starting transfers between devices, swap(): return lax.ppermute(value, 'ctx', [(i, i ^ step) for i in range(count)])  61.5 us
    dot_general x10, matrix products, dot(): lax.dot_general(left, right, (contract, ((), ())), preferred_element_type...  59.1 us
    reduce_scatter x4, waiting for transfers between devices, scatter_seq(): return lax.psum_scatter(value, 'seq', scatter_dimension=0, tiled=True)  33 us
    pallas_call x1, Pallas kernels, attention_backward(): pl.pallas_call(functools.partial(backward_kernel, block, heads, count), g...  20.8 us
    all_gather x4, waiting for transfers between devices, gather_seq(): return lax.all_gather(value, 'seq', axis=0, tiled=True)  16 us
    all_to_all x3, starting transfers between devices, exchange_ctx(): return lax.all_to_all(value, 'ctx', 0, 0)  15.2 us
  transfers between devices with their start and end apart: 73, of which 36 were waited for; matrix products, arithmetic and copies ran while one was open for 19% of the time, Pallas kernels for 19%

profile of v2, /device:TPU:0, one launch (start us, length us, event | category | flops | bytes accessed | tf_op | source)
XLA Modules:
  0.0 570.8 jit_solution(8568045589283640782)
XLA Ops:
  18.3 12.0 %all_to_all.20 = bf16[8,64,384]{2,1,0:T(8,128)(2,1)} all-to-all(bf16[8,64,384]{2,1,0:T(8,128)(2,1)S(1)} %copy.108), channel_id=1, replica_groups=mesh['seq'=4,'ctx'=8] {'ctx'}, dimensions={0} | all-to-all | bytes 786432 | tf_op jit(solution)/shard_map/all_to_all | solution.py:238
  35.3 5.9 %collective-permute-done.3 = bf16[96,2048]{1,0:T(8,128)(2,1)S(1)} collective-permute-done((bf16[96,2048]{1,0:T(8,128)(2,1)S(1)}, bf16[96,2048]{1,0:T(8,128)(2,1)S(1)}, u32[]{:S(2)}, u32[]{:S(2)}) %collective-permute-start.3) | collective-permute-done | bytes 393248 | tf_op jit(solution)/shard_map/ppermute | solution.py:32
  53.3 12.3 %collective-permute-start.13 = (f32[1,704]{1,0:T(1,128)S(1)}, f32[1,704]{1,0:T(1,128)S(1)}, u32[]{:S(2)}, u32[]{:S(2)}) collective-permute-start(f32[1,704]{1,0:T(1,128)S(1)} %pad_maximum_fusion.5), channel_id=1, source_target_pairs={{0,4},{1,5},{2,6},{3,7},{4,0},{5,1},{6,2},{7,3},{8,12},{9,13},{10,... | collective-permute-start | bytes 8456 | tf_op jit(solution)/shard_map/ppermute | solution.py:32
  86.9 9.7 %all-to-all-done.1 = bf16[8,64,1408]{2,1,0:T(8,128)(2,1)} async-done(((bf16[8,64,1408]{2,1,0:T(8,128)(2,1)}), bf16[8,64,1408]{2,1,0:T(8,128)(2,1)}, u32[]{:S(2)}, u32[]{:S(2)}) %all-to-all-start.1) | async-done | bytes 1441824 | tf_op jit(solution)/shard_map/all_to_all | solution.py:238
  113.4 13.6 %attention_forward.1 = (f32[256,1536]{1,0:T(8,128)}, bf16[1536,256]{1,0:T(8,128)(2,1)}, f32[4,1536]{1,0:T(4,128)}) custom-call(bf16[1536,64]{1,0:T(8,128)(2,1)} %copy.121.key_ref, bf16[64,1536]{1,0:T(8,128)(2,1)} %copy.112.value_ref, bf16[256,1536]{1,0:T(8,128)(2,1)} %bitcast.275, s32[1,1536]{1,0:T(1,128)} %reduce_sum.93.start_ref), custom_call_target="tpu_custom_call" | custom-call | tf_op jit(solution)/shard_map/attention_forward/pallas_call | solution.py:413
  127.0 8.2 %collective-permute-done.19 = bf16[192,2048]{1,0:T(8,128)(2,1)S(1)} collective-permute-done((bf16[192,2048]{1,0:T(8,128)(2,1)S(1)}, bf16[192,2048]{1,0:T(8,128)(2,1)S(1)}, u32[]{:S(2)}, u32[]{:S(2)}) %collective-permute-start.19) | collective-permute-done | bytes 786464 | tf_op jit(solution)/shard_map/ppermute | solution.py:32
  139.8 5.8 %collective-permute-done.21 = bf16[768,2048]{1,0:T(8,128)(2,1)} collective-permute-done((bf16[768,2048]{1,0:T(8,128)(2,1)S(1)}, bf16[768,2048]{1,0:T(8,128)(2,1)}, u32[]{:S(2)}, u32[]{:S(2)}) %collective-permute-start.21) | collective-permute-done | bytes 3145760 | tf_op jit(solution)/shard_map/ppermute | solution.py:32
  155.2 14.9 %collective-permute-done.24 = bf16[1,2,96,2048]{3,2,1,0:T(8,128)(2,1)} collective-permute-done((bf16[1,2,96,2048]{3,2,1,0:T(8,128)(2,1)}, bf16[1,2,96,2048]{3,2,1,0:T(8,128)(2,1)}, u32[]{:S(2)}, u32[]{:S(2)}) %collective-permute-start.24) | collective-permute-done | bytes 786464 | tf_op jit(solution)/shard_map/ppermute | solution.py:32
  176.3 5.8 %collective-permute-done.25 = bf16[1,1,96,2048]{3,2,1,0:T(8,128)(2,1)S(1)} collective-permute-done((bf16[1,1,96,2048]{3,2,1,0:T(8,128)(2,1)S(1)}, bf16[1,1,96,2048]{3,2,1,0:T(8,128)(2,1)S(1)}, u32[]{:S(2)}, u32[]{:S(2)}) %collective-permute-start.25) | collective-permute-done | bytes 393248 | tf_op jit(solution)/shard_map/ppermute | solution.py:32
  189.7 10.7 %collective-permute-done.30 = bf16[96,2048]{1,0:T(8,128)(2,1)S(1)} collective-permute-done((bf16[96,2048]{1,0:T(8,128)(2,1)S(1)}, bf16[96,2048]{1,0:T(8,128)(2,1)S(1)}, u32[]{:S(2)}, u32[]{:S(2)}) %collective-permute-start.30) | collective-permute-done | bytes 393248 | tf_op jit(solution)/shard_map/ppermute | solution.py:32
  204.2 16.4 %collective-permute-done.32 = bf16[1,2,96,2048]{3,2,1,0:T(8,128)(2,1)S(1)} collective-permute-done((bf16[1,2,96,2048]{3,2,1,0:T(8,128)(2,1)S(1)}, bf16[1,2,96,2048]{3,2,1,0:T(8,128)(2,1)S(1)}, u32[]{:S(2)}, u32[]{:S(2)}) %collective-permute-start.32) | collective-permute-done | bytes 786464 | tf_op jit(solution)/shard_map/ppermute | solution.py:32
  230.1 16.4 %hidden_layer.1 = (bf16[1536,704]{1,0:T(8,128)(2,1)}, bf16[1536,704]{1,0:T(8,128)(2,1)}, bf16[1536,704]{1,0:T(8,128)(2,1)}) custom-call(bf16[1536,2048]{1,0:T(8,128)(2,1)} %bitcast.256, bf16[2048,1408]{1,0:T(8,128)(2,1)} %all-gather.9.cloned.1.call-done.weight_ref), custom_call_target="tpu_custom_call" | custom-call | tf_op jit(solution)/shard_map/hidden_layer/pallas_call | solution.py:363
  246.5 7.7 %convolution_convert_fusion.3 = bf16[704,2048]{1,0:T(8,128)(2,1)} fusion(bf16[1536,704]{1,0:T(8,128)(2,1)} %get-tuple-element.111.row_ref, bf16[1536,2048]{1,0:T(8,128)(2,1)S(1)} %bitcast.253), kind=kOutput, calls=%fused_computation.9 | convolution fusion | flops 4430626816 | bytes 11337728 | tf_op jit(solution)/shard_map/dot_general | solution.py:24
  254.3 16.0 %all-gather.11.cloned.1.call-done.down_ref.weight_ref = bf16[704,2048]{1,0:T(8,128)(2,1)} async-done(((bf16[176,2048]{1,0:T(8,128)(2,1)}), bf16[704,2048]{1,0:T(8,128)(2,1)}) %all-gather.11.cloned.1.call-update) | async-done | bytes 2883600 | tf_op jit(solution)/shard_map/all_gather | solution.py:230
  270.3 15.6 %hidden_back_away.1 = (bf16[768,1408]{1,0:T(8,128)(2,1)}, bf16[768,2048]{1,0:T(8,128)(2,1)}) custom-call(bf16[1536,2048]{1,0:T(8,128)(2,1)} %bitcast.251, bf16[704,2048]{1,0:T(8,128)(2,1)} %all-gather.11.cloned.1.call-done.down_ref.weight_ref, bf16[1536,704]{1,0:T(8,128)(2,1)} %get-tuple-element.102.slope_ref, ...), custom_call_target="tpu_custom_call" | custom-call | tf_op jit(solution)/shard_map/hidden_back_away/pallas_call | solution.py:363
  286.0 6.0 %collective-permute-done.38.refs_0_ = bf16[768,2048]{1,0:T(8,128)(2,1)} collective-permute-done((bf16[768,2048]{1,0:T(8,128)(2,1)}, bf16[768,2048]{1,0:T(8,128)(2,1)}, u32[]{:S(2)}, u32[]{:S(2)}) %collective-permute-start.38) | collective-permute-done | bytes 3145760 | tf_op jit(solution)/shard_map/ppermute | solution.py:32
  292.0 15.8 %hidden_back_stay.1 = (bf16[768,1408]{1,0:T(8,128)(2,1)}, bf16[768,2048]{1,0:T(8,128)(2,1)}) custom-call(bf16[1536,2048]{1,0:T(8,128)(2,1)} %bitcast.252, bf16[704,2048]{1,0:T(8,128)(2,1)} %all-gather.11.cloned.1.call-done.down_ref.weight_ref, bf16[1536,704]{1,0:T(8,128)(2,1)} %get-tuple-element.102.slope_ref, ...), custom_call_target="tpu_custom_call" | custom-call | tf_op jit(solution)/shard_map/hidden_back_stay/pallas_call | solution.py:363
  307.8 14.2 %convolution_convert_fusion = bf16[2048,1408]{1,0:T(8,128)(2,1)} fusion(bf16[1536,2048]{1,0:T(8,128)(2,1)S(1)} %bitcast.259, bf16[768,1408]{1,0:T(8,128)(2,1)} %get-tuple-element.108, bf16[768,1408]{1,0:T(8,128)(2,1)} %get-tuple-element.107), kind=kOutput, calls=%fused_computation.1 | convolution fusion | flops 8869904384 | bytes 16384000 | tf_op jit(solution)/shard_map/dot_general | solution.py:24
  327.6 16.5 %collective-permute-done.41 = bf16[1,2,96,2048]{3,2,1,0:T(8,128)(2,1)S(1)} collective-permute-done((bf16[1,2,96,2048]{3,2,1,0:T(8,128)(2,1)S(1)}, bf16[1,2,96,2048]{3,2,1,0:T(8,128)(2,1)S(1)}, u32[]{:S(2)}, u32[]{:S(2)}) %collective-permute-start.41) | collective-permute-done | bytes 786464 | tf_op jit(solution)/shard_map/ppermute | solution.py:32
  347.8 7.1 %collective-permute-done.42 = bf16[1,1,96,2048]{3,2,1,0:T(8,128)(2,1)S(1)} collective-permute-done((bf16[1,1,96,2048]{3,2,1,0:T(8,128)(2,1)S(1)}, bf16[1,1,96,2048]{3,2,1,0:T(8,128)(2,1)S(1)}, u32[]{:S(2)}, u32[]{:S(2)}) %collective-permute-start.42) | collective-permute-done | bytes 393248 | tf_op jit(solution)/shard_map/ppermute | solution.py:32
  356.7 6.8 %out_away.1 = bf16[768,2048]{1,0:T(8,128)(2,1)} custom-call(bf16[1536,704]{1,0:T(8,128)(2,1)} %get-tuple-element.111.row_ref, bf16[704,2048]{1,0:T(8,128)(2,1)} %all-gather.11.cloned.1.call-done.down_ref.weight_ref), custom_call_target="tpu_custom_call" | custom-call | tf_op jit(solution)/shard_map/out_away/pallas_call | solution.py:363
  367.5 9.4 %collective-permute-done.43 = bf16[96,2048]{1,0:T(8,128)(2,1)S(1)} collective-permute-done((bf16[96,2048]{1,0:T(8,128)(2,1)S(1)}, bf16[96,2048]{1,0:T(8,128)(2,1)S(1)}, u32[]{:S(2)}, u32[]{:S(2)}) %collective-permute-start.43) | collective-permute-done | bytes 393248 | tf_op jit(solution)/shard_map/ppermute | solution.py:32
  381.7 7.2 %out_stay.1 = bf16[768,2048]{1,0:T(8,128)(2,1)} custom-call(bf16[1536,704]{1,0:T(8,128)(2,1)} %get-tuple-element.111.row_ref, bf16[704,2048]{1,0:T(8,128)(2,1)} %all-gather.11.cloned.1.call-done.down_ref.weight_ref, bf16[768,2048]{1,0:T(8,128)(2,1)} %collective-permute-done.47.refs_0_), custom_call_target="tpu_custom_call" | custom-call | tf_op jit(solution)/shard_map/out_stay/pallas_call | solution.py:363
  388.9 7.3 %collective-permute-done.44 = bf16[1,2,96,2048]{3,2,1,0:T(8,128)(2,1)S(1)} collective-permute-done((bf16[1,2,96,2048]{3,2,1,0:T(8,128)(2,1)S(1)}, bf16[1,2,96,2048]{3,2,1,0:T(8,128)(2,1)S(1)}, u32[]{:S(2)}, u32[]{:S(2)}) %collective-permute-start.44) | collective-permute-done | bytes 786464 | tf_op jit(solution)/shard_map/ppermute | solution.py:32
  409.9 5.7 convolution_convert_fusion.5
  415.6 5.6 convolution_convert_fusion.6.grad_ref
  424.4 7.3 %reduce-scatter.7.cloned.1.call-done = bf16[512,1408]{1,0:T(8,128)(2,1)} async-done(((bf16[2048,1408]{1,0:T(8,128)(2,1)}), bf16[512,1408]{1,0:T(8,128)(2,1)}) %reduce-scatter.7.cloned.1.call-update) | async-done | bytes 1441808 | tf_op jit(solution)/shard_map/reduce_scatter | solution.py:234
  435.4 20.8 %attention_backward.1 = (f32[256,1536]{1,0:T(8,128)}, f32[64,1536]{1,0:T(8,128)}, f32[64,1536]{1,0:T(8,128)}) custom-call(bf16[1536,64]{1,0:T(8,128)(2,1)} %copy.121.key_ref, bf16[64,1536]{1,0:T(8,128)(2,1)} %bitcast.300, bf16[1536,64]{1,0:T(8,128)(2,1)} %bitcast.281, bf16[256,1536]{1,0:T(8,128)(2,1)} %bitcast.276, ...), custom_call_target="tpu_custom_call" | custom-call | flops 24999999488 | tf_op jit(solution)/shard_map/attention_backward/pallas_call | solution.py:501
  462.2 7.4 %convolution_convert_fusion.4 = bf16[2048,384]{1,0:T(8,128)(2,1)} fusion(bf16[1536,2048]{1,0:T(8,128)(2,1)} %bitcast.266, bf16[384,1536]{1,0:T(8,128)(2,1)S(1)} %pad_maximum_fusion.1), kind=kOutput, calls=%fused_computation.10 | convolution fusion | flops 2416705536 | bytes 9043968 | tf_op jit(solution)/shard_map/dot_general | solution.py:24
  486.6 5.5 collective-permute-done.54
  510.0 22.7 %reduce-scatter.11.cloned.1.call-done = bf16[512,384]{1,0:T(8,128)(2,1)} async-done(((bf16[2048,384]{1,0:T(8,128)(2,1)}), bf16[512,384]{1,0:T(8,128)(2,1)}) %reduce-scatter.11.cloned.1.call-update) | async-done | bytes 393232 | tf_op jit(solution)/shard_map/reduce_scatter | solution.py:234
  532.7 7.1 %all-to-all-start.3 = ((bf16[8,64,384]{2,1,0:T(8,128)(2,1)}), bf16[8,64,384]{2,1,0:T(8,128)(2,1)S(1)}, u32[]{:S(2)}, u32[]{:S(2)}) async-start(bf16[8,64,384]{2,1,0:T(8,128)(2,1)} %bitcast.307), calls=%async_computation.7 | async-start | bytes 786432 | tf_op jit(solution)/shard_map/all_to_all | solution.py:238
  (446 shorter events, 211.4 us)
Async XLA Ops:
  7.2 96.7 %all-gather.5.cloned.1.call-start = ((), (), s32[]{:S(2)}) async-start(), calls=%async_computation.8 | async-start | bytes 1966080 | tf_op jit(solution)/shard_map/all_gather | solution.py:230
  30.3 107.1 %all-gather.7.cloned.1.call-start = ((), (), s32[]{:S(2)}) async-start(), calls=%async_computation.9 | async-start | bytes 1310720 | tf_op jit(solution)/shard_map/all_gather | solution.py:230
  31.7 20.4 %collective-permute-start.17 = (bf16[64,2048]{1,0:T(8,128)(2,1)}, bf16[64,2048]{1,0:T(8,128)(2,1)}, u32[]{:S(2)}, u32[]{:S(2)}) collective-permute-start(bf16[64,2048]{1,0:T(8,128)(2,1)} %param.19), channel_id=1, source_target_pairs={{0,0},{1,8},{2,16},{3,24},{4,1},{5,9},{6,17},{7,25},{8,2},{9,10},{... | collective-permute-start | bytes 786440 | tf_op jit(solution)/shard_map/ppermute | solution.py:593
  44.2 33.3 %collective-permute-start.5 = (bf16[1,2,96,2048]{3,2,1,0:T(8,128)(2,1)}, bf16[1,2,96,2048]{3,2,1,0:T(8,128)(2,1)S(1)}, u32[]{:S(2)}, u32[]{:S(2)}) collective-permute-start(bf16[1,2,96,2048]{3,2,1,0:T(8,128)(2,1)} %maximum_select_fusion.1), channel_id=1, source_target_pairs={{0,4},{1,5},{2,6},{3,7},{4,0},{5,1},{6,2},{7,3},{8,12},{9,13},{10,... | collective-permute-start | bytes 2359304 | tf_op jit(solution)/shard_map/ppermute | solution.py:32
  49.6 28.2 %collective-permute-start.8 = (bf16[2,1,96,2048]{3,2,1,0:T(8,128)(2,1)}, bf16[2,1,96,2048]{3,2,1,0:T(8,128)(2,1)S(1)}, u32[]{:S(2)}, u32[]{:S(2)}) collective-permute-start(bf16[2,1,96,2048]{3,2,1,0:T(8,128)(2,1)} %maximum_select_fusion.3), channel_id=1, source_target_pairs={{0,2},{1,3},{2,0},{3,1},{4,6},{5,7},{6,4},{7,5},{8,10},{9,11},{10,... | collective-permute-start | bytes 2359304 | tf_op jit(solution)/shard_map/ppermute | solution.py:32
  72.4 24.2 %all-to-all-start.1 = ((bf16[8,64,1408]{2,1,0:T(8,128)(2,1)}), bf16[8,64,1408]{2,1,0:T(8,128)(2,1)}, u32[]{:S(2)}, u32[]{:S(2)}) async-start(bf16[8,64,1408]{2,1,0:T(8,128)(2,1)} %split_units.1), calls=%async_computation.1 | async-start | bytes 2883584 | tf_op jit(solution)/shard_map/all_to_all | solution.py:238
  76.9 153.2 %all-gather.9.cloned.1.call-start = ((), (), s32[]{:S(2)}) async-start(), calls=%async_computation.10 | async-start | bytes 7208960 | tf_op jit(solution)/shard_map/all_gather | solution.py:230
  96.6 173.7 %all-gather.11.cloned.1.call-start = ((), (), s32[]{:S(2)}) async-start(), calls=%async_computation.11 | async-start | bytes 3604480 | tf_op jit(solution)/shard_map/all_gather | solution.py:230
  100.4 26.6 %collective-permute-start.20 = (bf16[192,2048]{1,0:T(8,128)(2,1)S(1)}, bf16[192,2048]{1,0:T(8,128)(2,1)S(1)}, u32[]{:S(2)}, u32[]{:S(2)}) collective-permute-start(bf16[192,2048]{1,0:T(8,128)(2,1)S(1)} %copy-done.17), channel_id=1, source_target_pairs={{0,6},{1,7},{2,4},{3,5},{4,2},{5,3},{6,0},{7,1},{8,14},{9,15},{10,... | collective-permute-start | bytes 2359304 | tf_op jit(solution)/shard_map/ppermute | solution.py:32
  100.8 34.3 %collective-permute-start.19 = (bf16[192,2048]{1,0:T(8,128)(2,1)S(1)}, bf16[192,2048]{1,0:T(8,128)(2,1)S(1)}, u32[]{:S(2)}, u32[]{:S(2)}) collective-permute-start(bf16[192,2048]{1,0:T(8,128)(2,1)S(1)} %copy-done.17), channel_id=1, source_target_pairs={{0,4},{1,5},{2,6},{3,7},{4,0},{5,1},{6,2},{7,3},{8,12},{9,13},{10,... | collective-permute-start | bytes 2359304 | tf_op jit(solution)/shard_map/ppermute | solution.py:32
  102.2 33.3 %collective-permute-start.18 = (bf16[192,2048]{1,0:T(8,128)(2,1)S(1)}, bf16[192,2048]{1,0:T(8,128)(2,1)}, u32[]{:S(2)}, u32[]{:S(2)}) collective-permute-start(bf16[192,2048]{1,0:T(8,128)(2,1)S(1)} %copy-done.17), channel_id=1, source_target_pairs={{0,2},{1,3},{2,0},{3,1},{4,6},{5,7},{6,4},{7,5},{8,10},{9,11},{10,... | collective-permute-start | bytes 2359304 | tf_op jit(solution)/shard_map/ppermute | solution.py:32
  150.2 19.9 %collective-permute-start.24 = (bf16[1,2,96,2048]{3,2,1,0:T(8,128)(2,1)}, bf16[1,2,96,2048]{3,2,1,0:T(8,128)(2,1)}, u32[]{:S(2)}, u32[]{:S(2)}) collective-permute-start(bf16[1,2,96,2048]{3,2,1,0:T(8,128)(2,1)} %dynamic-slice_bitcast_fusion.6), channel_id=1, source_target_pairs={{0,4},{1,5},{2,6},{3,7},{4,0},{5,1},{6,2},{7,3},{8,12},{9,13},{10,... | collective-permute-start | bytes 2359304 | tf_op jit(solution)/shard_map/ppermute | solution.py:32
  152.7 20.8 %collective-permute-start.22 = (bf16[2,1,96,2048]{3,2,1,0:T(8,128)(2,1)}, bf16[2,1,96,2048]{3,2,1,0:T(8,128)(2,1)}, u32[]{:S(2)}, u32[]{:S(2)}) collective-permute-start(bf16[2,1,96,2048]{3,2,1,0:T(8,128)(2,1)} %dynamic-slice_bitcast_fusion.7), channel_id=1, source_target_pairs={{0,2},{1,3},{2,0},{3,1},{4,6},{5,7},{6,4},{7,5},{8,10},{9,11},{10,... | collective-permute-start | bytes 2359304 | tf_op jit(solution)/shard_map/ppermute | solution.py:32
  155.1 224.2 %reduce-scatter.5.cloned.1.call-start = ((), (), s32[]{:S(2)}) async-start(), calls=%async_computation.12 | async-start | bytes 3604480 | tf_op jit(solution)/shard_map/reduce_scatter | solution.py:234
  200.4 22.9 %collective-permute-start.29 = (bf16[192,2048]{1,0:T(8,128)(2,1)S(1)}, bf16[192,2048]{1,0:T(8,128)(2,1)S(1)}, u32[]{:S(2)}, u32[]{:S(2)}) collective-permute-start(bf16[192,2048]{1,0:T(8,128)(2,1)S(1)} %copy-done.48), channel_id=1, source_target_pairs={{0,1},{1,0},{2,3},{3,2},{4,5},{5,4},{6,7},{7,6},{8,9},{9,8},{10,11... | collective-permute-start | bytes 2359304 | tf_op jit(solution)/shard_map/ppermute | solution.py:32
  200.5 20.0 %collective-permute-start.32 = (bf16[1,2,96,2048]{3,2,1,0:T(8,128)(2,1)S(1)}, bf16[1,2,96,2048]{3,2,1,0:T(8,128)(2,1)S(1)}, u32[]{:S(2)}, u32[]{:S(2)}) collective-permute-start(bf16[1,2,96,2048]{3,2,1,0:T(8,128)(2,1)S(1)} %maximum_select_fusion.5), channel_id=1, source_target_pairs={{0,4},{1,5},{2,6},{3,7},{4,0},{5,1},{6,2},{7,3},{8,12},{9,13},{10,... | collective-permute-start | bytes 2359304 | tf_op jit(solution)/shard_map/ppermute | solution.py:32
  201.8 21.6 %collective-permute-start.31 = (bf16[1,2,96,2048]{3,2,1,0:T(8,128)(2,1)S(1)}, bf16[1,2,96,2048]{3,2,1,0:T(8,128)(2,1)S(1)}, u32[]{:S(2)}, u32[]{:S(2)}) collective-permute-start(bf16[1,2,96,2048]{3,2,1,0:T(8,128)(2,1)S(1)} %maximum_select_fusion.5), channel_id=1, source_target_pairs={{0,1},{1,0},{2,3},{3,2},{4,5},{5,4},{6,7},{7,6},{8,9},{9,8},{10,11... | collective-permute-start | bytes 2359304 | tf_op jit(solution)/shard_map/ppermute | solution.py:32
  203.4 19.8 %collective-permute-start.36 = (bf16[2,1,96,2048]{3,2,1,0:T(8,128)(2,1)S(1)}, bf16[2,1,96,2048]{3,2,1,0:T(8,128)(2,1)S(1)}, u32[]{:S(2)}, u32[]{:S(2)}) collective-permute-start(bf16[2,1,96,2048]{3,2,1,0:T(8,128)(2,1)S(1)} %maximum_select_fusion.7), channel_id=1, source_target_pairs={{0,2},{1,3},{2,0},{3,1},{4,6},{5,7},{6,4},{7,5},{8,10},{9,11},{10,... | collective-permute-start | bytes 2359304 | tf_op jit(solution)/shard_map/ppermute | solution.py:32
  204.0 19.4 %collective-permute-start.35 = (bf16[2,1,96,2048]{3,2,1,0:T(8,128)(2,1)S(1)}, bf16[2,1,96,2048]{3,2,1,0:T(8,128)(2,1)S(1)}, u32[]{:S(2)}, u32[]{:S(2)}) collective-permute-start(bf16[2,1,96,2048]{3,2,1,0:T(8,128)(2,1)S(1)} %maximum_select_fusion.7), channel_id=1, source_target_pairs={{0,1},{1,0},{2,3},{3,2},{4,5},{5,4},{6,7},{7,6},{8,9},{9,8},{10,11... | collective-permute-start | bytes 2359304 | tf_op jit(solution)/shard_map/ppermute | solution.py:32
  254.2 177.4 %reduce-scatter.7.cloned.1.call-start = ((), (), s32[]{:S(2)}) async-start(), calls=%async_computation.13 | async-start | bytes 7208960 | tf_op jit(solution)/shard_map/reduce_scatter | solution.py:234
  322.0 140.2 %reduce-scatter.9.cloned.1.call-start = ((), (), s32[]{:S(2)}) async-start(), calls=%async_computation.14 | async-start | bytes 1310720 | tf_op jit(solution)/shard_map/reduce_scatter | solution.py:234
  324.5 19.6 %collective-permute-start.41 = (bf16[1,2,96,2048]{3,2,1,0:T(8,128)(2,1)S(1)}, bf16[1,2,96,2048]{3,2,1,0:T(8,128)(2,1)S(1)}, u32[]{:S(2)}, u32[]{:S(2)}) collective-permute-start(bf16[1,2,96,2048]{3,2,1,0:T(8,128)(2,1)S(1)} %dynamic-slice_bitcast_fusion.4), channel_id=1, source_target_pairs={{0,4},{1,5},{2,6},{3,7},{4,0},{5,1},{6,2},{7,3},{8,12},{9,13},{10,... | collective-permute-start | bytes 2359304 | tf_op jit(solution)/shard_map/ppermute | solution.py:32
  326.1 19.9 %collective-permute-start.39 = (bf16[2,1,96,2048]{3,2,1,0:T(8,128)(2,1)S(1)}, bf16[2,1,96,2048]{3,2,1,0:T(8,128)(2,1)S(1)}, u32[]{:S(2)}, u32[]{:S(2)}) collective-permute-start(bf16[2,1,96,2048]{3,2,1,0:T(8,128)(2,1)S(1)} %dynamic-slice_bitcast_fusion.5), channel_id=1, source_target_pairs={{0,2},{1,3},{2,0},{3,1},{4,6},{5,7},{6,4},{7,5},{8,10},{9,11},{10,... | collective-permute-start | bytes 2359304 | tf_op jit(solution)/shard_map/ppermute | solution.py:32
  377.0 19.2 %collective-permute-start.44 = (bf16[1,2,96,2048]{3,2,1,0:T(8,128)(2,1)S(1)}, bf16[1,2,96,2048]{3,2,1,0:T(8,128)(2,1)S(1)}, u32[]{:S(2)}, u32[]{:S(2)}) collective-permute-start(bf16[1,2,96,2048]{3,2,1,0:T(8,128)(2,1)S(1)} %maximum_select_fusion.8), channel_id=1, source_target_pairs={{0,4},{1,5},{2,6},{3,7},{4,0},{5,1},{6,2},{7,3},{8,12},{9,13},{10,... | collective-permute-start | bytes 2359304 | tf_op jit(solution)/shard_map/ppermute | solution.py:32
  378.7 18.9 %collective-permute-start.46 = (bf16[2,1,96,2048]{3,2,0,1:T(8,128)(2,1)S(1)}, bf16[2,1,96,2048]{3,2,0,1:T(8,128)(2,1)S(1)}, u32[]{:S(2)}, u32[]{:S(2)}) collective-permute-start(bf16[2,1,96,2048]{3,2,0,1:T(8,128)(2,1)S(1)} %bitcast_select_fusion), channel_id=1, source_target_pairs={{0,2},{1,3},{2,0},{3,1},{4,6},{5,7},{6,4},{7,5},{8,10},{9,11},{10,... | collective-permute-start | bytes 2359304 | tf_op jit(solution)/shard_map/ppermute | solution.py:32
  402.5 19.8 %collective-permute-start.53 = (bf16[1,2,96,2048]{3,2,1,0:T(8,128)(2,1)}, bf16[1,2,96,2048]{3,2,1,0:T(8,128)(2,1)}, u32[]{:S(2)}, u32[]{:S(2)}) collective-permute-start(bf16[1,2,96,2048]{3,2,1,0:T(8,128)(2,1)} %get-tuple-element.163), channel_id=1, source_target_pairs={{0,4},{1,5},{2,6},{3,7},{4,0},{5,1},{6,2},{7,3},{8,12},{9,13},{10,... | collective-permute-start | bytes 2359304 | tf_op jit(solution)/shard_map/ppermute | solution.py:32
  404.9 19.5 %collective-permute-start.52 = (bf16[2,1,96,2048]{3,2,1,0:T(8,128)(2,1)}, bf16[2,1,96,2048]{3,2,1,0:T(8,128)(2,1)}, u32[]{:S(2)}, u32[]{:S(2)}) collective-permute-start(bf16[2,1,96,2048]{3,2,1,0:T(8,128)(2,1)} %get-tuple-element.165), channel_id=1, source_target_pairs={{0,2},{1,3},{2,0},{3,1},{4,6},{5,7},{6,4},{7,5},{8,10},{9,11},{10,... | collective-permute-start | bytes 2359304 | tf_op jit(solution)/shard_map/ppermute | solution.py:32
  431.7 30.5 %all-to-all-start.2 = ((bf16[8,64,1408]{2,1,0:T(8,128)(2,1)}), bf16[8,64,1408]{2,1,0:T(8,128)(2,1)S(1)}, u32[]{:S(2)}, u32[]{:S(2)}) async-start(bf16[8,64,1408]{2,1,0:T(8,128)(2,1)} %bitcast.293), calls=%async_computation.5 | async-start | bytes 2883584 | tf_op jit(solution)/shard_map/all_to_all | solution.py:238
  435.3 97.4 %reduce-scatter.11.cloned.1.call-start = ((), (), s32[]{:S(2)}) async-start(), calls=%async_computation.15 | async-start | bytes 1966080 | tf_op jit(solution)/shard_map/reduce_scatter | solution.py:234
  485.1 19.0 %collective-permute-start.55 = (bf16[1,1,96,2048]{3,2,1,0:T(8,128)(2,1)}, bf16[1,1,96,2048]{3,2,1,0:T(8,128)(2,1)S(1)}, u32[]{:S(2)}, u32[]{:S(2)}) collective-permute-start(bf16[1,1,96,2048]{3,2,1,0:T(8,128)(2,1)} %dynamic-slice_convert_fusion.2), channel_id=1, source_target_pairs={{0,2},{1,3},{2,0},{3,1},{4,6},{5,7},{6,4},{7,5},{8,10},{9,11},{10,... | collective-permute-start | bytes 1179656 | tf_op jit(solution)/shard_map/ppermute | solution.py:32
  499.4 33.3 %collective-permute-start.58 = (bf16[1,2,96,2048]{3,2,1,0:T(8,128)(2,1)}, bf16[1,2,96,2048]{3,2,1,0:T(8,128)(2,1)}, u32[]{:S(2)}, u32[]{:S(2)}) collective-permute-start(bf16[1,2,96,2048]{3,2,1,0:T(8,128)(2,1)} %get-tuple-element.159), channel_id=1, source_target_pairs={{0,4},{1,5},{2,6},{3,7},{4,0},{5,1},{6,2},{7,3},{8,12},{9,13},{10,... | collective-permute-start | bytes 2359304 | tf_op jit(solution)/shard_map/ppermute | solution.py:32
  502.5 30.2 %collective-permute-start.57 = (bf16[2,1,96,2048]{3,2,1,0:T(8,128)(2,1)}, bf16[2,1,96,2048]{3,2,1,0:T(8,128)(2,1)}, u32[]{:S(2)}, u32[]{:S(2)}) collective-permute-start(bf16[2,1,96,2048]{3,2,1,0:T(8,128)(2,1)} %get-tuple-element.161), channel_id=1, source_target_pairs={{0,2},{1,3},{2,0},{3,1},{4,6},{5,7},{6,4},{7,5},{8,10},{9,11},{10,... | collective-permute-start | bytes 2359304 | tf_op jit(solution)/shard_map/ppermute | solution.py:32
  (121 other events, 1251.2 us)
Sparse Core Ops, SparseCore 0:
  30.5 44.4 all-gather.4
  76.5 26.9 all-gather.6
  105.1 106.1 all-gather.8
  212.8 57.4 all-gather.10
  272.4 54.8 reduce-scatter.4
  329.5 102.1 reduce-scatter.6
  434.5 27.6 reduce-scatter.8
  486.7 45.9 reduce-scatter.10

commit v3 on v2

--- a/solution.py
+++ b/solution.py
@@ -48,13 +48,16 @@
     return [(step, (me // step) % 2) for step in bits]
 
 
-def gather_first(value):
+def gather_first(value, beside=None):
     count = lax.axis_size("ctx")
     bits = chip_bits()
     half = value.shape[0] // 2
     steps = (bits[0][0], bits[-1][0])
     parts = [value[:half], value[half:]]
-    return [(part, swap(part, step, count)) for part, step in zip(parts, steps)]
+    if beside is not None:
+        parts, beside = lax.optimization_barrier((parts, beside))
+    first = [(part, swap(part, step, count)) for part, step in zip(parts, steps)]
+    return first if beside is None else (first, beside)
 
 
 def gather_second(first):
@@ -179,6 +182,22 @@
     return [(i, (i % seqs) * ranks + i // seqs) for i in range(seqs * ranks)]
 
 
+def to_owners(value):
+    seqs, ranks = lax.axis_size("seq"), lax.axis_size("ctx")
+    me = lax.axis_index("ctx")
+    share = ranks // seqs
+    blocks = value.reshape(seqs, -1, value.shape[1])
+    whole = blank(blocks.shape, value.dtype)
+    came = []
+    for turn in range(seqs):
+        piece = lax.dynamic_index_in_dim(blocks, (me // share + seqs - turn) % seqs, 0, False)
+        pairs = [(r, r % share * seqs + (r // share - turn) % seqs) for r in range(ranks)]
+        came.append(lax.ppermute(piece, "ctx", pairs))
+        spot = (me % seqs + turn) % seqs
+        whole = lax.dynamic_update_index_in_dim(whole, came[-1], spot, 0)
+    return whole.reshape(value.shape), came
+
+
 def of_core(value, core):
     count = lax.axis_size("ctx")
     blocks = value.reshape(count // 2, 2, value.shape[0] // count, value.shape[1])
@@ -197,33 +216,45 @@
     return blocks_of((dot(stay, right, contract) + arrived.astype(f32)).astype(bf16))
 
 
-def scatter_step(current, at):
-    step, bit = chip_bits()[at]
+def scatter_parts(current, at):
+    bit = chip_bits()[at][1]
     axis = current.ndim - 3 - at
-    away = lax.dynamic_slice_in_dim(current, 1 - bit, 1, axis).astype(bf16)
     stay = lax.dynamic_slice_in_dim(current, bit, 1, axis).astype(f32)
-    return stay, swap(away, step, lax.axis_size("ctx"))
-
-
-def scatter_first(pairs):
-    bits = len(chip_bits())
+    return stay, lax.dynamic_slice_in_dim(current, 1 - bit, 1, axis).astype(bf16)
+
+
+def scatter_first(pairs, beside=()):
+    count = lax.axis_size("ctx")
+    bits = chip_bits()
     half, depth = pairs.shape[1] // 2, pairs.shape[2]
-    pairs = pairs.reshape((2,) * bits + (2, half, depth))
-    return scatter_step(pairs[..., 0, :, :], 0), scatter_step(pairs[..., 1, :, :], bits - 1)
+    pairs = pairs.reshape((2,) * len(bits) + (2, half, depth))
+    low = scatter_parts(pairs[..., 0, :, :], 0)
+    high = scatter_parts(pairs[..., 1, :, :], len(bits) - 1)
+    aways, beside = lax.optimization_barrier(((low[1], high[1]), beside))
+    first = [
+        (stay, swap(away, bits[at][0], count))
+        for (stay, _), away, at in ((low, aways[0], 0), (high, aways[1], len(bits) - 1))
+    ]
+    return first, beside
 
 
 def scatter_rest(first):
-    bits = len(chip_bits())
-    low, high = first
-    for at in range(1, bits):
-        low = scatter_step(low[0] + low[1].astype(f32), at)
-        high = scatter_step(high[0] + high[1].astype(f32), bits - 1 - at)
-    sums = [stay + arrived.astype(f32) for stay, arrived in (low, high)]
-    return jnp.concatenate([part.reshape(part.shape[-2:]) for part in sums])
+    count = lax.axis_size("ctx")
+    bits = chip_bits()
+    last = []
+    sums = []
+    for which, (stay, arrived) in enumerate(first):
+        for at in range(1, len(bits)):
+            at = len(bits) - 1 - at if which else at
+            stay, away = scatter_parts(stay + arrived.astype(f32), at)
+            arrived = swap(away, bits[at][0], count)
+        last.append(arrived)
+        sums.append(stay + arrived.astype(f32))
+    return jnp.concatenate([part.reshape(part.shape[-2:]) for part in sums]), last
 
 
 def scatter_pairs(pairs):
-    return scatter_rest(scatter_first(pairs))
+    return scatter_rest(scatter_first(pairs)[0])[0]
 
 
 def gather_seq(value):
@@ -345,7 +376,7 @@
     refs[-1][...] = out.astype(bf16)
 
 
-def by_rows(kernel, rows, weight, widths, name, part=None, also=None):
+def by_rows(kernel, rows, weight, widths, name, part=None, also=None, cost=LIGHT):
     number, parts = part or (0, 1)
     count = rows[0].shape[0] // parts
     block = 256 if count % 256 == 0 else count
@@ -367,7 +398,7 @@
         out_specs=[pl.BlockSpec((block, width), lambda i: (i, 0)) for width in widths],
         out_shape=[jax.ShapeDtypeStruct((count, width), bf16) for width in widths],
         compiler_params=pltpu.CompilerParams(vmem_limit_bytes=56 * 1024 * 1024),
-        cost_estimate=LIGHT,
+        cost_estimate=cost,
         name=name,
     )(*arrays)
 
@@ -375,7 +406,35 @@
 def product(rows, weight, contract, part, name):
     kernel = functools.partial(product_kernel, contract)
     width = weight.shape[1 - contract[1][0]]
-    return by_rows(kernel, rows, weight, [width], name, part)[0]
+    cost = pl.CostEstimate(flops=7_000_000_000, transcendentals=0, bytes_accessed=0)
+    return by_rows(kernel, rows, weight, [width], name, part, None, cost)[0]
+
+
+def outer_kernel(row_ref, *refs):
+    *others, out_ref = refs
+    first, total = 0, 0.0
+    for ref in others:
+        end = first + ref.shape[0]
+        total = total + dot(row_ref[first:end, :], ref[...], ((0,), (0,)))
+        first = end
+    out_ref[...] = total.astype(bf16)
+
+
+def outer(row, others):
+    count, depth = row.shape
+    width = others[0].shape[1]
+    block = 512 if depth % 512 == 0 else depth
+    return pl.pallas_call(
+        outer_kernel,
+        grid=(depth // block,),
+        in_specs=[pl.BlockSpec((count, block), lambda i: (0, i))]
+        + [pl.BlockSpec(other.shape, lambda i: (0, 0)) for other in others],
+        out_specs=pl.BlockSpec((block, width), lambda i: (i, 0)),
+        out_shape=jax.ShapeDtypeStruct((depth, width), bf16),
+        compiler_params=pltpu.CompilerParams(vmem_limit_bytes=56 * 1024 * 1024),
+        cost_estimate=LIGHT,
+        name="outer",
+    )(row, *others)
 
 
 def attention_block(length):
@@ -587,6 +646,7 @@
     gain_one_row, gain_two_row, seg_row, small = gather_small(spread, segments)
     mix = exchange_ctx(after(mix, last)).reshape(ranks * rows, -1)
     mix_wide = gather_seq(mix)
+    gain_one_row, gain_two_row, seg_row, small = gather_small(spread, segments)
     tokens_second = gather_second(lax.optimization_barrier((tokens_first, mix))[0])
     pair = split_units(after(gate_weight, mix, *small), up_weight, units)
     pair = exchange_ctx(pair).reshape(ranks * rows, -1)
@@ -645,10 +705,11 @@
     given.append(swap(away, 1, ranks))
     back_stay, two_pairs = by_rows(back, given, down_wide, wide, "hidden_back_stay", (0, 2), both)
     two_pairs = blocks_of(two_pairs)
-    grad_pair_in = jnp.concatenate([back_stay, back_away])
     grad_down = scatter_seq(grad_down).astype(f32)
-    shaped_two = scatter_pairs(two_pairs) * gain_two_row
-    grad_pair = dot(normed_two_all, grad_pair_in, ((0,), (0,)), bf16)
+    two_first, back_stay = scatter_first(two_pairs, back_stay)
+    shaped_two, _ = scatter_rest(two_first)
+    shaped_two = shaped_two * gain_two_row
+    grad_pair = outer(normed_two_all, [back_stay, back_away])
     shaped_two = after(shaped_two, grad_pair)
     grad_pair = scatter_seq(grad_pair)
     mean_two = jnp.mean(shaped_two * hidden, axis=-1, keepdims=True)
@@ -658,23 +719,21 @@
         - hidden * (factor_two * factor_two * factor_two * mean_two)
     )
 
-    branch_first = gather_first(grad_hidden.astype(bf16))
+    branch_first, activated = gather_first(grad_hidden.astype(bf16), activated)
     branch_second = gather_second(branch_first)
-    activated = after(activated, shaped_two)
     away = product([activated], down_wide, rows_by, (1, 2), "out_away")
     given = [after(activated, away), swap(away, 1, ranks)]
     out_pairs = blocks_of(product(given, down_wide, rows_by, (0, 2), "out_stay"))
     branch_second, out_pairs = lax.optimization_barrier((branch_second, out_pairs))
-    out_first = scatter_first(out_pairs)
+    out_first, _ = scatter_first(out_pairs)
     branch_all = gather_place(branch_second)
     grad_proj = dot(out_low, branch_all, ((0,), (0,)), bf16)
-    grad_out_t = dot(proj_wide, branch_all, columns_by, bf16)
-    grad_out_t, out_first, grad_down, grad_proj = lax.optimization_barrier(
-        (grad_out_t, out_first, grad_down, grad_proj)
-    )
-    grad_out_t = after(grad_out_t, grad_pair)
+    grad_out_t = after(dot(proj_wide, branch_all, columns_by, bf16), grad_proj, grad_pair)
+    grad_out_t, out_first = lax.optimization_barrier((grad_out_t, out_first))
+    out_sum, out_last = scatter_rest(out_first)
+    grad_proj, came = to_owners(grad_proj)
+    grad_out_t = after(grad_out_t, *came)
     grad_proj = scatter_seq(grad_proj)
-    out_sum = scatter_rest(out_first)
     grad_query_t, grad_key_t, grad_value_t = attention_backward(
         query_t, key_n, key_t, value_n, grad_out_t, out_t, lse, start_row
     )
@@ -687,19 +746,16 @@
         axis=0,
     ).astype(bf16)
     grad_pair = exchange_ctx(grad_pair.reshape(ranks, rows, -1))
-    grad_mixed = after(grad_mixed, out_sum, grad_proj, grad_pair)
+    grad_mixed = after(grad_mixed, grad_down, grad_pair, grad_proj)
+    grad_mix = dot(normed_all, grad_mixed, ((0,), (1,)), bf16)
     block_out = (hidden + out_sum).astype(bf16)
-    grad_mix = dot(normed_all, grad_mixed, ((0,), (1,)), bf16)
-    mixed_n = after(grad_mixed.T, grad_mix)
+    mixed_n = after(grad_mixed.T, grad_mix, *out_last)
     grad_mix = scatter_seq(grad_mix)
     shaped_one = pair_up(mixed_n, mix_wide, columns_by)
     grad_gate, grad_up, grad_feedforward = join_units(grad_pair, gate_weight, up_weight, units)
-    shaped_first = scatter_first(shaped_one)
-    arrived = [part for _, part in shaped_first]
-    shaped_first, grad_gate, block_out = lax.optimization_barrier(
-        (shaped_first, grad_gate, block_out)
-    )
-    shaped_one = scatter_rest(shaped_first)
+    shaped_first, _ = scatter_first(shaped_one)
+    shaped_first, grad_mix = lax.optimization_barrier((shaped_first, grad_mix, grad_gate))[:2]
+    shaped_one, arrived = scatter_rest(shaped_first)
     shaped_one = shaped_one * gain_one_row
     mean_one = jnp.mean(shaped_one * inputs, axis=-1, keepdims=True)
     grad_tokens = (
@@ -717,7 +773,7 @@
 
     grad_feedforward = grad_feedforward[:, 0] / feedforward_gain.astype(f32)
 
-    grad_mix = exchange_ctx(after(grad_mix, *arrived).reshape(ranks, rows, -1))
+    grad_mix = exchange_ctx(grad_mix.reshape(ranks, rows, -1))
     grad_query = grad_mix[:, :, :width].transpose(1, 0, 2).reshape(rows, -1).astype(f32)
     grad_key = join_heads(grad_mix[:, :, width : width + HD])
     grad_value = join_heads(grad_mix[:, :, width + HD :])
@@ -726,8 +782,7 @@
         + row_sum(grad_key, key_weight)
         + row_sum(grad_value, value_weight)
     ) / attention_gain.astype(f32)
-    back_order = [(b, a) for a, b in head_order()]
-    grad_projection = lax.ppermute(grad_proj, BOTH, back_order).astype(f32)
+    grad_projection = grad_proj.astype(f32)
     return (
         block_out,
         grad_tokens,

time: 578 us -> 568 us (0.983)
  waiting for transfers between devices: 208 us -> 169 us
  starting transfers between devices: 87.6 us -> 109 us
  matrix products: 59.1 us -> 41.6 us
  Pallas kernels: 111 us -> 125 us
    ppermute x58, waiting for transfers between devices: 147 us -> 126 us  [swap(): return lax.ppermute(value, 'ctx', [(i, i ^ step) for i in range(count)])]
    reduce_scatter x4, waiting for transfers between devices: 33 us -> 12.9 us  [scatter_seq(): return lax.psum_scatter(value, 'seq', scatter_dimension=0, tiled=True)]
    dot_general x10 -> x9, matrix products: 59.1 us -> 41.6 us  [dot(): lax.dot_general(left, right, (contract, ((), ())), preferred_element_type...]
    pallas_call x0 -> x1, Pallas kernels: none -> 14.5 us  [outer(): pl.pallas_call(outer_kernel, grid=(depth // block,), in_specs=[pl.BlockSp...]
    ppermute x1 -> x4, starting transfers between devices: 0.81 us -> 15.1 us  [to_owners(): came.append(lax.ppermute(piece, 'ctx', pairs))]
    ppermute x1 -> x4, waiting for transfers between devices: 0.01 us -> 11.4 us  [to_owners(): came.append(lax.ppermute(piece, 'ctx', pairs))]
    all_gather x4, starting transfers between devices: 0.69 us -> 10.3 us  [gather_seq(): return lax.all_gather(value, 'seq', axis=0, tiled=True)]
    all_gather x4, waiting for transfers between devices: 16 us -> 7.69 us  [gather_seq(): return lax.all_gather(value, 'seq', axis=0, tiled=True)]
  transfers between devices with their start and end apart: 73 -> 76, of which waited for: 36 -> 35; matrix products, arithmetic and copies ran while one was open for 19% -> 18% of each run, Pallas kernels for 19% -> 22%
where the time goes in v3:
time: 568 us; the launch traced here: 560 us
  waiting for transfers between devices  169 us (30%)
  Pallas kernels  125 us (22%)
  starting transfers between devices  109 us (19%)
  other arithmetic  46.1 us (8%)
  matrix products  41.6 us (7%)
  local copies, waits for them, and re-layouts  40.8 us (7%)
  between operations  16.1 us (3%)
  blocking collectives  12 us (2%)
    ppermute x58, waiting for transfers between devices, swap(): return lax.ppermute(value, 'ctx', [(i, i ^ step) for i in range(count)])  126 us
    ppermute x58, starting transfers between devices, swap(): return lax.ppermute(value, 'ctx', [(i, i ^ step) for i in range(count)])  62.8 us
    pallas_call x5, Pallas kernels, by_rows(): pl.pallas_call(kernel, grid=(count // block,), in_specs=specs, out_specs=...  61.2 us
    dot_general x9, matrix products, dot(): lax.dot_general(left, right, (contract, ((), ())), preferred_element_type...  41.6 us
    pallas_call x1, Pallas kernels, attention_backward(): pl.pallas_call(functools.partial(backward_kernel, block, heads, count), g...  20.9 us
    unnamed x154, local copies, waits for them, and re-layouts  16.9 us
    ppermute x4, starting transfers between devices, to_owners(): came.append(lax.ppermute(piece, 'ctx', pairs))  15.1 us
    pallas_call x1, Pallas kernels, outer(): pl.pallas_call(outer_kernel, grid=(depth // block,), in_specs=[pl.BlockSp...  14.5 us
  transfers between devices with their start and end apart: 76, of which 35 were waited for; matrix products, arithmetic and copies ran while one was open for 18% of the time, Pallas kernels for 22%

profile of v3, /device:TPU:0, one launch (start us, length us, event | category | flops | bytes accessed | tf_op | source)
XLA Modules:
  0.0 559.8 jit_solution(11291580224226804584)
XLA Ops:
  18.3 12.0 %all_to_all.20 = bf16[8,64,384]{2,1,0:T(8,128)(2,1)} all-to-all(bf16[8,64,384]{2,1,0:T(8,128)(2,1)S(1)} %copy.108), channel_id=1, replica_groups=mesh['seq'=4,'ctx'=8] {'ctx'}, dimensions={0} | all-to-all | bytes 786432 | tf_op jit(solution)/shard_map/all_to_all | solution.py:269
  35.3 6.0 %collective-permute-done.3 = bf16[96,2048]{1,0:T(8,128)(2,1)S(1)} collective-permute-done((bf16[96,2048]{1,0:T(8,128)(2,1)S(1)}, bf16[96,2048]{1,0:T(8,128)(2,1)S(1)}, u32[]{:S(2)}, u32[]{:S(2)}) %collective-permute-start.3) | collective-permute-done | bytes 393248 | tf_op jit(solution)/shard_map/ppermute | solution.py:32
  53.3 12.3 %collective-permute-start.13 = (f32[1,704]{1,0:T(1,128)S(1)}, f32[1,704]{1,0:T(1,128)S(1)}, u32[]{:S(2)}, u32[]{:S(2)}) collective-permute-start(f32[1,704]{1,0:T(1,128)S(1)} %pad_maximum_fusion.4), channel_id=1, source_target_pairs={{0,4},{1,5},{2,6},{3,7},{4,0},{5,1},{6,2},{7,3},{8,12},{9,13},{10,... | collective-permute-start | bytes 8456 | tf_op jit(solution)/shard_map/ppermute | solution.py:32
  72.4 4.4 all-to-all-start.1
  87.0 9.6 %all-to-all-done.1 = bf16[8,64,1408]{2,1,0:T(8,128)(2,1)} async-done(((bf16[8,64,1408]{2,1,0:T(8,128)(2,1)}), bf16[8,64,1408]{2,1,0:T(8,128)(2,1)}, u32[]{:S(2)}, u32[]{:S(2)}) %all-to-all-start.1) | async-done | bytes 1441824 | tf_op jit(solution)/shard_map/all_to_all | solution.py:269
  96.6 10.2 %all-gather.11.cloned.1.call-start = ((), (), s32[]{:S(2)}) async-start(), calls=%async_computation.11 | async-start | bytes 3604480 | tf_op jit(solution)/shard_map/all_gather | solution.py:261
  112.4 5.7 %fusion.32 = f32[384,1536]{1,0:T(8,128)S(1)} fusion(bf16[2048,384]{1,0:T(8,128)(2,1)} %all-gather.5.cloned.1.call-done, bf16[1536,2048]{1,0:T(8,128)(2,1)} %bitcast.277), kind=kOutput, calls=%fused_computation.155 | convolution fusion | flops 2415919104 | bytes 10223616 | tf_op jit(solution)/shard_map/dot_general | solution.py:24
  122.3 13.4 %attention_forward.1 = (f32[256,1536]{1,0:T(8,128)}, bf16[1536,256]{1,0:T(8,128)(2,1)}, f32[4,1536]{1,0:T(4,128)}) custom-call(bf16[1536,64]{1,0:T(8,128)(2,1)} %copy.111.key_ref, bf16[64,1536]{1,0:T(8,128)(2,1)} %copy.112.value_ref, bf16[256,1536]{1,0:T(8,128)(2,1)} %bitcast.290, s32[1,1536]{1,0:T(1,128)} %reduce_sum.93.start_ref), custom_call_target="tpu_custom_call" | custom-call | tf_op jit(solution)/shard_map/attention_forward/pallas_call | solution.py:472
  135.7 8.0 %collective-permute-done.18 = bf16[192,2048]{1,0:T(8,128)(2,1)S(1)} collective-permute-done((bf16[192,2048]{1,0:T(8,128)(2,1)S(1)}, bf16[192,2048]{1,0:T(8,128)(2,1)S(1)}, u32[]{:S(2)}, u32[]{:S(2)}) %collective-permute-start.18) | collective-permute-done | bytes 786464 | tf_op jit(solution)/shard_map/ppermute | solution.py:32
  148.4 5.8 %collective-permute-done.21 = bf16[768,2048]{1,0:T(8,128)(2,1)} collective-permute-done((bf16[768,2048]{1,0:T(8,128)(2,1)S(1)}, bf16[768,2048]{1,0:T(8,128)(2,1)}, u32[]{:S(2)}, u32[]{:S(2)}) %collective-permute-start.21) | collective-permute-done | bytes 3145760 | tf_op jit(solution)/shard_map/ppermute | solution.py:32
  163.0 15.8 %collective-permute-done.22 = bf16[2,1,96,2048]{3,2,1,0:T(8,128)(2,1)} collective-permute-done((bf16[2,1,96,2048]{3,2,1,0:T(8,128)(2,1)S(1)}, bf16[2,1,96,2048]{3,2,1,0:T(8,128)(2,1)}, u32[]{:S(2)}, u32[]{:S(2)}) %collective-permute-start.22) | collective-permute-done | bytes 786464 | tf_op jit(solution)/shard_map/ppermute | solution.py:32
  184.9 6.0 %collective-permute-done.23 = bf16[1,1,96,2048]{3,2,1,0:T(8,128)(2,1)S(1)} collective-permute-done((bf16[1,1,96,2048]{3,2,1,0:T(8,128)(2,1)S(1)}, bf16[1,1,96,2048]{3,2,1,0:T(8,128)(2,1)S(1)}, u32[]{:S(2)}, u32[]{:S(2)}) %collective-permute-start.23) | collective-permute-done | bytes 393248 | tf_op jit(solution)/shard_map/ppermute | solution.py:32
  198.6 9.7 %collective-permute-done.30 = bf16[96,2048]{1,0:T(8,128)(2,1)S(1)} collective-permute-done((bf16[96,2048]{1,0:T(8,128)(2,1)S(1)}, bf16[96,2048]{1,0:T(8,128)(2,1)S(1)}, u32[]{:S(2)}, u32[]{:S(2)}) %collective-permute-start.30) | collective-permute-done | bytes 393248 | tf_op jit(solution)/shard_map/ppermute | solution.py:32
  213.7 14.8 %collective-permute-done.32 = bf16[1,2,96,2048]{3,2,1,0:T(8,128)(2,1)S(1)} collective-permute-done((bf16[1,2,96,2048]{3,2,1,0:T(8,128)(2,1)S(1)}, bf16[1,2,96,2048]{3,2,1,0:T(8,128)(2,1)S(1)}, u32[]{:S(2)}, u32[]{:S(2)}) %collective-permute-start.32) | collective-permute-done | bytes 786464 | tf_op jit(solution)/shard_map/ppermute | solution.py:32
  238.3 16.5 %hidden_layer.1 = (bf16[1536,704]{1,0:T(8,128)(2,1)}, bf16[1536,704]{1,0:T(8,128)(2,1)}, bf16[1536,704]{1,0:T(8,128)(2,1)}) custom-call(bf16[1536,2048]{1,0:T(8,128)(2,1)} %bitcast.264, bf16[2048,1408]{1,0:T(8,128)(2,1)} %all-gather.9.cloned.1.call-done.weight_ref), custom_call_target="tpu_custom_call" | custom-call | tf_op jit(solution)/shard_map/hidden_layer/pallas_call | solution.py:394
  254.8 7.8 %convolution_convert_fusion.2 = bf16[704,2048]{1,0:T(8,128)(2,1)} fusion(bf16[1536,704]{1,0:T(8,128)(2,1)} %get-tuple-element.126.row_ref, bf16[1536,2048]{1,0:T(8,128)(2,1)S(1)} %bitcast.270), kind=kOutput, calls=%fused_computation.5 | convolution fusion | flops 4430626816 | bytes 11337728 | tf_op jit(solution)/shard_map/dot_general | solution.py:24
  262.6 7.7 %all-gather.11.cloned.1.call-done.down_ref.weight_ref = bf16[704,2048]{1,0:T(8,128)(2,1)} async-done(((bf16[176,2048]{1,0:T(8,128)(2,1)}), bf16[704,2048]{1,0:T(8,128)(2,1)}) %all-gather.11.cloned.1.call-update) | async-done | bytes 2883600 | tf_op jit(solution)/shard_map/all_gather | solution.py:261
  270.3 15.6 %hidden_back_away.1 = (bf16[768,1408]{1,0:T(8,128)(2,1)}, bf16[768,2048]{1,0:T(8,128)(2,1)}) custom-call(bf16[1536,2048]{1,0:T(8,128)(2,1)} %bitcast.268, bf16[704,2048]{1,0:T(8,128)(2,1)} %all-gather.11.cloned.1.call-done.down_ref.weight_ref, bf16[1536,704]{1,0:T(8,128)(2,1)} %get-tuple-element.112.slope_ref, ...), custom_call_target="tpu_custom_call" | custom-call | tf_op jit(solution)/shard_map/hidden_back_away/pallas_call | solution.py:394
  285.9 5.9 %collective-permute-done.38.refs_0_ = bf16[768,2048]{1,0:T(8,128)(2,1)S(1)} collective-permute-done((bf16[768,2048]{1,0:T(8,128)(2,1)}, bf16[768,2048]{1,0:T(8,128)(2,1)S(1)}, u32[]{:S(2)}, u32[]{:S(2)}) %collective-permute-start.38) | collective-permute-done | bytes 3145760 | tf_op jit(solution)/shard_map/ppermute | solution.py:32
  293.5 15.8 %hidden_back_stay.1 = (bf16[768,1408]{1,0:T(8,128)(2,1)}, bf16[768,2048]{1,0:T(8,128)(2,1)}) custom-call(bf16[1536,2048]{1,0:T(8,128)(2,1)} %bitcast.269, bf16[704,2048]{1,0:T(8,128)(2,1)} %all-gather.11.cloned.1.call-done.down_ref.weight_ref, bf16[1536,704]{1,0:T(8,128)(2,1)} %get-tuple-element.112.slope_ref, ...), custom_call_target="tpu_custom_call" | custom-call | tf_op jit(solution)/shard_map/hidden_back_stay/pallas_call | solution.py:394
  316.5 14.5 %outer.1 = bf16[2048,1408]{1,0:T(8,128)(2,1)} custom-call(bf16[1536,2048]{1,0:T(8,128)(2,1)} %bitcast.265, bf16[768,1408]{1,0:T(8,128)(2,1)} %get-tuple-element.120.refs_0_, bf16[768,1408]{1,0:T(8,128)(2,1)} %get-tuple-element.121.refs_1_), custom_call_target="tpu_custom_call" | custom-call | tf_op jit(solution)/shard_map/outer/pallas_call | solution.py:427
  339.7 5.8 %collective-permute-done.40 = bf16[1,1,96,2048]{3,2,1,0:T(8,128)(2,1)S(1)} collective-permute-done((bf16[1,1,96,2048]{3,2,1,0:T(8,128)(2,1)S(1)}, bf16[1,1,96,2048]{3,2,1,0:T(8,128)(2,1)S(1)}, u32[]{:S(2)}, u32[]{:S(2)}) %collective-permute-start.40) | collective-permute-done | bytes 393248 | tf_op jit(solution)/shard_map/ppermute | solution.py:32
  351.8 6.2 %out_away.1 = bf16[768,2048]{1,0:T(8,128)(2,1)} custom-call(bf16[1536,704]{1,0:T(8,128)(2,1)} %get-tuple-element.126.row_ref, bf16[704,2048]{1,0:T(8,128)(2,1)} %all-gather.11.cloned.1.call-done.down_ref.weight_ref), custom_call_target="tpu_custom_call" | custom-call | flops 7000000000 | tf_op jit(solution)/shard_map/out_away/pallas_call | solution.py:394
  359.9 9.6 %collective-permute-done.45 = bf16[96,2048]{1,0:T(8,128)(2,1)S(1)} collective-permute-done((bf16[96,2048]{1,0:T(8,128)(2,1)S(1)}, bf16[96,2048]{1,0:T(8,128)(2,1)S(1)}, u32[]{:S(2)}, u32[]{:S(2)}) %collective-permute-start.45) | collective-permute-done | bytes 393248 | tf_op jit(solution)/shard_map/ppermute | solution.py:32
  374.3 7.2 %out_stay.1 = bf16[768,2048]{1,0:T(8,128)(2,1)} custom-call(bf16[1536,704]{1,0:T(8,128)(2,1)} %get-tuple-element.126.row_ref, bf16[704,2048]{1,0:T(8,128)(2,1)} %all-gather.11.cloned.1.call-done.down_ref.weight_ref, bf16[768,2048]{1,0:T(8,128)(2,1)} %collective-permute-done.47.refs_0_), custom_call_target="tpu_custom_call" | custom-call | flops 7000000000 | tf_op jit(solution)/shard_map/out_stay/pallas_call | solution.py:394
  381.4 7.6 %collective-permute-done.46 = bf16[2,1,96,2048]{3,2,0,1:T(8,128)(2,1)S(1)} collective-permute-done((bf16[2,1,96,2048]{3,2,0,1:T(8,128)(2,1)S(1)}, bf16[2,1,96,2048]{3,2,0,1:T(8,128)(2,1)S(1)}, u32[]{:S(2)}, u32[]{:S(2)}) %collective-permute-start.46) | collective-permute-done | bytes 786464 | tf_op jit(solution)/shard_map/ppermute | solution.py:32
  402.8 4.7 convolution_convert_fusion.4
  413.4 12.1 %collective-permute-start.57 = (bf16[64,2048]{1,0:T(8,128)(2,1)S(1)}, bf16[64,2048]{1,0:T(8,128)(2,1)S(1)}, u32[]{:S(2)}, u32[]{:S(2)}) collective-permute-start(bf16[64,2048]{1,0:T(8,128)(2,1)S(1)} %get-tuple-element.189), channel_id=1, source_target_pairs={{0,3},{1,7},{2,0},{3,4},{4,1},{5,5},{6,2},{7,6},{8,11},{9,15},{10,... | collective-permute-start | bytes 786440 | tf_op jit(solution)/shard_map/ppermute | solution.py:195
  425.6 11.4 %collective-permute-done.57 = bf16[64,2048]{1,0:T(8,128)(2,1)S(1)} collective-permute-done((bf16[64,2048]{1,0:T(8,128)(2,1)S(1)}, bf16[64,2048]{1,0:T(8,128)(2,1)S(1)}, u32[]{:S(2)}, u32[]{:S(2)}) %collective-permute-start.57) | collective-permute-done | bytes 262176 | tf_op jit(solution)/shard_map/ppermute | solution.py:195
  441.8 20.9 %attention_backward.1 = (f32[256,1536]{1,0:T(8,128)}, f32[64,1536]{1,0:T(8,128)}, f32[64,1536]{1,0:T(8,128)}) custom-call(bf16[1536,64]{1,0:T(8,128)(2,1)} %copy.111.key_ref, bf16[64,1536]{1,0:T(8,128)(2,1)} %bitcast.317, bf16[1536,64]{1,0:T(8,128)(2,1)} %bitcast.296, bf16[256,1536]{1,0:T(8,128)(2,1)} %bitcast.291, ...), custom_call_target="tpu_custom_call" | custom-call | flops 24999999488 | tf_op jit(solution)/shard_map/attention_backward/pallas_call | solution.py:560
  475.2 7.4 %convolution_convert_fusion.3 = bf16[2048,384]{1,0:T(8,128)(2,1)} fusion(bf16[1536,2048]{1,0:T(8,128)(2,1)} %bitcast.278, bf16[384,1536]{1,0:T(8,128)(2,1)S(1)} %pad_maximum_fusion), kind=kOutput, calls=%fused_computation.6 | convolution fusion | flops 2416705536 | bytes 9043968 | tf_op jit(solution)/shard_map/dot_general | solution.py:24
  511.4 12.8 %reduce-scatter.11.cloned.1.call-done = bf16[512,384]{1,0:T(8,128)(2,1)} async-done(((bf16[2048,384]{1,0:T(8,128)(2,1)}), bf16[512,384]{1,0:T(8,128)(2,1)}) %reduce-scatter.11.cloned.1.call-update) | async-done | bytes 393232 | tf_op jit(solution)/shard_map/reduce_scatter | solution.py:265
  (448 shorter events, 220.7 us)
Async XLA Ops:
  7.2 105.2 %all-gather.5.cloned.1.call-start = ((), (), s32[]{:S(2)}) async-start(), calls=%async_computation.8 | async-start | bytes 1966080 | tf_op jit(solution)/shard_map/all_gather | solution.py:261
  30.3 115.7 %all-gather.7.cloned.1.call-start = ((), (), s32[]{:S(2)}) async-start(), calls=%async_computation.9 | async-start | bytes 1310720 | tf_op jit(solution)/shard_map/all_gather | solution.py:261
  31.7 20.3 %collective-permute-start.20 = (bf16[64,2048]{1,0:T(8,128)(2,1)}, bf16[64,2048]{1,0:T(8,128)(2,1)}, u32[]{:S(2)}, u32[]{:S(2)}) collective-permute-start(bf16[64,2048]{1,0:T(8,128)(2,1)} %param.19), channel_id=1, source_target_pairs={{0,0},{1,8},{2,16},{3,24},{4,1},{5,9},{6,17},{7,25},{8,2},{9,10},{... | collective-permute-start | bytes 786440 | tf_op jit(solution)/shard_map/ppermute | solution.py:653
  44.2 33.3 %collective-permute-start.5 = (bf16[1,2,96,2048]{3,2,1,0:T(8,128)(2,1)}, bf16[1,2,96,2048]{3,2,1,0:T(8,128)(2,1)S(1)}, u32[]{:S(2)}, u32[]{:S(2)}) collective-permute-start(bf16[1,2,96,2048]{3,2,1,0:T(8,128)(2,1)} %maximum_select_fusion.1), channel_id=1, source_target_pairs={{0,4},{1,5},{2,6},{3,7},{4,0},{5,1},{6,2},{7,3},{8,12},{9,13},{10,... | collective-permute-start | bytes 2359304 | tf_op jit(solution)/shard_map/ppermute | solution.py:32
  49.6 28.3 %collective-permute-start.8 = (bf16[2,1,96,2048]{3,2,1,0:T(8,128)(2,1)}, bf16[2,1,96,2048]{3,2,1,0:T(8,128)(2,1)S(1)}, u32[]{:S(2)}, u32[]{:S(2)}) collective-permute-start(bf16[2,1,96,2048]{3,2,1,0:T(8,128)(2,1)} %maximum_select_fusion.3), channel_id=1, source_target_pairs={{0,2},{1,3},{2,0},{3,1},{4,6},{5,7},{6,4},{7,5},{8,10},{9,11},{10,... | collective-permute-start | bytes 2359304 | tf_op jit(solution)/shard_map/ppermute | solution.py:32
  72.4 24.2 %all-to-all-start.1 = ((bf16[8,64,1408]{2,1,0:T(8,128)(2,1)}), bf16[8,64,1408]{2,1,0:T(8,128)(2,1)}, u32[]{:S(2)}, u32[]{:S(2)}) async-start(bf16[8,64,1408]{2,1,0:T(8,128)(2,1)} %split_units.1), calls=%async_computation.1 | async-start | bytes 2883584 | tf_op jit(solution)/shard_map/all_to_all | solution.py:269
  76.9 161.4 %all-gather.9.cloned.1.call-start = ((), (), s32[]{:S(2)}) async-start(), calls=%async_computation.10 | async-start | bytes 7208960 | tf_op jit(solution)/shard_map/all_gather | solution.py:261
  96.6 173.7 %all-gather.11.cloned.1.call-start = ((), (), s32[]{:S(2)}) async-start(), calls=%async_computation.11 | async-start | bytes 3604480 | tf_op jit(solution)/shard_map/all_gather | solution.py:261
  108.9 26.8 %collective-permute-start.19 = (bf16[192,2048]{1,0:T(8,128)(2,1)S(1)}, bf16[192,2048]{1,0:T(8,128)(2,1)S(1)}, u32[]{:S(2)}, u32[]{:S(2)}) collective-permute-start(bf16[192,2048]{1,0:T(8,128)(2,1)S(1)} %copy-done.17), channel_id=1, source_target_pairs={{0,6},{1,7},{2,4},{3,5},{4,2},{5,3},{6,0},{7,1},{8,14},{9,15},{10,... | collective-permute-start | bytes 2359304 | tf_op jit(solution)/shard_map/ppermute | solution.py:32
  109.4 34.3 %collective-permute-start.18 = (bf16[192,2048]{1,0:T(8,128)(2,1)S(1)}, bf16[192,2048]{1,0:T(8,128)(2,1)S(1)}, u32[]{:S(2)}, u32[]{:S(2)}) collective-permute-start(bf16[192,2048]{1,0:T(8,128)(2,1)S(1)} %copy-done.17), channel_id=1, source_target_pairs={{0,4},{1,5},{2,6},{3,7},{4,0},{5,1},{6,2},{7,3},{8,12},{9,13},{10,... | collective-permute-start | bytes 2359304 | tf_op jit(solution)/shard_map/ppermute | solution.py:32
  110.8 33.3 %collective-permute-start.17 = (bf16[192,2048]{1,0:T(8,128)(2,1)S(1)}, bf16[192,2048]{1,0:T(8,128)(2,1)}, u32[]{:S(2)}, u32[]{:S(2)}) collective-permute-start(bf16[192,2048]{1,0:T(8,128)(2,1)S(1)} %copy-done.17), channel_id=1, source_target_pairs={{0,2},{1,3},{2,0},{3,1},{4,6},{5,7},{6,4},{7,5},{8,10},{9,11},{10,... | collective-permute-start | bytes 2359304 | tf_op jit(solution)/shard_map/ppermute | solution.py:32
  158.9 19.9 %collective-permute-start.22 = (bf16[2,1,96,2048]{3,2,1,0:T(8,128)(2,1)S(1)}, bf16[2,1,96,2048]{3,2,1,0:T(8,128)(2,1)}, u32[]{:S(2)}, u32[]{:S(2)}) collective-permute-start(bf16[2,1,96,2048]{3,2,1,0:T(8,128)(2,1)S(1)} %dynamic-slice_bitcast_fusion.7), channel_id=1, source_target_pairs={{0,2},{1,3},{2,0},{3,1},{4,6},{5,7},{6,4},{7,5},{8,10},{9,11},{10,... | collective-permute-start | bytes 2359304 | tf_op jit(solution)/shard_map/ppermute | solution.py:32
  160.9 20.8 %collective-permute-start.24 = (bf16[1,2,96,2048]{3,2,1,0:T(8,128)(2,1)S(1)}, bf16[1,2,96,2048]{3,2,1,0:T(8,128)(2,1)}, u32[]{:S(2)}, u32[]{:S(2)}) collective-permute-start(bf16[1,2,96,2048]{3,2,1,0:T(8,128)(2,1)S(1)} %dynamic-slice_bitcast_fusion.6), channel_id=1, source_target_pairs={{0,4},{1,5},{2,6},{3,7},{4,0},{5,1},{6,2},{7,3},{8,12},{9,13},{10,... | collective-permute-start | bytes 2359304 | tf_op jit(solution)/shard_map/ppermute | solution.py:32
  163.0 208.9 %reduce-scatter.7.cloned.1.call-start = ((), (), s32[]{:S(2)}) async-start(), calls=%async_computation.13 | async-start | bytes 3604480 | tf_op jit(solution)/shard_map/reduce_scatter | solution.py:265
  208.3 23.3 %collective-permute-start.29 = (bf16[192,2048]{1,0:T(8,128)(2,1)S(1)}, bf16[192,2048]{1,0:T(8,128)(2,1)S(1)}, u32[]{:S(2)}, u32[]{:S(2)}) collective-permute-start(bf16[192,2048]{1,0:T(8,128)(2,1)S(1)} %copy-done.55), channel_id=1, source_target_pairs={{0,1},{1,0},{2,3},{3,2},{4,5},{5,4},{6,7},{7,6},{8,9},{9,8},{10,11... | collective-permute-start | bytes 2359304 | tf_op jit(solution)/shard_map/ppermute | solution.py:32
  208.4 20.0 %collective-permute-start.32 = (bf16[1,2,96,2048]{3,2,1,0:T(8,128)(2,1)S(1)}, bf16[1,2,96,2048]{3,2,1,0:T(8,128)(2,1)S(1)}, u32[]{:S(2)}, u32[]{:S(2)}) collective-permute-start(bf16[1,2,96,2048]{3,2,1,0:T(8,128)(2,1)S(1)} %maximum_select_fusion.5), channel_id=1, source_target_pairs={{0,4},{1,5},{2,6},{3,7},{4,0},{5,1},{6,2},{7,3},{8,12},{9,13},{10,... | collective-permute-start | bytes 2359304 | tf_op jit(solution)/shard_map/ppermute | solution.py:32
  210.1 21.6 %collective-permute-start.31 = (bf16[1,2,96,2048]{3,2,1,0:T(8,128)(2,1)S(1)}, bf16[1,2,96,2048]{3,2,1,0:T(8,128)(2,1)S(1)}, u32[]{:S(2)}, u32[]{:S(2)}) collective-permute-start(bf16[1,2,96,2048]{3,2,1,0:T(8,128)(2,1)S(1)} %maximum_select_fusion.5), channel_id=1, source_target_pairs={{0,1},{1,0},{2,3},{3,2},{4,5},{5,4},{6,7},{7,6},{8,9},{9,8},{10,11... | collective-permute-start | bytes 2359304 | tf_op jit(solution)/shard_map/ppermute | solution.py:32
  211.7 19.8 %collective-permute-start.36 = (bf16[2,1,96,2048]{3,2,1,0:T(8,128)(2,1)S(1)}, bf16[2,1,96,2048]{3,2,1,0:T(8,128)(2,1)S(1)}, u32[]{:S(2)}, u32[]{:S(2)}) collective-permute-start(bf16[2,1,96,2048]{3,2,1,0:T(8,128)(2,1)S(1)} %maximum_select_fusion.7), channel_id=1, source_target_pairs={{0,2},{1,3},{2,0},{3,1},{4,6},{5,7},{6,4},{7,5},{8,10},{9,11},{10,... | collective-permute-start | bytes 2359304 | tf_op jit(solution)/shard_map/ppermute | solution.py:32
  262.6 175.5 %reduce-scatter.5.cloned.1.call-start = ((), (), s32[]{:S(2)}) async-start(), calls=%async_computation.12 | async-start | bytes 7208960 | tf_op jit(solution)/shard_map/reduce_scatter | solution.py:265
  313.5 19.9 %collective-permute-start.39 = (bf16[2,1,96,2048]{3,2,1,0:T(8,128)(2,1)}, bf16[2,1,96,2048]{3,2,1,0:T(8,128)(2,1)}, u32[]{:S(2)}, u32[]{:S(2)}) collective-permute-start(bf16[2,1,96,2048]{3,2,1,0:T(8,128)(2,1)} %dynamic-slice_bitcast_fusion.5), channel_id=1, source_target_pairs={{0,2},{1,3},{2,0},{3,1},{4,6},{5,7},{6,4},{7,5},{8,10},{9,11},{10,... | collective-permute-start | bytes 2359304 | tf_op jit(solution)/shard_map/ppermute | solution.py:32
  315.0 21.6 %collective-permute-start.41 = (bf16[1,2,96,2048]{3,2,1,0:T(8,128)(2,1)S(1)}, bf16[1,2,96,2048]{3,2,1,0:T(8,128)(2,1)}, u32[]{:S(2)}, u32[]{:S(2)}) collective-permute-start(bf16[1,2,96,2048]{3,2,1,0:T(8,128)(2,1)S(1)} %dynamic-slice_bitcast_fusion.4), channel_id=1, source_target_pairs={{0,4},{1,5},{2,6},{3,7},{4,0},{5,1},{6,2},{7,3},{8,12},{9,13},{10,... | collective-permute-start | bytes 2359304 | tf_op jit(solution)/shard_map/ppermute | solution.py:32
  330.9 144.2 %reduce-scatter.9.cloned.1.call-start = ((), (), s32[]{:S(2)}) async-start(), calls=%async_computation.14 | async-start | bytes 1310720 | tf_op jit(solution)/shard_map/reduce_scatter | solution.py:265
  369.7 19.3 %collective-permute-start.46 = (bf16[2,1,96,2048]{3,2,0,1:T(8,128)(2,1)S(1)}, bf16[2,1,96,2048]{3,2,0,1:T(8,128)(2,1)S(1)}, u32[]{:S(2)}, u32[]{:S(2)}) collective-permute-start(bf16[2,1,96,2048]{3,2,0,1:T(8,128)(2,1)S(1)} %bitcast_select_fusion), channel_id=1, source_target_pairs={{0,2},{1,3},{2,0},{3,1},{4,6},{5,7},{6,4},{7,5},{8,10},{9,11},{10,... | collective-permute-start | bytes 2359304 | tf_op jit(solution)/shard_map/ppermute | solution.py:32
  397.0 44.7 %collective-permute-start.52 = (bf16[2,1,96,2048]{3,2,1,0:T(8,128)(2,1)}, bf16[2,1,96,2048]{3,2,1,0:T(8,128)(2,1)}, u32[]{:S(2)}, u32[]{:S(2)}) collective-permute-start(bf16[2,1,96,2048]{3,2,1,0:T(8,128)(2,1)} %get-tuple-element.133), channel_id=1, source_target_pairs={{0,2},{1,3},{2,0},{3,1},{4,6},{5,7},{6,4},{7,5},{8,10},{9,11},{10,... | collective-permute-start | bytes 2359304 | tf_op jit(solution)/shard_map/ppermute | solution.py:32
  397.7 44.1 %collective-permute-start.53 = (bf16[1,2,96,2048]{3,2,1,0:T(8,128)(2,1)}, bf16[1,2,96,2048]{3,2,1,0:T(8,128)(2,1)}, u32[]{:S(2)}, u32[]{:S(2)}) collective-permute-start(bf16[1,2,96,2048]{3,2,1,0:T(8,128)(2,1)} %get-tuple-element.134), channel_id=1, source_target_pairs={{0,4},{1,5},{2,6},{3,7},{4,0},{5,1},{6,2},{7,3},{8,12},{9,13},{10,... | collective-permute-start | bytes 2359304 | tf_op jit(solution)/shard_map/ppermute | solution.py:32
  407.7 29.4 %collective-permute-start.59 = (bf16[64,2048]{1,0:T(8,128)(2,1)S(1)}, bf16[64,2048]{1,0:T(8,128)(2,1)S(1)}, u32[]{:S(2)}, u32[]{:S(2)}) collective-permute-start(bf16[64,2048]{1,0:T(8,128)(2,1)S(1)} %get-tuple-element.187), channel_id=1, source_target_pairs={{0,1},{1,5},{2,2},{3,6},{4,3},{5,7},{6,0},{7,4},{8,9},{9,13},{10,1... | collective-permute-start | bytes 786440 | tf_op jit(solution)/shard_map/ppermute | solution.py:195
  409.7 27.3 %collective-permute-start.58 = (bf16[64,2048]{1,0:T(8,128)(2,1)S(1)}, bf16[64,2048]{1,0:T(8,128)(2,1)S(1)}, u32[]{:S(2)}, u32[]{:S(2)}) collective-permute-start(bf16[64,2048]{1,0:T(8,128)(2,1)S(1)} %get-tuple-element.188), channel_id=1, source_target_pairs={{0,2},{1,6},{2,3},{3,7},{4,0},{5,4},{6,1},{7,5},{8,10},{9,14},{10,... | collective-permute-start | bytes 786440 | tf_op jit(solution)/shard_map/ppermute | solution.py:195
  413.4 23.6 %collective-permute-start.57 = (bf16[64,2048]{1,0:T(8,128)(2,1)S(1)}, bf16[64,2048]{1,0:T(8,128)(2,1)S(1)}, u32[]{:S(2)}, u32[]{:S(2)}) collective-permute-start(bf16[64,2048]{1,0:T(8,128)(2,1)S(1)} %get-tuple-element.189), channel_id=1, source_target_pairs={{0,3},{1,7},{2,0},{3,4},{4,1},{5,5},{6,2},{7,6},{8,11},{9,15},{10,... | collective-permute-start | bytes 786440 | tf_op jit(solution)/shard_map/ppermute | solution.py:195
  438.1 37.0 %all-to-all-start.2 = ((bf16[8,64,1408]{2,1,0:T(8,128)(2,1)}), bf16[8,64,1408]{2,1,0:T(8,128)(2,1)S(1)}, u32[]{:S(2)}, u32[]{:S(2)}) async-start(bf16[8,64,1408]{2,1,0:T(8,128)(2,1)} %bitcast.310), calls=%async_computation.4 | async-start | bytes 2883584 | tf_op jit(solution)/shard_map/all_to_all | solution.py:269
  441.7 82.5 %reduce-scatter.11.cloned.1.call-start = ((), (), s32[]{:S(2)}) async-start(), calls=%async_computation.15 | async-start | bytes 1966080 | tf_op jit(solution)/shard_map/reduce_scatter | solution.py:265
  504.3 20.0 %collective-permute-start.61 = (bf16[2,1,96,2048]{3,2,1,0:T(8,128)(2,1)}, bf16[2,1,96,2048]{3,2,1,0:T(8,128)(2,1)}, u32[]{:S(2)}, u32[]{:S(2)}) collective-permute-start(bf16[2,1,96,2048]{3,2,1,0:T(8,128)(2,1)} %get-tuple-element.149), channel_id=1, source_target_pairs={{0,2},{1,3},{2,0},{3,1},{4,6},{5,7},{6,4},{7,5},{8,10},{9,11},{10,... | collective-permute-start | bytes 2359304 | tf_op jit(solution)/shard_map/ppermute | solution.py:32
  505.9 19.6 %collective-permute-start.62 = (bf16[1,2,96,2048]{3,2,1,0:T(8,128)(2,1)}, bf16[1,2,96,2048]{3,2,1,0:T(8,128)(2,1)}, u32[]{:S(2)}, u32[]{:S(2)}) collective-permute-start(bf16[1,2,96,2048]{3,2,1,0:T(8,128)(2,1)} %get-tuple-element.150), channel_id=1, source_target_pairs={{0,4},{1,5},{2,6},{3,7},{4,0},{5,1},{6,2},{7,3},{8,12},{9,13},{10,... | collective-permute-start | bytes 2359304 | tf_op jit(solution)/shard_map/ppermute | solution.py:32
  (120 other events, 1042.7 us)
Sparse Core Ops, SparseCore 0:
  30.5 44.4 all-gather.4
  76.5 26.9 all-gather.6
  105.1 106.1 all-gather.8
  212.8 57.4 all-gather.10
  272.4 54.8 reduce-scatter.6
  331.1 100.5 reduce-scatter.4
  438.2 23.9 reduce-scatter.8
  491.2 33.0 reduce-scatter.10

commit v4 on v3

--- a/solution.py
+++ b/solution.py
@@ -269,19 +269,19 @@
     return lax.all_to_all(value, "ctx", 0, 0)
 
 
-def gather_small(spread, segments):
-    seqs, ranks = lax.axis_size("seq"), lax.axis_size("ctx")
-    me = lax.axis_index("ctx")
-    line = jnp.concatenate([spread.reshape(1, -1), segments.astype(f32)], axis=1)
-    chips = send_chips(line)
-    others = {step: swap(piece, 1, ranks) for step, piece in chips.items()}
-    table = jnp.zeros((ranks, line.shape[1]), f32)
-    for step, piece in chips.items():
-        table = lax.dynamic_update_slice_in_dim(table, piece, me ^ step, 0)
-        table = lax.dynamic_update_slice_in_dim(table, others[step], me ^ step ^ 1, 0)
-    width = spread.size
+def small_rows(spread, segments, width):
+    line = jnp.concatenate([spread.reshape(-1), segments.reshape(-1).astype(f32)]).astype(bf16)
+    count = -(-line.size // (16 * width)) * 16
+    return jnp.pad(line, (0, count * width - line.size)).reshape(count, width)
+
+
+def read_small(table, spread, segments):
+    ranks, seqs = table.shape[0], spread.shape[0]
+    table = table.reshape(ranks, -1)
+    width, count = spread.size, segments.size
     gains = table[:, :width].reshape(ranks, seqs, 2, -1).transpose(2, 1, 0, 3).reshape(2, -1)
-    return gains[:1], gains[1:], table[:, width:].reshape(1, -1), list(others.values())
+    gains = gains.astype(f32)
+    return gains[:1], gains[1:], table[:, width : width + count].astype(f32).reshape(1, -1)
 
 
 def unit_pieces(seqs, ranks, units):
@@ -403,10 +403,12 @@
     )(*arrays)
 
 
-def product(rows, weight, contract, part, name):
+HIDDEN_COST = pl.CostEstimate(flops=7_000_000_000, transcendentals=0, bytes_accessed=0)
+
+
+def product(rows, weight, contract, part, name, cost=HIDDEN_COST):
     kernel = functools.partial(product_kernel, contract)
     width = weight.shape[1 - contract[1][0]]
-    cost = pl.CostEstimate(flops=7_000_000_000, transcendentals=0, bytes_accessed=0)
     return by_rows(kernel, rows, weight, [width], name, part, None, cost)[0]
 
 
@@ -643,15 +645,16 @@
         ],
         axis=2,
     ).transpose(1, 0, 2)
-    gain_one_row, gain_two_row, seg_row, small = gather_small(spread, segments)
-    mix = exchange_ctx(after(mix, last)).reshape(ranks * rows, -1)
-    mix_wide = gather_seq(mix)
-    gain_one_row, gain_two_row, seg_row, small = gather_small(spread, segments)
+    small = small_rows(spread, segments, mix.shape[2])
+    small = jnp.broadcast_to(small[None], (ranks,) + small.shape)
+    mix = exchange_ctx(jnp.concatenate([mix, small], axis=1))
+    gain_one_row, gain_two_row, seg_row = read_small(mix[:, rows:], spread, segments)
+    mix = mix[:, :rows].reshape(ranks * rows, -1)
+    proj_wide = gather_seq(lax.ppermute(after(projection, last), BOTH, head_order()))
+    mix_wide = gather_seq(after(mix, proj_wide))
     tokens_second = gather_second(lax.optimization_barrier((tokens_first, mix))[0])
-    pair = split_units(after(gate_weight, mix, *small), up_weight, units)
+    pair = split_units(after(gate_weight, mix), up_weight, units)
     pair = exchange_ctx(pair).reshape(ranks * rows, -1)
-    proj = lax.ppermute(after(projection, mix), BOTH, head_order())
-    proj_wide = gather_seq(proj)
 
     start = jnp.sum((seg_row < seg_row.T).astype(jnp.int32), axis=1)
     positions = jnp.arange(length, dtype=jnp.int32) - start
@@ -728,9 +731,11 @@
     out_first, _ = scatter_first(out_pairs)
     branch_all = gather_place(branch_second)
     grad_proj = dot(out_low, branch_all, ((0,), (0,)), bf16)
-    grad_out_t = after(dot(proj_wide, branch_all, columns_by, bf16), grad_proj, grad_pair)
+    grad_out_t = after(dot(proj_wide, branch_all, columns_by, bf16), grad_proj)
     grad_out_t, out_first = lax.optimization_barrier((grad_out_t, out_first))
     out_sum, out_last = scatter_rest(out_first)
+    grad_out_t = after(grad_out_t, *out_last)
+    grad_out_t = after(grad_out_t, grad_pair)
     grad_proj, came = to_owners(grad_proj)
     grad_out_t = after(grad_out_t, *came)
     grad_proj = scatter_seq(grad_proj)
@@ -747,14 +752,20 @@
     ).astype(bf16)
     grad_pair = exchange_ctx(grad_pair.reshape(ranks, rows, -1))
     grad_mixed = after(grad_mixed, grad_down, grad_pair, grad_proj)
-    grad_mix = dot(normed_all, grad_mixed, ((0,), (1,)), bf16)
     block_out = (hidden + out_sum).astype(bf16)
-    mixed_n = after(grad_mixed.T, grad_mix, *out_last)
+    mixed_n = grad_mixed.T
+    core = lax.axis_index("ctx") % 2
+    parts = [of_core(mixed_n, 1 - core), of_core(mixed_n, core)]
+    away = product(parts[:1], mix_wide, columns_by, None, "mixed_away", LIGHT)
+    grad_mix = dot(normed_all, after(grad_mixed, away), ((0,), (1,)), bf16)
     grad_mix = scatter_seq(grad_mix)
-    shaped_one = pair_up(mixed_n, mix_wide, columns_by)
+    parts = [after(parts[1], away), swap(away, 1, ranks)]
+    shaped_one = blocks_of(product(parts, mix_wide, columns_by, None, "mixed_stay", LIGHT))
     grad_gate, grad_up, grad_feedforward = join_units(grad_pair, gate_weight, up_weight, units)
     shaped_first, _ = scatter_first(shaped_one)
-    shaped_first, grad_mix = lax.optimization_barrier((shaped_first, grad_mix, grad_gate))[:2]
+    shaped_first, grad_mix = lax.optimization_barrier(
+        (shaped_first, grad_mix, grad_gate)
+    )[:2]
     shaped_one, arrived = scatter_rest(shaped_first)
     shaped_one = shaped_one * gain_one_row
     mean_one = jnp.mean(shaped_one * inputs, axis=-1, keepdims=True)

time: 568 us -> 558 us (0.982)
  blocking collectives: 12 us -> 0 us
  starting transfers between devices: 109 us -> 97.8 us
  Pallas kernels: 125 us -> 136 us
  waiting for transfers between devices: 169 us -> 178 us
  matrix products: 41.6 us -> 32.8 us
    all_to_all x3 -> x4, starting transfers between devices: 11.7 us -> 34.2 us  [exchange_ctx(): return lax.all_to_all(value, 'ctx', 0, 0)]
    ppermute x58 -> x51, starting transfers between devices: 62.8 us -> 48.7 us  [swap(): return lax.ppermute(value, 'ctx', [(i, i ^ step) for i in range(count)])]
    all_gather x4, waiting for transfers between devices: 7.69 us -> 21.4 us  [gather_seq(): return lax.all_gather(value, 'seq', axis=0, tiled=True)]
    all_to_all x1 -> x0, blocking collectives: 12 us -> none  [exchange_ctx(): return lax.all_to_all(value, 'ctx', 0, 0)]
    ppermute x4, waiting for transfers between devices: 11.4 us -> 0.01 us  [to_owners(): came.append(lax.ppermute(piece, 'ctx', pairs))]
    pallas_call x5 -> x7, Pallas kernels: 61.2 us -> 72.5 us  [by_rows(): pl.pallas_call(kernel, grid=(count // block,), in_specs=specs, out_specs=...]
    all_gather x4, starting transfers between devices: 10.3 us -> 0.16 us  [gather_seq(): return lax.all_gather(value, 'seq', axis=0, tiled=True)]
    dot_general x9 -> x7, matrix products: 41.6 us -> 32.8 us  [dot(): lax.dot_general(left, right, (contract, ((), ())), preferred_element_type...]
  transfers between devices with their start and end apart: 76 -> 70, of which waited for: 35 -> 29; matrix products, arithmetic and copies ran while one was open for 18% -> 17% of each run, Pallas kernels for 22% -> 24%
where the time goes in v4:
time: 558 us; the launch traced here: 548 us
  waiting for transfers between devices  178 us (32%)
  Pallas kernels  136 us (24%)
  starting transfers between devices  97.8 us (18%)
  local copies, waits for them, and re-layouts  43.6 us (8%)
  other arithmetic  42.9 us (8%)
  matrix products  32.8 us (6%)
  between operations  16.1 us (3%)
    ppermute x51, waiting for transfers between devices, swap(): return lax.ppermute(value, 'ctx', [(i, i ^ step) for i in range(count)])  128 us
    pallas_call x7, Pallas kernels, by_rows(): pl.pallas_call(kernel, grid=(count // block,), in_specs=specs, out_specs=...  72.5 us
    ppermute x51, starting transfers between devices, swap(): return lax.ppermute(value, 'ctx', [(i, i ^ step) for i in range(count)])  48.7 us
    all_to_all x4, starting transfers between devices, exchange_ctx(): return lax.all_to_all(value, 'ctx', 0, 0)  34.2 us
    dot_general x7, matrix products, dot(): lax.dot_general(left, right, (contract, ((), ())), preferred_element_type...  32.8 us
    all_gather x4, waiting for transfers between devices, gather_seq(): return lax.all_gather(value, 'seq', axis=0, tiled=True)  21.4 us
    pallas_call x1, Pallas kernels, attention_backward(): pl.pallas_call(functools.partial(backward_kernel, block, heads, count), g...  20.8 us
    unnamed x159, local copies, waits for them, and re-layouts  17.3 us
  transfers between devices with their start and end apart: 70, of which 29 were waited for; matrix products, arithmetic and copies ran while one was open for 17% of the time, Pallas kernels for 24%

profile of v4, /device:TPU:0, one launch (start us, length us, event | category | flops | bytes accessed | tf_op | source)
XLA Modules:
  0.0 547.9 jit_solution(6526365952182375266)
XLA Ops:
  24.0 19.8 %all-to-all-start = ((bf16[8,80,384]{2,1,0:T(8,128)(2,1)}), bf16[8,80,384]{2,1,0:T(8,128)(2,1)S(1)}, u32[]{:S(2)}, u32[]{:S(2)}) async-start(bf16[8,80,384]{2,1,0:T(8,128)(2,1)} %pad_maximum_fusion.2), calls=%async_computation | async-start | bytes 983040 | tf_op jit(solution)/shard_map/all_to_all | solution.py:269
  47.4 6.2 %all-to-all-done = bf16[8,80,384]{2,1,0:T(8,128)(2,1)S(1)} async-done(((bf16[8,80,384]{2,1,0:T(8,128)(2,1)}), bf16[8,80,384]{2,1,0:T(8,128)(2,1)S(1)}, u32[]{:S(2)}, u32[]{:S(2)}) %all-to-all-start) | async-done | bytes 491552 | tf_op jit(solution)/shard_map/all_to_all | solution.py:269
  54.5 8.9 %all-gather.5.cloned.1.call-done = bf16[256,2048]{1,0:T(8,128)(2,1)} async-done(((bf16[64,2048]{1,0:T(8,128)(2,1)}), bf16[256,2048]{1,0:T(8,128)(2,1)}) %all-gather.5.cloned.1.call-update) | async-done | bytes 1048592 | tf_op jit(solution)/shard_map/all_gather | solution.py:261
  77.5 8.4 %collective-permute-done.6 = bf16[1,2,96,2048]{3,2,1,0:T(8,128)(2,1)S(1)} collective-permute-done((bf16[1,2,96,2048]{3,2,1,0:T(8,128)(2,1)}, bf16[1,2,96,2048]{3,2,1,0:T(8,128)(2,1)S(1)}, u32[]{:S(2)}, u32[]{:S(2)}) %collective-permute-start.6) | collective-permute-done | bytes 786464 | tf_op jit(solution)/shard_map/ppermute | solution.py:32
  96.6 5.7 %all-to-all-done.1 = bf16[8,64,1408]{2,1,0:T(8,128)(2,1)} async-done(((bf16[8,64,1408]{2,1,0:T(8,128)(2,1)}), bf16[8,64,1408]{2,1,0:T(8,128)(2,1)}, u32[]{:S(2)}, u32[]{:S(2)}) %all-to-all-start.1) | async-done | bytes 1441824 | tf_op jit(solution)/shard_map/all_to_all | solution.py:269
  108.0 5.8 %fusion.37 = f32[384,1536]{1,0:T(8,128)S(1)} fusion(bf16[2048,384]{1,0:T(8,128)(2,1)} %all-gather.7.cloned.1.call-done.weight_ref, bf16[1536,2048]{1,0:T(8,128)(2,1)} %bitcast.280), kind=kOutput, calls=%fused_computation.164 | convolution fusion | flops 2415919104 | bytes 10223616 | tf_op jit(solution)/shard_map/dot_general | solution.py:24
  118.7 13.7 %attention_forward.1 = (f32[256,1536]{1,0:T(8,128)}, bf16[1536,256]{1,0:T(8,128)(2,1)}, f32[4,1536]{1,0:T(4,128)}) custom-call(bf16[1536,64]{1,0:T(8,128)(2,1)} %copy.125.key_ref, bf16[64,1536]{1,0:T(8,128)(2,1)} %copy.126.value_ref, bf16[256,1536]{1,0:T(8,128)(2,1)} %bitcast.292, s32[1,1536]{1,0:T(1,128)} %reduce_sum.93.start_ref), custom_call_target="tpu_custom_call" | custom-call | tf_op jit(solution)/shard_map/attention_forward/pallas_call | solution.py:474
  132.5 6.1 %collective-permute-done.12 = bf16[192,2048]{1,0:T(8,128)(2,1)S(1)} collective-permute-done((bf16[192,2048]{1,0:T(8,128)(2,1)S(1)}, bf16[192,2048]{1,0:T(8,128)(2,1)S(1)}, u32[]{:S(2)}, u32[]{:S(2)}) %collective-permute-start.12) | collective-permute-done | bytes 786464 | tf_op jit(solution)/shard_map/ppermute | solution.py:32
  141.9 5.8 %collective-permute-done.14 = bf16[768,2048]{1,0:T(8,128)(2,1)} collective-permute-done((bf16[768,2048]{1,0:T(8,128)(2,1)S(1)}, bf16[768,2048]{1,0:T(8,128)(2,1)}, u32[]{:S(2)}, u32[]{:S(2)}) %collective-permute-start.14) | collective-permute-done | bytes 3145760 | tf_op jit(solution)/shard_map/ppermute | solution.py:32
  155.1 17.1 %collective-permute-done.15 = bf16[2,1,96,2048]{3,2,1,0:T(8,128)(2,1)} collective-permute-done((bf16[2,1,96,2048]{3,2,1,0:T(8,128)(2,1)S(1)}, bf16[2,1,96,2048]{3,2,1,0:T(8,128)(2,1)}, u32[]{:S(2)}, u32[]{:S(2)}) %collective-permute-start.15) | collective-permute-done | bytes 786464 | tf_op jit(solution)/shard_map/ppermute | solution.py:32
  177.0 7.0 %collective-permute-done.16 = bf16[1,1,96,2048]{3,2,1,0:T(8,128)(2,1)S(1)} collective-permute-done((bf16[1,1,96,2048]{3,2,1,0:T(8,128)(2,1)S(1)}, bf16[1,1,96,2048]{3,2,1,0:T(8,128)(2,1)S(1)}, u32[]{:S(2)}, u32[]{:S(2)}) %collective-permute-start.16) | collective-permute-done | bytes 393248 | tf_op jit(solution)/shard_map/ppermute | solution.py:32
  191.4 10.0 %collective-permute-done.23 = bf16[96,2048]{1,0:T(8,128)(2,1)S(1)} collective-permute-done((bf16[96,2048]{1,0:T(8,128)(2,1)S(1)}, bf16[96,2048]{1,0:T(8,128)(2,1)S(1)}, u32[]{:S(2)}, u32[]{:S(2)}) %collective-permute-start.23) | collective-permute-done | bytes 393248 | tf_op jit(solution)/shard_map/ppermute | solution.py:32
  205.8 15.8 %collective-permute-done.25 = bf16[1,2,96,2048]{3,2,1,0:T(8,128)(2,1)S(1)} collective-permute-done((bf16[1,2,96,2048]{3,2,1,0:T(8,128)(2,1)S(1)}, bf16[1,2,96,2048]{3,2,1,0:T(8,128)(2,1)S(1)}, u32[]{:S(2)}, u32[]{:S(2)}) %collective-permute-start.25) | collective-permute-done | bytes 786464 | tf_op jit(solution)/shard_map/ppermute | solution.py:32
  231.5 16.4 %hidden_layer.1 = (bf16[1536,704]{1,0:T(8,128)(2,1)}, bf16[1536,704]{1,0:T(8,128)(2,1)}, bf16[1536,704]{1,0:T(8,128)(2,1)}) custom-call(bf16[1536,2048]{1,0:T(8,128)(2,1)} %bitcast.266, bf16[2048,1408]{1,0:T(8,128)(2,1)} %all-gather.9.cloned.1.call-done.weight_ref), custom_call_target="tpu_custom_call" | custom-call | tf_op jit(solution)/shard_map/hidden_layer/pallas_call | solution.py:394
  247.9 7.7 %convolution_convert_fusion.1 = bf16[704,2048]{1,0:T(8,128)(2,1)} fusion(bf16[1536,704]{1,0:T(8,128)(2,1)} %get-tuple-element.128.row_ref, bf16[1536,2048]{1,0:T(8,128)(2,1)S(1)} %bitcast.272), kind=kOutput, calls=%fused_computation.3 | convolution fusion | flops 4430626816 | bytes 11337728 | tf_op jit(solution)/shard_map/dot_general | solution.py:24
  255.7 12.6 %all-gather.11.cloned.1.call-done.down_ref.weight_ref = bf16[704,2048]{1,0:T(8,128)(2,1)} async-done(((bf16[176,2048]{1,0:T(8,128)(2,1)}), bf16[704,2048]{1,0:T(8,128)(2,1)}) %all-gather.11.cloned.1.call-update) | async-done | bytes 2883600 | tf_op jit(solution)/shard_map/all_gather | solution.py:261
  268.3 15.6 %hidden_back_away.1 = (bf16[768,1408]{1,0:T(8,128)(2,1)}, bf16[768,2048]{1,0:T(8,128)(2,1)}) custom-call(bf16[1536,2048]{1,0:T(8,128)(2,1)} %bitcast.270, bf16[704,2048]{1,0:T(8,128)(2,1)} %all-gather.11.cloned.1.call-done.down_ref.weight_ref, bf16[1536,704]{1,0:T(8,128)(2,1)} %get-tuple-element.114.slope_ref, ...), custom_call_target="tpu_custom_call" | custom-call | tf_op jit(solution)/shard_map/hidden_back_away/pallas_call | solution.py:394
  283.9 5.9 %collective-permute-done.31.refs_0_ = bf16[768,2048]{1,0:T(8,128)(2,1)S(1)} collective-permute-done((bf16[768,2048]{1,0:T(8,128)(2,1)}, bf16[768,2048]{1,0:T(8,128)(2,1)S(1)}, u32[]{:S(2)}, u32[]{:S(2)}) %collective-permute-start.31) | collective-permute-done | bytes 3145760 | tf_op jit(solution)/shard_map/ppermute | solution.py:32
  291.5 15.8 %hidden_back_stay.1 = (bf16[768,1408]{1,0:T(8,128)(2,1)}, bf16[768,2048]{1,0:T(8,128)(2,1)}) custom-call(bf16[1536,2048]{1,0:T(8,128)(2,1)} %bitcast.271, bf16[704,2048]{1,0:T(8,128)(2,1)} %all-gather.11.cloned.1.call-done.down_ref.weight_ref, bf16[1536,704]{1,0:T(8,128)(2,1)} %get-tuple-element.114.slope_ref, ...), custom_call_target="tpu_custom_call" | custom-call | tf_op jit(solution)/shard_map/hidden_back_stay/pallas_call | solution.py:394
  314.4 14.5 %outer.1 = bf16[2048,1408]{1,0:T(8,128)(2,1)} custom-call(bf16[1536,2048]{1,0:T(8,128)(2,1)} %bitcast.267, bf16[768,1408]{1,0:T(8,128)(2,1)} %get-tuple-element.122.refs_0_, bf16[768,1408]{1,0:T(8,128)(2,1)} %get-tuple-element.123.refs_1_), custom_call_target="tpu_custom_call" | custom-call | tf_op jit(solution)/shard_map/outer/pallas_call | solution.py:429
  337.6 5.8 %collective-permute-done.33 = bf16[1,1,96,2048]{3,2,1,0:T(8,128)(2,1)S(1)} collective-permute-done((bf16[1,1,96,2048]{3,2,1,0:T(8,128)(2,1)S(1)}, bf16[1,1,96,2048]{3,2,1,0:T(8,128)(2,1)S(1)}, u32[]{:S(2)}, u32[]{:S(2)}) %collective-permute-start.33) | collective-permute-done | bytes 393248 | tf_op jit(solution)/shard_map/ppermute | solution.py:32
  349.8 6.2 %out_away.1 = bf16[768,2048]{1,0:T(8,128)(2,1)} custom-call(bf16[1536,704]{1,0:T(8,128)(2,1)} %get-tuple-element.128.row_ref, bf16[704,2048]{1,0:T(8,128)(2,1)} %all-gather.11.cloned.1.call-done.down_ref.weight_ref), custom_call_target="tpu_custom_call" | custom-call | flops 7000000000 | tf_op jit(solution)/shard_map/out_away/pallas_call | solution.py:394
  357.9 9.6 %collective-permute-done.38 = bf16[96,2048]{1,0:T(8,128)(2,1)S(1)} collective-permute-done((bf16[96,2048]{1,0:T(8,128)(2,1)S(1)}, bf16[96,2048]{1,0:T(8,128)(2,1)S(1)}, u32[]{:S(2)}, u32[]{:S(2)}) %collective-permute-start.38) | collective-permute-done | bytes 393248 | tf_op jit(solution)/shard_map/ppermute | solution.py:32
  372.2 7.2 %out_stay.1 = bf16[768,2048]{1,0:T(8,128)(2,1)} custom-call(bf16[1536,704]{1,0:T(8,128)(2,1)} %get-tuple-element.128.row_ref, bf16[704,2048]{1,0:T(8,128)(2,1)} %all-gather.11.cloned.1.call-done.down_ref.weight_ref, bf16[768,2048]{1,0:T(8,128)(2,1)} %collective-permute-done.40.refs_0_), custom_call_target="tpu_custom_call" | custom-call | flops 7000000000 | tf_op jit(solution)/shard_map/out_stay/pallas_call | solution.py:394
  379.4 7.6 %collective-permute-done.39 = bf16[2,1,96,2048]{3,2,0,1:T(8,128)(2,1)S(1)} collective-permute-done((bf16[2,1,96,2048]{3,2,0,1:T(8,128)(2,1)S(1)}, bf16[2,1,96,2048]{3,2,0,1:T(8,128)(2,1)S(1)}, u32[]{:S(2)}, u32[]{:S(2)}) %collective-permute-start.39) | collective-permute-done | bytes 786464 | tf_op jit(solution)/shard_map/ppermute | solution.py:32
  418.0 6.3 %collective-permute-start.48 = (bf16[1,1,96,2048]{3,2,1,0:T(8,128)(2,1)S(1)}, bf16[1,1,96,2048]{3,2,1,0:T(8,128)(2,1)S(1)}, u32[]{:S(2)}, u32[]{:S(2)}) collective-permute-start(bf16[1,1,96,2048]{3,2,1,0:T(8,128)(2,1)S(1)} %dynamic-slice_convert_fusion.2), channel_id=1, source_target_pairs={{0,2},{1,3},{2,0},{3,1},{4,6},{5,7},{6,4},{7,5},{8,10},{9,11},{10,... | collective-permute-start | bytes 1179656 | tf_op jit(solution)/shard_map/ppermute | solution.py:32
  425.4 6.2 %collective-permute-done.47 = bf16[1,1,96,2048]{3,2,1,0:T(8,128)(2,1)S(1)} collective-permute-done((bf16[1,1,96,2048]{3,2,1,0:T(8,128)(2,1)S(1)}, bf16[1,1,96,2048]{3,2,1,0:T(8,128)(2,1)S(1)}, u32[]{:S(2)}, u32[]{:S(2)}) %collective-permute-start.47) | collective-permute-done | bytes 393248 | tf_op jit(solution)/shard_map/ppermute | solution.py:32
  432.4 6.3 %all-to-all-start.2 = ((bf16[8,64,1408]{2,1,0:T(8,128)(2,1)}), bf16[8,64,1408]{2,1,0:T(8,128)(2,1)S(1)}, u32[]{:S(2)}, u32[]{:S(2)}) async-start(bf16[8,64,1408]{2,1,0:T(8,128)(2,1)} %bitcast.314), calls=%async_computation.4 | async-start | bytes 2883584 | tf_op jit(solution)/shard_map/all_to_all | solution.py:269
  438.8 20.8 %attention_backward.1 = (f32[256,1536]{1,0:T(8,128)}, f32[64,1536]{1,0:T(8,128)}, f32[64,1536]{1,0:T(8,128)}) custom-call(bf16[1536,64]{1,0:T(8,128)(2,1)} %copy.125.key_ref, bf16[64,1536]{1,0:T(8,128)(2,1)} %bitcast.321, bf16[1536,64]{1,0:T(8,128)(2,1)} %bitcast.300, bf16[256,1536]{1,0:T(8,128)(2,1)} %bitcast.293, ...), custom_call_target="tpu_custom_call" | custom-call | flops 24999999488 | tf_op jit(solution)/shard_map/attention_backward/pallas_call | solution.py:562
  472.0 7.4 %convolution_convert_fusion.2 = bf16[2048,384]{1,0:T(8,128)(2,1)} fusion(bf16[1536,2048]{1,0:T(8,128)(2,1)} %bitcast.281, bf16[384,1536]{1,0:T(8,128)(2,1)S(1)} %pad_maximum_fusion), kind=kOutput, calls=%fused_computation.4 | convolution fusion | flops 2416705536 | bytes 9043968 | tf_op jit(solution)/shard_map/dot_general | solution.py:24
  479.6 6.2 %mixed_stay.1 = bf16[768,2048]{1,0:T(8,128)(2,1)} custom-call(bf16[768,384]{1,0:T(8,128)(2,1)} %bitcast.296, bf16[2048,384]{1,0:T(8,128)(2,1)} %all-gather.7.cloned.1.call-done.weight_ref, bf16[768,2048]{1,0:T(8,128)(2,1)} %collective-permute-done.53.refs_0_), custom_call_target="tpu_custom_call" | custom-call | tf_op jit(solution)/shard_map/mixed_stay/pallas_call | solution.py:394
  499.7 13.8 %reduce-scatter.11.cloned.1.call-done = bf16[512,384]{1,0:T(8,128)(2,1)} async-done(((bf16[2048,384]{1,0:T(8,128)(2,1)}), bf16[512,384]{1,0:T(8,128)(2,1)}) %reduce-scatter.11.cloned.1.call-update) | async-done | bytes 393232 | tf_op jit(solution)/shard_map/reduce_scatter | solution.py:265
  (437 shorter events, 209.5 us)
Async XLA Ops:
  7.2 56.2 %all-gather.5.cloned.1.call-start = ((), (), s32[]{:S(2)}) async-start(), calls=%async_computation.8 | async-start | bytes 1310720 | tf_op jit(solution)/shard_map/all_gather | solution.py:261
  24.0 29.6 %all-to-all-start = ((bf16[8,80,384]{2,1,0:T(8,128)(2,1)}), bf16[8,80,384]{2,1,0:T(8,128)(2,1)S(1)}, u32[]{:S(2)}, u32[]{:S(2)}) async-start(bf16[8,80,384]{2,1,0:T(8,128)(2,1)} %pad_maximum_fusion.2), calls=%async_computation | async-start | bytes 983040 | tf_op jit(solution)/shard_map/all_to_all | solution.py:269
  43.8 64.2 %all-gather.7.cloned.1.call-start = ((), (), s32[]{:S(2)}) async-start(), calls=%async_computation.9 | async-start | bytes 1966080 | tf_op jit(solution)/shard_map/all_gather | solution.py:261
  43.9 19.5 %collective-permute-start.4 = (bf16[96,2048]{1,0:T(8,128)(2,1)S(1)}, bf16[96,2048]{1,0:T(8,128)(2,1)S(1)}, u32[]{:S(2)}, u32[]{:S(2)}) collective-permute-start(bf16[96,2048]{1,0:T(8,128)(2,1)S(1)} %get-tuple-element.91), channel_id=1, source_target_pairs={{0,4},{1,5},{2,6},{3,7},{4,0},{5,1},{6,2},{7,3},{8,12},{9,13},{10,... | collective-permute-start | bytes 1179656 | tf_op jit(solution)/shard_map/ppermute | solution.py:32
  65.3 20.7 %collective-permute-start.6 = (bf16[1,2,96,2048]{3,2,1,0:T(8,128)(2,1)}, bf16[1,2,96,2048]{3,2,1,0:T(8,128)(2,1)S(1)}, u32[]{:S(2)}, u32[]{:S(2)}) collective-permute-start(bf16[1,2,96,2048]{3,2,1,0:T(8,128)(2,1)} %maximum_select_fusion.1), channel_id=1, source_target_pairs={{0,4},{1,5},{2,6},{3,7},{4,0},{5,1},{6,2},{7,3},{8,12},{9,13},{10,... | collective-permute-start | bytes 2359304 | tf_op jit(solution)/shard_map/ppermute | solution.py:32
  67.8 20.7 %collective-permute-start.9 = (bf16[2,1,96,2048]{3,2,1,0:T(8,128)(2,1)}, bf16[2,1,96,2048]{3,2,1,0:T(8,128)(2,1)S(1)}, u32[]{:S(2)}, u32[]{:S(2)}) collective-permute-start(bf16[2,1,96,2048]{3,2,1,0:T(8,128)(2,1)} %maximum_select_fusion.3), channel_id=1, source_target_pairs={{0,2},{1,3},{2,0},{3,1},{4,6},{5,7},{6,4},{7,5},{8,10},{9,11},{10,... | collective-permute-start | bytes 2359304 | tf_op jit(solution)/shard_map/ppermute | solution.py:32
  69.7 22.4 %collective-permute-start.5 = (bf16[1,2,96,2048]{3,2,1,0:T(8,128)(2,1)}, bf16[1,2,96,2048]{3,2,1,0:T(8,128)(2,1)}, u32[]{:S(2)}, u32[]{:S(2)}) collective-permute-start(bf16[1,2,96,2048]{3,2,1,0:T(8,128)(2,1)} %maximum_select_fusion.1), channel_id=1, source_target_pairs={{0,1},{1,0},{2,3},{3,2},{4,5},{5,4},{6,7},{7,6},{8,9},{9,8},{10,11... | collective-permute-start | bytes 2359304 | tf_op jit(solution)/shard_map/ppermute | solution.py:32
  69.7 22.4 %collective-permute-start.8 = (bf16[2,1,96,2048]{3,2,1,0:T(8,128)(2,1)}, bf16[2,1,96,2048]{3,2,1,0:T(8,128)(2,1)}, u32[]{:S(2)}, u32[]{:S(2)}) collective-permute-start(bf16[2,1,96,2048]{3,2,1,0:T(8,128)(2,1)} %maximum_select_fusion.3), channel_id=1, source_target_pairs={{0,1},{1,0},{2,3},{3,2},{4,5},{5,4},{6,7},{7,6},{8,9},{9,8},{10,11... | collective-permute-start | bytes 2359304 | tf_op jit(solution)/shard_map/ppermute | solution.py:32
  72.1 30.3 %all-to-all-start.1 = ((bf16[8,64,1408]{2,1,0:T(8,128)(2,1)}), bf16[8,64,1408]{2,1,0:T(8,128)(2,1)}, u32[]{:S(2)}, u32[]{:S(2)}) async-start(bf16[8,64,1408]{2,1,0:T(8,128)(2,1)} %split_units.1), calls=%async_computation.1 | async-start | bytes 2883584 | tf_op jit(solution)/shard_map/all_to_all | solution.py:269
  76.5 154.9 %all-gather.9.cloned.1.call-start = ((), (), s32[]{:S(2)}) async-start(), calls=%async_computation.10 | async-start | bytes 7208960 | tf_op jit(solution)/shard_map/all_gather | solution.py:261
  102.4 165.9 %all-gather.11.cloned.1.call-start = ((), (), s32[]{:S(2)}) async-start(), calls=%async_computation.11 | async-start | bytes 3604480 | tf_op jit(solution)/shard_map/all_gather | solution.py:261
  104.5 28.0 %collective-permute-start.13 = (bf16[192,2048]{1,0:T(8,128)(2,1)S(1)}, bf16[192,2048]{1,0:T(8,128)(2,1)S(1)}, u32[]{:S(2)}, u32[]{:S(2)}) collective-permute-start(bf16[192,2048]{1,0:T(8,128)(2,1)S(1)} %copy-done.17), channel_id=1, source_target_pairs={{0,6},{1,7},{2,4},{3,5},{4,2},{5,3},{6,0},{7,1},{8,14},{9,15},{10,... | collective-permute-start | bytes 2359304 | tf_op jit(solution)/shard_map/ppermute | solution.py:32
  106.0 32.6 %collective-permute-start.12 = (bf16[192,2048]{1,0:T(8,128)(2,1)S(1)}, bf16[192,2048]{1,0:T(8,128)(2,1)S(1)}, u32[]{:S(2)}, u32[]{:S(2)}) collective-permute-start(bf16[192,2048]{1,0:T(8,128)(2,1)S(1)} %copy-done.17), channel_id=1, source_target_pairs={{0,4},{1,5},{2,6},{3,7},{4,0},{5,1},{6,2},{7,3},{8,12},{9,13},{10,... | collective-permute-start | bytes 2359304 | tf_op jit(solution)/shard_map/ppermute | solution.py:32
  107.5 31.1 %collective-permute-start.11 = (bf16[192,2048]{1,0:T(8,128)(2,1)S(1)}, bf16[192,2048]{1,0:T(8,128)(2,1)}, u32[]{:S(2)}, u32[]{:S(2)}) collective-permute-start(bf16[192,2048]{1,0:T(8,128)(2,1)S(1)} %copy-done.17), channel_id=1, source_target_pairs={{0,2},{1,3},{2,0},{3,1},{4,6},{5,7},{6,4},{7,5},{8,10},{9,11},{10,... | collective-permute-start | bytes 2359304 | tf_op jit(solution)/shard_map/ppermute | solution.py:32
  152.5 19.7 %collective-permute-start.15 = (bf16[2,1,96,2048]{3,2,1,0:T(8,128)(2,1)S(1)}, bf16[2,1,96,2048]{3,2,1,0:T(8,128)(2,1)}, u32[]{:S(2)}, u32[]{:S(2)}) collective-permute-start(bf16[2,1,96,2048]{3,2,1,0:T(8,128)(2,1)S(1)} %dynamic-slice_bitcast_fusion.7), channel_id=1, source_target_pairs={{0,2},{1,3},{2,0},{3,1},{4,6},{5,7},{6,4},{7,5},{8,10},{9,11},{10,... | collective-permute-start | bytes 2359304 | tf_op jit(solution)/shard_map/ppermute | solution.py:32
  153.7 21.2 %collective-permute-start.17 = (bf16[1,2,96,2048]{3,2,1,0:T(8,128)(2,1)S(1)}, bf16[1,2,96,2048]{3,2,1,0:T(8,128)(2,1)}, u32[]{:S(2)}, u32[]{:S(2)}) collective-permute-start(bf16[1,2,96,2048]{3,2,1,0:T(8,128)(2,1)S(1)} %dynamic-slice_bitcast_fusion.6), channel_id=1, source_target_pairs={{0,4},{1,5},{2,6},{3,7},{4,0},{5,1},{6,2},{7,3},{8,12},{9,13},{10,... | collective-permute-start | bytes 2359304 | tf_op jit(solution)/shard_map/ppermute | solution.py:32
  155.0 214.8 %reduce-scatter.7.cloned.1.call-start = ((), (), s32[]{:S(2)}) async-start(), calls=%async_computation.13 | async-start | bytes 3604480 | tf_op jit(solution)/shard_map/reduce_scatter | solution.py:265
  201.4 23.3 %collective-permute-start.22 = (bf16[192,2048]{1,0:T(8,128)(2,1)S(1)}, bf16[192,2048]{1,0:T(8,128)(2,1)S(1)}, u32[]{:S(2)}, u32[]{:S(2)}) collective-permute-start(bf16[192,2048]{1,0:T(8,128)(2,1)S(1)} %copy-done.52), channel_id=1, source_target_pairs={{0,1},{1,0},{2,3},{3,2},{4,5},{5,4},{6,7},{7,6},{8,9},{9,8},{10,11... | collective-permute-start | bytes 2359304 | tf_op jit(solution)/shard_map/ppermute | solution.py:32
  201.6 20.0 %collective-permute-start.25 = (bf16[1,2,96,2048]{3,2,1,0:T(8,128)(2,1)S(1)}, bf16[1,2,96,2048]{3,2,1,0:T(8,128)(2,1)S(1)}, u32[]{:S(2)}, u32[]{:S(2)}) collective-permute-start(bf16[1,2,96,2048]{3,2,1,0:T(8,128)(2,1)S(1)} %maximum_select_fusion.5), channel_id=1, source_target_pairs={{0,4},{1,5},{2,6},{3,7},{4,0},{5,1},{6,2},{7,3},{8,12},{9,13},{10,... | collective-permute-start | bytes 2359304 | tf_op jit(solution)/shard_map/ppermute | solution.py:32
  203.2 21.6 %collective-permute-start.24 = (bf16[1,2,96,2048]{3,2,1,0:T(8,128)(2,1)S(1)}, bf16[1,2,96,2048]{3,2,1,0:T(8,128)(2,1)S(1)}, u32[]{:S(2)}, u32[]{:S(2)}) collective-permute-start(bf16[1,2,96,2048]{3,2,1,0:T(8,128)(2,1)S(1)} %maximum_select_fusion.5), channel_id=1, source_target_pairs={{0,1},{1,0},{2,3},{3,2},{4,5},{5,4},{6,7},{7,6},{8,9},{9,8},{10,11... | collective-permute-start | bytes 2359304 | tf_op jit(solution)/shard_map/ppermute | solution.py:32
  204.8 19.8 %collective-permute-start.29 = (bf16[2,1,96,2048]{3,2,1,0:T(8,128)(2,1)S(1)}, bf16[2,1,96,2048]{3,2,1,0:T(8,128)(2,1)S(1)}, u32[]{:S(2)}, u32[]{:S(2)}) collective-permute-start(bf16[2,1,96,2048]{3,2,1,0:T(8,128)(2,1)S(1)} %maximum_select_fusion.7), channel_id=1, source_target_pairs={{0,2},{1,3},{2,0},{3,1},{4,6},{5,7},{6,4},{7,5},{8,10},{9,11},{10,... | collective-permute-start | bytes 2359304 | tf_op jit(solution)/shard_map/ppermute | solution.py:32
  255.7 176.0 %reduce-scatter.5.cloned.1.call-start = ((), (), s32[]{:S(2)}) async-start(), calls=%async_computation.12 | async-start | bytes 7208960 | tf_op jit(solution)/shard_map/reduce_scatter | solution.py:265
  311.5 19.9 %collective-permute-start.32 = (bf16[2,1,96,2048]{3,2,1,0:T(8,128)(2,1)}, bf16[2,1,96,2048]{3,2,1,0:T(8,128)(2,1)}, u32[]{:S(2)}, u32[]{:S(2)}) collective-permute-start(bf16[2,1,96,2048]{3,2,1,0:T(8,128)(2,1)} %dynamic-slice_bitcast_fusion.5), channel_id=1, source_target_pairs={{0,2},{1,3},{2,0},{3,1},{4,6},{5,7},{6,4},{7,5},{8,10},{9,11},{10,... | collective-permute-start | bytes 2359304 | tf_op jit(solution)/shard_map/ppermute | solution.py:32
  312.9 21.6 %collective-permute-start.34 = (bf16[1,2,96,2048]{3,2,1,0:T(8,128)(2,1)S(1)}, bf16[1,2,96,2048]{3,2,1,0:T(8,128)(2,1)}, u32[]{:S(2)}, u32[]{:S(2)}) collective-permute-start(bf16[1,2,96,2048]{3,2,1,0:T(8,128)(2,1)S(1)} %dynamic-slice_bitcast_fusion.4), channel_id=1, source_target_pairs={{0,4},{1,5},{2,6},{3,7},{4,0},{5,1},{6,2},{7,3},{8,12},{9,13},{10,... | collective-permute-start | bytes 2359304 | tf_op jit(solution)/shard_map/ppermute | solution.py:32
  328.9 133.7 %reduce-scatter.9.cloned.1.call-start = ((), (), s32[]{:S(2)}) async-start(), calls=%async_computation.14 | async-start | bytes 1310720 | tf_op jit(solution)/shard_map/reduce_scatter | solution.py:265
  367.6 19.3 %collective-permute-start.39 = (bf16[2,1,96,2048]{3,2,0,1:T(8,128)(2,1)S(1)}, bf16[2,1,96,2048]{3,2,0,1:T(8,128)(2,1)S(1)}, u32[]{:S(2)}, u32[]{:S(2)}) collective-permute-start(bf16[2,1,96,2048]{3,2,0,1:T(8,128)(2,1)S(1)} %bitcast_select_fusion), channel_id=1, source_target_pairs={{0,2},{1,3},{2,0},{3,1},{4,6},{5,7},{6,4},{7,5},{8,10},{9,11},{10,... | collective-permute-start | bytes 2359304 | tf_op jit(solution)/shard_map/ppermute | solution.py:32
  392.2 19.8 %collective-permute-start.45 = (bf16[2,1,96,2048]{3,2,1,0:T(8,128)(2,1)S(1)}, bf16[2,1,96,2048]{3,2,1,0:T(8,128)(2,1)S(1)}, u32[]{:S(2)}, u32[]{:S(2)}) collective-permute-start(bf16[2,1,96,2048]{3,2,1,0:T(8,128)(2,1)S(1)} %get-tuple-element.135), channel_id=1, source_target_pairs={{0,2},{1,3},{2,0},{3,1},{4,6},{5,7},{6,4},{7,5},{8,10},{9,11},{10,... | collective-permute-start | bytes 2359304 | tf_op jit(solution)/shard_map/ppermute | solution.py:32
  392.9 19.8 %collective-permute-start.46 = (bf16[1,2,96,2048]{3,2,1,0:T(8,128)(2,1)S(1)}, bf16[1,2,96,2048]{3,2,1,0:T(8,128)(2,1)S(1)}, u32[]{:S(2)}, u32[]{:S(2)}) collective-permute-start(bf16[1,2,96,2048]{3,2,1,0:T(8,128)(2,1)S(1)} %get-tuple-element.136), channel_id=1, source_target_pairs={{0,4},{1,5},{2,6},{3,7},{4,0},{5,1},{6,2},{7,3},{8,12},{9,13},{10,... | collective-permute-start | bytes 2359304 | tf_op jit(solution)/shard_map/ppermute | solution.py:32
  432.4 30.2 %all-to-all-start.2 = ((bf16[8,64,1408]{2,1,0:T(8,128)(2,1)}), bf16[8,64,1408]{2,1,0:T(8,128)(2,1)S(1)}, u32[]{:S(2)}, u32[]{:S(2)}) async-start(bf16[8,64,1408]{2,1,0:T(8,128)(2,1)} %bitcast.314), calls=%async_computation.4 | async-start | bytes 2883584 | tf_op jit(solution)/shard_map/all_to_all | solution.py:269
  438.8 74.8 %reduce-scatter.11.cloned.1.call-start = ((), (), s32[]{:S(2)}) async-start(), calls=%async_computation.15 | async-start | bytes 1966080 | tf_op jit(solution)/shard_map/reduce_scatter | solution.py:265
  490.8 22.8 %collective-permute-start.54 = (bf16[2,1,96,2048]{3,2,1,0:T(8,128)(2,1)}, bf16[2,1,96,2048]{3,2,1,0:T(8,128)(2,1)}, u32[]{:S(2)}, u32[]{:S(2)}) collective-permute-start(bf16[2,1,96,2048]{3,2,1,0:T(8,128)(2,1)} %get-tuple-element.152), channel_id=1, source_target_pairs={{0,2},{1,3},{2,0},{3,1},{4,6},{5,7},{6,4},{7,5},{8,10},{9,11},{10,... | collective-permute-start | bytes 2359304 | tf_op jit(solution)/shard_map/ppermute | solution.py:32
  492.5 21.0 %collective-permute-start.55 = (bf16[1,2,96,2048]{3,2,1,0:T(8,128)(2,1)}, bf16[1,2,96,2048]{3,2,1,0:T(8,128)(2,1)}, u32[]{:S(2)}, u32[]{:S(2)}) collective-permute-start(bf16[1,2,96,2048]{3,2,1,0:T(8,128)(2,1)} %get-tuple-element.153), channel_id=1, source_target_pairs={{0,4},{1,5},{2,6},{3,7},{4,0},{5,1},{6,2},{7,3},{8,12},{9,13},{10,... | collective-permute-start | bytes 2359304 | tf_op jit(solution)/shard_map/ppermute | solution.py:32
  (116 other events, 1035.4 us)
Sparse Core Ops, SparseCore 0:
  19.6 43.7 all-gather.4
  65.5 36.5 all-gather.6
  103.7 105.5 all-gather.8
  210.7 57.4 all-gather.10
  270.4 54.8 reduce-scatter.6
  329.0 100.5 reduce-scatter.4
  432.5 27.6 reduce-scatter.8
  479.6 33.8 reduce-scatter.10

commit v5 on v4

--- a/solution.py
+++ b/solution.py
@@ -238,19 +238,21 @@
     return first, beside
 
 
-def scatter_rest(first):
+def scatter_rest(first, beside=None):
     count = lax.axis_size("ctx")
     bits = chip_bits()
-    last = []
-    sums = []
+    kept, last = [], []
     for which, (stay, arrived) in enumerate(first):
         for at in range(1, len(bits)):
             at = len(bits) - 1 - at if which else at
             stay, away = scatter_parts(stay + arrived.astype(f32), at)
             arrived = swap(away, bits[at][0], count)
+        kept.append(stay)
         last.append(arrived)
-        sums.append(stay + arrived.astype(f32))
-    return jnp.concatenate([part.reshape(part.shape[-2:]) for part in sums]), last
+    if beside is not None:
+        last, beside = lax.optimization_barrier((last, beside))
+    sums = [stay + arrived.astype(f32) for stay, arrived in zip(kept, last)]
+    return jnp.concatenate([part.reshape(part.shape[-2:]) for part in sums]), last, beside
 
 
 def scatter_pairs(pairs):
@@ -710,7 +712,7 @@
     two_pairs = blocks_of(two_pairs)
     grad_down = scatter_seq(grad_down).astype(f32)
     two_first, back_stay = scatter_first(two_pairs, back_stay)
-    shaped_two, _ = scatter_rest(two_first)
+    shaped_two = scatter_rest(two_first)[0]
     shaped_two = shaped_two * gain_two_row
     grad_pair = outer(normed_two_all, [back_stay, back_away])
     shaped_two = after(shaped_two, grad_pair)
@@ -733,7 +735,7 @@
     grad_proj = dot(out_low, branch_all, ((0,), (0,)), bf16)
     grad_out_t = after(dot(proj_wide, branch_all, columns_by, bf16), grad_proj)
     grad_out_t, out_first = lax.optimization_barrier((grad_out_t, out_first))
-    out_sum, out_last = scatter_rest(out_first)
+    out_sum, out_last, _ = scatter_rest(out_first)
     grad_out_t = after(grad_out_t, *out_last)
     grad_out_t = after(grad_out_t, grad_pair)
     grad_proj, came = to_owners(grad_proj)
@@ -763,10 +765,8 @@
     shaped_one = blocks_of(product(parts, mix_wide, columns_by, None, "mixed_stay", LIGHT))
     grad_gate, grad_up, grad_feedforward = join_units(grad_pair, gate_weight, up_weight, units)
     shaped_first, _ = scatter_first(shaped_one)
-    shaped_first, grad_mix = lax.optimization_barrier(
-        (shaped_first, grad_mix, grad_gate)
-    )[:2]
-    shaped_one, arrived = scatter_rest(shaped_first)
+    shaped_first = lax.optimization_barrier((shaped_first, grad_gate))[0]
+    shaped_one, _, grad_mix = scatter_rest(shaped_first, grad_mix)
     shaped_one = shaped_one * gain_one_row
     mean_one = jnp.mean(shaped_one * inputs, axis=-1, keepdims=True)
     grad_tokens = (

time: 558 us -> 564 us (1.011)
    ppermute x51, waiting for transfers between devices: 128 us -> 144 us  [swap(): return lax.ppermute(value, 'ctx', [(i, i ^ step) for i in range(count)])]
    reduce_scatter x4, waiting for transfers between devices: 13.9 us -> 0.04 us  [scatter_seq(): return lax.psum_scatter(value, 'seq', scatter_dimension=0, tiled=True)]
    unnamed x159 -> x151, local copies, waits for them, and re-layouts: 17.3 us -> 16.4 us
  transfers between devices with their start and end apart: 70 -> 70, of which waited for: 29 -> 31; matrix products, arithmetic and copies ran while one was open for 17% -> 17% of each run, Pallas kernels for 24% -> 24%
where the time goes in v5:
time: 564 us; the launch traced here: 554 us
  waiting for transfers between devices  183 us (32%)
  Pallas kernels  136 us (24%)
  starting transfers between devices  96.2 us (17%)
  other arithmetic  47.9 us (8%)
  local copies, waits for them, and re-layouts  41.9 us (7%)
  matrix products  32.8 us (6%)
  between operations  16 us (3%)
    ppermute x51, waiting for transfers between devices, swap(): return lax.ppermute(value, 'ctx', [(i, i ^ step) for i in range(count)])  144 us
    pallas_call x7, Pallas kernels, by_rows(): pl.pallas_call(kernel, grid=(count // block,), in_specs=specs, out_specs=...  72.5 us
    ppermute x51, starting transfers between devices, swap(): return lax.ppermute(value, 'ctx', [(i, i ^ step) for i in range(count)])  46.5 us
    all_to_all x4, starting transfers between devices, exchange_ctx(): return lax.all_to_all(value, 'ctx', 0, 0)  34.8 us
    dot_general x7, matrix products, dot(): lax.dot_general(left, right, (contract, ((), ())), preferred_element_type...  32.8 us
    all_gather x4, waiting for transfers between devices, gather_seq(): return lax.all_gather(value, 'seq', axis=0, tiled=True)  21.5 us
    pallas_call x1, Pallas kernels, attention_backward(): pl.pallas_call(functools.partial(backward_kernel, block, heads, count), g...  20.8 us
    unnamed x151, local copies, waits for them, and re-layouts  16.4 us
  transfers between devices with their start and end apart: 70, of which 31 were waited for; matrix products, arithmetic and copies ran while one was open for 17% of the time, Pallas kernels for 24%

profile of v5, /device:TPU:0, one launch (start us, length us, event | category | flops | bytes accessed | tf_op | source)
XLA Modules:
  0.0 553.9 jit_solution(9820884657579699491)
XLA Ops:
  24.0 19.8 %all-to-all-start = ((bf16[8,80,384]{2,1,0:T(8,128)(2,1)}), bf16[8,80,384]{2,1,0:T(8,128)(2,1)S(1)}, u32[]{:S(2)}, u32[]{:S(2)}) async-start(bf16[8,80,384]{2,1,0:T(8,128)(2,1)} %pad_maximum_fusion.2), calls=%async_computation | async-start | bytes 983040 | tf_op jit(solution)/shard_map/all_to_all | solution.py:271
  47.4 6.2 %all-to-all-done = bf16[8,80,384]{2,1,0:T(8,128)(2,1)S(1)} async-done(((bf16[8,80,384]{2,1,0:T(8,128)(2,1)}), bf16[8,80,384]{2,1,0:T(8,128)(2,1)S(1)}, u32[]{:S(2)}, u32[]{:S(2)}) %all-to-all-start) | async-done | bytes 491552 | tf_op jit(solution)/shard_map/all_to_all | solution.py:271
  54.5 8.9 %all-gather.5.cloned.1.call-done = bf16[256,2048]{1,0:T(8,128)(2,1)} async-done(((bf16[64,2048]{1,0:T(8,128)(2,1)}), bf16[256,2048]{1,0:T(8,128)(2,1)}) %all-gather.5.cloned.1.call-update) | async-done | bytes 1048592 | tf_op jit(solution)/shard_map/all_gather | solution.py:263
  77.1 8.8 %collective-permute-done.6 = bf16[1,2,96,2048]{3,2,1,0:T(8,128)(2,1)S(1)} collective-permute-done((bf16[1,2,96,2048]{3,2,1,0:T(8,128)(2,1)}, bf16[1,2,96,2048]{3,2,1,0:T(8,128)(2,1)S(1)}, u32[]{:S(2)}, u32[]{:S(2)}) %collective-permute-start.6) | collective-permute-done | bytes 786464 | tf_op jit(solution)/shard_map/ppermute | solution.py:32
  96.6 5.7 %all-to-all-done.1 = bf16[8,64,1408]{2,1,0:T(8,128)(2,1)} async-done(((bf16[8,64,1408]{2,1,0:T(8,128)(2,1)}), bf16[8,64,1408]{2,1,0:T(8,128)(2,1)}, u32[]{:S(2)}, u32[]{:S(2)}) %all-to-all-start.1) | async-done | bytes 1441824 | tf_op jit(solution)/shard_map/all_to_all | solution.py:271
  108.0 5.8 %fusion.37 = f32[384,1536]{1,0:T(8,128)S(1)} fusion(bf16[2048,384]{1,0:T(8,128)(2,1)} %all-gather.7.cloned.1.call-done.weight_ref, bf16[1536,2048]{1,0:T(8,128)(2,1)} %bitcast.280), kind=kOutput, calls=%fused_computation.164 | convolution fusion | flops 2415919104 | bytes 10223616 | tf_op jit(solution)/shard_map/dot_general | solution.py:24
  118.0 13.7 %attention_forward.1 = (f32[256,1536]{1,0:T(8,128)}, bf16[1536,256]{1,0:T(8,128)(2,1)}, f32[4,1536]{1,0:T(4,128)}) custom-call(bf16[1536,64]{1,0:T(8,128)(2,1)} %copy.125.key_ref, bf16[64,1536]{1,0:T(8,128)(2,1)} %copy.126.value_ref, bf16[256,1536]{1,0:T(8,128)(2,1)} %bitcast.292, s32[1,1536]{1,0:T(1,128)} %reduce_sum.93.start_ref), custom_call_target="tpu_custom_call" | custom-call | tf_op jit(solution)/shard_map/attention_forward/pallas_call | solution.py:476
  131.8 6.8 %collective-permute-done.12 = bf16[192,2048]{1,0:T(8,128)(2,1)S(1)} collective-permute-done((bf16[192,2048]{1,0:T(8,128)(2,1)S(1)}, bf16[192,2048]{1,0:T(8,128)(2,1)S(1)}, u32[]{:S(2)}, u32[]{:S(2)}) %collective-permute-start.12) | collective-permute-done | bytes 786464 | tf_op jit(solution)/shard_map/ppermute | solution.py:32
  141.9 5.8 %collective-permute-done.14 = bf16[768,2048]{1,0:T(8,128)(2,1)} collective-permute-done((bf16[768,2048]{1,0:T(8,128)(2,1)S(1)}, bf16[768,2048]{1,0:T(8,128)(2,1)}, u32[]{:S(2)}, u32[]{:S(2)}) %collective-permute-start.14) | collective-permute-done | bytes 3145760 | tf_op jit(solution)/shard_map/ppermute | solution.py:32
  155.1 17.1 %collective-permute-done.15 = bf16[2,1,96,2048]{3,2,1,0:T(8,128)(2,1)} collective-permute-done((bf16[2,1,96,2048]{3,2,1,0:T(8,128)(2,1)S(1)}, bf16[2,1,96,2048]{3,2,1,0:T(8,128)(2,1)}, u32[]{:S(2)}, u32[]{:S(2)}) %collective-permute-start.15) | collective-permute-done | bytes 786464 | tf_op jit(solution)/shard_map/ppermute | solution.py:32
  176.9 7.0 %collective-permute-done.16 = bf16[1,1,96,2048]{3,2,1,0:T(8,128)(2,1)S(1)} collective-permute-done((bf16[1,1,96,2048]{3,2,1,0:T(8,128)(2,1)S(1)}, bf16[1,1,96,2048]{3,2,1,0:T(8,128)(2,1)S(1)}, u32[]{:S(2)}, u32[]{:S(2)}) %collective-permute-start.16) | collective-permute-done | bytes 393248 | tf_op jit(solution)/shard_map/ppermute | solution.py:32
  191.4 10.0 %collective-permute-done.23 = bf16[96,2048]{1,0:T(8,128)(2,1)S(1)} collective-permute-done((bf16[96,2048]{1,0:T(8,128)(2,1)S(1)}, bf16[96,2048]{1,0:T(8,128)(2,1)S(1)}, u32[]{:S(2)}, u32[]{:S(2)}) %collective-permute-start.23) | collective-permute-done | bytes 393248 | tf_op jit(solution)/shard_map/ppermute | solution.py:32
  205.7 15.8 %collective-permute-done.25 = bf16[1,2,96,2048]{3,2,1,0:T(8,128)(2,1)S(1)} collective-permute-done((bf16[1,2,96,2048]{3,2,1,0:T(8,128)(2,1)S(1)}, bf16[1,2,96,2048]{3,2,1,0:T(8,128)(2,1)S(1)}, u32[]{:S(2)}, u32[]{:S(2)}) %collective-permute-start.25) | collective-permute-done | bytes 786464 | tf_op jit(solution)/shard_map/ppermute | solution.py:32
  231.4 16.4 %hidden_layer.1 = (bf16[1536,704]{1,0:T(8,128)(2,1)}, bf16[1536,704]{1,0:T(8,128)(2,1)}, bf16[1536,704]{1,0:T(8,128)(2,1)}) custom-call(bf16[1536,2048]{1,0:T(8,128)(2,1)} %bitcast.266, bf16[2048,1408]{1,0:T(8,128)(2,1)} %all-gather.9.cloned.1.call-done.weight_ref), custom_call_target="tpu_custom_call" | custom-call | tf_op jit(solution)/shard_map/hidden_layer/pallas_call | solution.py:396
  247.9 7.7 %convolution_convert_fusion.1 = bf16[704,2048]{1,0:T(8,128)(2,1)} fusion(bf16[1536,704]{1,0:T(8,128)(2,1)} %get-tuple-element.130.row_ref, bf16[1536,2048]{1,0:T(8,128)(2,1)S(1)} %bitcast.272), kind=kOutput, calls=%fused_computation.3 | convolution fusion | flops 4430626816 | bytes 11337728 | tf_op jit(solution)/shard_map/dot_general | solution.py:24
  255.7 12.6 %all-gather.11.cloned.1.call-done.down_ref.weight_ref = bf16[704,2048]{1,0:T(8,128)(2,1)} async-done(((bf16[176,2048]{1,0:T(8,128)(2,1)}), bf16[704,2048]{1,0:T(8,128)(2,1)}) %all-gather.11.cloned.1.call-update) | async-done | bytes 2883600 | tf_op jit(solution)/shard_map/all_gather | solution.py:263
  268.2 15.6 %hidden_back_away.1 = (bf16[768,1408]{1,0:T(8,128)(2,1)}, bf16[768,2048]{1,0:T(8,128)(2,1)}) custom-call(bf16[1536,2048]{1,0:T(8,128)(2,1)} %bitcast.270, bf16[704,2048]{1,0:T(8,128)(2,1)} %all-gather.11.cloned.1.call-done.down_ref.weight_ref, bf16[1536,704]{1,0:T(8,128)(2,1)} %get-tuple-element.116.slope_ref, ...), custom_call_target="tpu_custom_call" | custom-call | tf_op jit(solution)/shard_map/hidden_back_away/pallas_call | solution.py:396
  283.9 5.9 %collective-permute-done.31.refs_0_ = bf16[768,2048]{1,0:T(8,128)(2,1)S(1)} collective-permute-done((bf16[768,2048]{1,0:T(8,128)(2,1)}, bf16[768,2048]{1,0:T(8,128)(2,1)S(1)}, u32[]{:S(2)}, u32[]{:S(2)}) %collective-permute-start.31) | collective-permute-done | bytes 3145760 | tf_op jit(solution)/shard_map/ppermute | solution.py:32
  291.5 15.7 %hidden_back_stay.1 = (bf16[768,1408]{1,0:T(8,128)(2,1)}, bf16[768,2048]{1,0:T(8,128)(2,1)}) custom-call(bf16[1536,2048]{1,0:T(8,128)(2,1)} %bitcast.271, bf16[704,2048]{1,0:T(8,128)(2,1)} %all-gather.11.cloned.1.call-done.down_ref.weight_ref, bf16[1536,704]{1,0:T(8,128)(2,1)} %get-tuple-element.116.slope_ref, ...), custom_call_target="tpu_custom_call" | custom-call | tf_op jit(solution)/shard_map/hidden_back_stay/pallas_call | solution.py:396
  314.4 14.5 %outer.1 = bf16[2048,1408]{1,0:T(8,128)(2,1)} custom-call(bf16[1536,2048]{1,0:T(8,128)(2,1)} %bitcast.267, bf16[768,1408]{1,0:T(8,128)(2,1)} %get-tuple-element.124.refs_0_, bf16[768,1408]{1,0:T(8,128)(2,1)} %get-tuple-element.125.refs_1_), custom_call_target="tpu_custom_call" | custom-call | tf_op jit(solution)/shard_map/outer/pallas_call | solution.py:431
  337.6 5.8 %collective-permute-done.33 = bf16[1,1,96,2048]{3,2,1,0:T(8,128)(2,1)S(1)} collective-permute-done((bf16[1,1,96,2048]{3,2,1,0:T(8,128)(2,1)S(1)}, bf16[1,1,96,2048]{3,2,1,0:T(8,128)(2,1)S(1)}, u32[]{:S(2)}, u32[]{:S(2)}) %collective-permute-start.33) | collective-permute-done | bytes 393248 | tf_op jit(solution)/shard_map/ppermute | solution.py:32
  349.7 6.3 %out_away.1 = bf16[768,2048]{1,0:T(8,128)(2,1)} custom-call(bf16[1536,704]{1,0:T(8,128)(2,1)} %get-tuple-element.130.row_ref, bf16[704,2048]{1,0:T(8,128)(2,1)} %all-gather.11.cloned.1.call-done.down_ref.weight_ref), custom_call_target="tpu_custom_call" | custom-call | flops 7000000000 | tf_op jit(solution)/shard_map/out_away/pallas_call | solution.py:396
  357.8 9.7 %collective-permute-done.38 = bf16[96,2048]{1,0:T(8,128)(2,1)S(1)} collective-permute-done((bf16[96,2048]{1,0:T(8,128)(2,1)S(1)}, bf16[96,2048]{1,0:T(8,128)(2,1)S(1)}, u32[]{:S(2)}, u32[]{:S(2)}) %collective-permute-start.38) | collective-permute-done | bytes 393248 | tf_op jit(solution)/shard_map/ppermute | solution.py:32
  372.1 7.2 %out_stay.1 = bf16[768,2048]{1,0:T(8,128)(2,1)} custom-call(bf16[1536,704]{1,0:T(8,128)(2,1)} %get-tuple-element.130.row_ref, bf16[704,2048]{1,0:T(8,128)(2,1)} %all-gather.11.cloned.1.call-done.down_ref.weight_ref, bf16[768,2048]{1,0:T(8,128)(2,1)} %collective-permute-done.40.refs_0_), custom_call_target="tpu_custom_call" | custom-call | flops 7000000000 | tf_op jit(solution)/shard_map/out_stay/pallas_call | solution.py:396
  379.3 7.7 %collective-permute-done.39 = bf16[2,1,96,2048]{3,2,0,1:T(8,128)(2,1)S(1)} collective-permute-done((bf16[2,1,96,2048]{3,2,0,1:T(8,128)(2,1)S(1)}, bf16[2,1,96,2048]{3,2,0,1:T(8,128)(2,1)S(1)}, u32[]{:S(2)}, u32[]{:S(2)}) %collective-permute-start.39) | collective-permute-done | bytes 786464 | tf_op jit(solution)/shard_map/ppermute | solution.py:32
  398.1 5.7 %convolution_convert_fusion.4.grad_ref = bf16[256,1536]{1,0:T(8,128)(2,1)} fusion(bf16[256,2048]{1,0:T(8,128)(2,1)S(1)} %copy-done.36, bf16[1536,2048]{1,0:T(8,128)(2,1)} %bitcast.273), kind=kOutput, calls=%fused_computation.10 | convolution fusion | flops 1611005952 | bytes 8126464 | tf_op jit(solution)/shard_map/dot_general | solution.py:24
  425.4 6.3 %collective-permute-done.47 = bf16[1,1,96,2048]{3,2,1,0:T(8,128)(2,1)S(1)} collective-permute-done((bf16[1,1,96,2048]{3,2,1,0:T(8,128)(2,1)S(1)}, bf16[1,1,96,2048]{3,2,1,0:T(8,128)(2,1)S(1)}, u32[]{:S(2)}, u32[]{:S(2)}) %collective-permute-start.47) | collective-permute-done | bytes 393248 | tf_op jit(solution)/shard_map/ppermute | solution.py:32
  432.4 7.0 %all-to-all-start.2 = ((bf16[8,64,1408]{2,1,0:T(8,128)(2,1)}), bf16[8,64,1408]{2,1,0:T(8,128)(2,1)S(1)}, u32[]{:S(2)}, u32[]{:S(2)}) async-start(bf16[8,64,1408]{2,1,0:T(8,128)(2,1)} %bitcast.314), calls=%async_computation.4 | async-start | bytes 2883584 | tf_op jit(solution)/shard_map/all_to_all | solution.py:271
  439.5 20.8 %attention_backward.1 = (f32[256,1536]{1,0:T(8,128)}, f32[64,1536]{1,0:T(8,128)}, f32[64,1536]{1,0:T(8,128)}) custom-call(bf16[1536,64]{1,0:T(8,128)(2,1)} %copy.125.key_ref, bf16[64,1536]{1,0:T(8,128)(2,1)} %bitcast.321, bf16[1536,64]{1,0:T(8,128)(2,1)} %bitcast.300, bf16[256,1536]{1,0:T(8,128)(2,1)} %bitcast.293, ...), custom_call_target="tpu_custom_call" | custom-call | flops 24999999488 | tf_op jit(solution)/shard_map/attention_backward/pallas_call | solution.py:564
  472.7 7.4 %convolution_convert_fusion.2 = bf16[2048,384]{1,0:T(8,128)(2,1)} fusion(bf16[1536,2048]{1,0:T(8,128)(2,1)} %bitcast.281, bf16[384,1536]{1,0:T(8,128)(2,1)S(1)} %pad_maximum_fusion), kind=kOutput, calls=%fused_computation.4 | convolution fusion | flops 2416705536 | bytes 9043968 | tf_op jit(solution)/shard_map/dot_general | solution.py:24
  480.1 6.1 %mixed_stay.1 = bf16[768,2048]{1,0:T(8,128)(2,1)} custom-call(bf16[768,384]{1,0:T(8,128)(2,1)} %bitcast.296, bf16[2048,384]{1,0:T(8,128)(2,1)} %all-gather.7.cloned.1.call-done.weight_ref, bf16[768,2048]{1,0:T(8,128)(2,1)} %collective-permute-done.53.refs_0_), custom_call_target="tpu_custom_call" | custom-call | tf_op jit(solution)/shard_map/mixed_stay/pallas_call | solution.py:396
  499.4 12.4 %collective-permute-done.54 = bf16[2,1,96,2048]{3,2,1,0:T(8,128)(2,1)} collective-permute-done((bf16[2,1,96,2048]{3,2,1,0:T(8,128)(2,1)}, bf16[2,1,96,2048]{3,2,1,0:T(8,128)(2,1)}, u32[]{:S(2)}, u32[]{:S(2)}) %collective-permute-start.54) | collective-permute-done | bytes 786464 | tf_op jit(solution)/shard_map/ppermute | solution.py:32
  (429 shorter events, 215.7 us)
Async XLA Ops:
  7.2 56.2 %all-gather.5.cloned.1.call-start = ((), (), s32[]{:S(2)}) async-start(), calls=%async_computation.8 | async-start | bytes 1310720 | tf_op jit(solution)/shard_map/all_gather | solution.py:263
  24.0 29.6 %all-to-all-start = ((bf16[8,80,384]{2,1,0:T(8,128)(2,1)}), bf16[8,80,384]{2,1,0:T(8,128)(2,1)S(1)}, u32[]{:S(2)}, u32[]{:S(2)}) async-start(bf16[8,80,384]{2,1,0:T(8,128)(2,1)} %pad_maximum_fusion.2), calls=%async_computation | async-start | bytes 983040 | tf_op jit(solution)/shard_map/all_to_all | solution.py:271
  43.8 64.2 %all-gather.7.cloned.1.call-start = ((), (), s32[]{:S(2)}) async-start(), calls=%async_computation.9 | async-start | bytes 1966080 | tf_op jit(solution)/shard_map/all_gather | solution.py:263
  43.9 19.5 %collective-permute-start.4 = (bf16[96,2048]{1,0:T(8,128)(2,1)S(1)}, bf16[96,2048]{1,0:T(8,128)(2,1)S(1)}, u32[]{:S(2)}, u32[]{:S(2)}) collective-permute-start(bf16[96,2048]{1,0:T(8,128)(2,1)S(1)} %get-tuple-element.93), channel_id=1, source_target_pairs={{0,4},{1,5},{2,6},{3,7},{4,0},{5,1},{6,2},{7,3},{8,12},{9,13},{10,... | collective-permute-start | bytes 1179656 | tf_op jit(solution)/shard_map/ppermute | solution.py:32
  65.3 20.7 %collective-permute-start.6 = (bf16[1,2,96,2048]{3,2,1,0:T(8,128)(2,1)}, bf16[1,2,96,2048]{3,2,1,0:T(8,128)(2,1)S(1)}, u32[]{:S(2)}, u32[]{:S(2)}) collective-permute-start(bf16[1,2,96,2048]{3,2,1,0:T(8,128)(2,1)} %maximum_select_fusion.1), channel_id=1, source_target_pairs={{0,4},{1,5},{2,6},{3,7},{4,0},{5,1},{6,2},{7,3},{8,12},{9,13},{10,... | collective-permute-start | bytes 2359304 | tf_op jit(solution)/shard_map/ppermute | solution.py:32
  67.8 20.7 %collective-permute-start.9 = (bf16[2,1,96,2048]{3,2,1,0:T(8,128)(2,1)}, bf16[2,1,96,2048]{3,2,1,0:T(8,128)(2,1)S(1)}, u32[]{:S(2)}, u32[]{:S(2)}) collective-permute-start(bf16[2,1,96,2048]{3,2,1,0:T(8,128)(2,1)} %maximum_select_fusion.3), channel_id=1, source_target_pairs={{0,2},{1,3},{2,0},{3,1},{4,6},{5,7},{6,4},{7,5},{8,10},{9,11},{10,... | collective-permute-start | bytes 2359304 | tf_op jit(solution)/shard_map/ppermute | solution.py:32
  69.2 22.9 %collective-permute-start.5 = (bf16[1,2,96,2048]{3,2,1,0:T(8,128)(2,1)}, bf16[1,2,96,2048]{3,2,1,0:T(8,128)(2,1)}, u32[]{:S(2)}, u32[]{:S(2)}) collective-permute-start(bf16[1,2,96,2048]{3,2,1,0:T(8,128)(2,1)} %maximum_select_fusion.1), channel_id=1, source_target_pairs={{0,1},{1,0},{2,3},{3,2},{4,5},{5,4},{6,7},{7,6},{8,9},{9,8},{10,11... | collective-permute-start | bytes 2359304 | tf_op jit(solution)/shard_map/ppermute | solution.py:32
  69.3 22.8 %collective-permute-start.8 = (bf16[2,1,96,2048]{3,2,1,0:T(8,128)(2,1)}, bf16[2,1,96,2048]{3,2,1,0:T(8,128)(2,1)}, u32[]{:S(2)}, u32[]{:S(2)}) collective-permute-start(bf16[2,1,96,2048]{3,2,1,0:T(8,128)(2,1)} %maximum_select_fusion.3), channel_id=1, source_target_pairs={{0,1},{1,0},{2,3},{3,2},{4,5},{5,4},{6,7},{7,6},{8,9},{9,8},{10,11... | collective-permute-start | bytes 2359304 | tf_op jit(solution)/shard_map/ppermute | solution.py:32
  71.7 30.7 %all-to-all-start.1 = ((bf16[8,64,1408]{2,1,0:T(8,128)(2,1)}), bf16[8,64,1408]{2,1,0:T(8,128)(2,1)}, u32[]{:S(2)}, u32[]{:S(2)}) async-start(bf16[8,64,1408]{2,1,0:T(8,128)(2,1)} %split_units.1), calls=%async_computation.1 | async-start | bytes 2883584 | tf_op jit(solution)/shard_map/all_to_all | solution.py:271
  76.1 155.3 %all-gather.9.cloned.1.call-start = ((), (), s32[]{:S(2)}) async-start(), calls=%async_computation.10 | async-start | bytes 7208960 | tf_op jit(solution)/shard_map/all_gather | solution.py:263
  102.4 165.8 %all-gather.11.cloned.1.call-start = ((), (), s32[]{:S(2)}) async-start(), calls=%async_computation.11 | async-start | bytes 3604480 | tf_op jit(solution)/shard_map/all_gather | solution.py:263
  104.5 27.2 %collective-permute-start.13 = (bf16[192,2048]{1,0:T(8,128)(2,1)S(1)}, bf16[192,2048]{1,0:T(8,128)(2,1)S(1)}, u32[]{:S(2)}, u32[]{:S(2)}) collective-permute-start(bf16[192,2048]{1,0:T(8,128)(2,1)S(1)} %copy-done.17), channel_id=1, source_target_pairs={{0,6},{1,7},{2,4},{3,5},{4,2},{5,3},{6,0},{7,1},{8,14},{9,15},{10,... | collective-permute-start | bytes 2359304 | tf_op jit(solution)/shard_map/ppermute | solution.py:32
  106.0 32.6 %collective-permute-start.12 = (bf16[192,2048]{1,0:T(8,128)(2,1)S(1)}, bf16[192,2048]{1,0:T(8,128)(2,1)S(1)}, u32[]{:S(2)}, u32[]{:S(2)}) collective-permute-start(bf16[192,2048]{1,0:T(8,128)(2,1)S(1)} %copy-done.17), channel_id=1, source_target_pairs={{0,4},{1,5},{2,6},{3,7},{4,0},{5,1},{6,2},{7,3},{8,12},{9,13},{10,... | collective-permute-start | bytes 2359304 | tf_op jit(solution)/shard_map/ppermute | solution.py:32
  107.4 31.1 %collective-permute-start.11 = (bf16[192,2048]{1,0:T(8,128)(2,1)S(1)}, bf16[192,2048]{1,0:T(8,128)(2,1)}, u32[]{:S(2)}, u32[]{:S(2)}) collective-permute-start(bf16[192,2048]{1,0:T(8,128)(2,1)S(1)} %copy-done.17), channel_id=1, source_target_pairs={{0,2},{1,3},{2,0},{3,1},{4,6},{5,7},{6,4},{7,5},{8,10},{9,11},{10,... | collective-permute-start | bytes 2359304 | tf_op jit(solution)/shard_map/ppermute | solution.py:32
  152.5 19.7 %collective-permute-start.15 = (bf16[2,1,96,2048]{3,2,1,0:T(8,128)(2,1)S(1)}, bf16[2,1,96,2048]{3,2,1,0:T(8,128)(2,1)}, u32[]{:S(2)}, u32[]{:S(2)}) collective-permute-start(bf16[2,1,96,2048]{3,2,1,0:T(8,128)(2,1)S(1)} %dynamic-slice_bitcast_fusion.7), channel_id=1, source_target_pairs={{0,2},{1,3},{2,0},{3,1},{4,6},{5,7},{6,4},{7,5},{8,10},{9,11},{10,... | collective-permute-start | bytes 2359304 | tf_op jit(solution)/shard_map/ppermute | solution.py:32
  153.7 21.2 %collective-permute-start.17 = (bf16[1,2,96,2048]{3,2,1,0:T(8,128)(2,1)S(1)}, bf16[1,2,96,2048]{3,2,1,0:T(8,128)(2,1)}, u32[]{:S(2)}, u32[]{:S(2)}) collective-permute-start(bf16[1,2,96,2048]{3,2,1,0:T(8,128)(2,1)S(1)} %dynamic-slice_bitcast_fusion.6), channel_id=1, source_target_pairs={{0,4},{1,5},{2,6},{3,7},{4,0},{5,1},{6,2},{7,3},{8,12},{9,13},{10,... | collective-permute-start | bytes 2359304 | tf_op jit(solution)/shard_map/ppermute | solution.py:32
  155.0 214.7 %reduce-scatter.7.cloned.1.call-start = ((), (), s32[]{:S(2)}) async-start(), calls=%async_computation.13 | async-start | bytes 3604480 | tf_op jit(solution)/shard_map/reduce_scatter | solution.py:267
  201.4 23.3 %collective-permute-start.22 = (bf16[192,2048]{1,0:T(8,128)(2,1)S(1)}, bf16[192,2048]{1,0:T(8,128)(2,1)S(1)}, u32[]{:S(2)}, u32[]{:S(2)}) collective-permute-start(bf16[192,2048]{1,0:T(8,128)(2,1)S(1)} %copy-done.49), channel_id=1, source_target_pairs={{0,1},{1,0},{2,3},{3,2},{4,5},{5,4},{6,7},{7,6},{8,9},{9,8},{10,11... | collective-permute-start | bytes 2359304 | tf_op jit(solution)/shard_map/ppermute | solution.py:32
  201.5 20.0 %collective-permute-start.25 = (bf16[1,2,96,2048]{3,2,1,0:T(8,128)(2,1)S(1)}, bf16[1,2,96,2048]{3,2,1,0:T(8,128)(2,1)S(1)}, u32[]{:S(2)}, u32[]{:S(2)}) collective-permute-start(bf16[1,2,96,2048]{3,2,1,0:T(8,128)(2,1)S(1)} %maximum_select_fusion.5), channel_id=1, source_target_pairs={{0,4},{1,5},{2,6},{3,7},{4,0},{5,1},{6,2},{7,3},{8,12},{9,13},{10,... | collective-permute-start | bytes 2359304 | tf_op jit(solution)/shard_map/ppermute | solution.py:32
  203.2 21.6 %collective-permute-start.24 = (bf16[1,2,96,2048]{3,2,1,0:T(8,128)(2,1)S(1)}, bf16[1,2,96,2048]{3,2,1,0:T(8,128)(2,1)S(1)}, u32[]{:S(2)}, u32[]{:S(2)}) collective-permute-start(bf16[1,2,96,2048]{3,2,1,0:T(8,128)(2,1)S(1)} %maximum_select_fusion.5), channel_id=1, source_target_pairs={{0,1},{1,0},{2,3},{3,2},{4,5},{5,4},{6,7},{7,6},{8,9},{9,8},{10,11... | collective-permute-start | bytes 2359304 | tf_op jit(solution)/shard_map/ppermute | solution.py:32
  204.8 19.8 %collective-permute-start.29 = (bf16[2,1,96,2048]{3,2,1,0:T(8,128)(2,1)S(1)}, bf16[2,1,96,2048]{3,2,1,0:T(8,128)(2,1)S(1)}, u32[]{:S(2)}, u32[]{:S(2)}) collective-permute-start(bf16[2,1,96,2048]{3,2,1,0:T(8,128)(2,1)S(1)} %maximum_select_fusion.7), channel_id=1, source_target_pairs={{0,2},{1,3},{2,0},{3,1},{4,6},{5,7},{6,4},{7,5},{8,10},{9,11},{10,... | collective-permute-start | bytes 2359304 | tf_op jit(solution)/shard_map/ppermute | solution.py:32
  255.6 176.1 %reduce-scatter.5.cloned.1.call-start = ((), (), s32[]{:S(2)}) async-start(), calls=%async_computation.12 | async-start | bytes 7208960 | tf_op jit(solution)/shard_map/reduce_scatter | solution.py:267
  311.4 19.9 %collective-permute-start.32 = (bf16[2,1,96,2048]{3,2,1,0:T(8,128)(2,1)}, bf16[2,1,96,2048]{3,2,1,0:T(8,128)(2,1)}, u32[]{:S(2)}, u32[]{:S(2)}) collective-permute-start(bf16[2,1,96,2048]{3,2,1,0:T(8,128)(2,1)} %dynamic-slice_bitcast_fusion.5), channel_id=1, source_target_pairs={{0,2},{1,3},{2,0},{3,1},{4,6},{5,7},{6,4},{7,5},{8,10},{9,11},{10,... | collective-permute-start | bytes 2359304 | tf_op jit(solution)/shard_map/ppermute | solution.py:32
  312.9 21.6 %collective-permute-start.34 = (bf16[1,2,96,2048]{3,2,1,0:T(8,128)(2,1)S(1)}, bf16[1,2,96,2048]{3,2,1,0:T(8,128)(2,1)}, u32[]{:S(2)}, u32[]{:S(2)}) collective-permute-start(bf16[1,2,96,2048]{3,2,1,0:T(8,128)(2,1)S(1)} %dynamic-slice_bitcast_fusion.4), channel_id=1, source_target_pairs={{0,4},{1,5},{2,6},{3,7},{4,0},{5,1},{6,2},{7,3},{8,12},{9,13},{10,... | collective-permute-start | bytes 2359304 | tf_op jit(solution)/shard_map/ppermute | solution.py:32
  328.9 134.4 %reduce-scatter.9.cloned.1.call-start = ((), (), s32[]{:S(2)}) async-start(), calls=%async_computation.14 | async-start | bytes 1310720 | tf_op jit(solution)/shard_map/reduce_scatter | solution.py:267
  367.6 19.3 %collective-permute-start.39 = (bf16[2,1,96,2048]{3,2,0,1:T(8,128)(2,1)S(1)}, bf16[2,1,96,2048]{3,2,0,1:T(8,128)(2,1)S(1)}, u32[]{:S(2)}, u32[]{:S(2)}) collective-permute-start(bf16[2,1,96,2048]{3,2,0,1:T(8,128)(2,1)S(1)} %bitcast_select_fusion), channel_id=1, source_target_pairs={{0,2},{1,3},{2,0},{3,1},{4,6},{5,7},{6,4},{7,5},{8,10},{9,11},{10,... | collective-permute-start | bytes 2359304 | tf_op jit(solution)/shard_map/ppermute | solution.py:32
  392.1 19.8 %collective-permute-start.45 = (bf16[2,1,96,2048]{3,2,1,0:T(8,128)(2,1)S(1)}, bf16[2,1,96,2048]{3,2,1,0:T(8,128)(2,1)S(1)}, u32[]{:S(2)}, u32[]{:S(2)}) collective-permute-start(bf16[2,1,96,2048]{3,2,1,0:T(8,128)(2,1)S(1)} %get-tuple-element.137), channel_id=1, source_target_pairs={{0,2},{1,3},{2,0},{3,1},{4,6},{5,7},{6,4},{7,5},{8,10},{9,11},{10,... | collective-permute-start | bytes 2359304 | tf_op jit(solution)/shard_map/ppermute | solution.py:32
  392.9 19.8 %collective-permute-start.46 = (bf16[1,2,96,2048]{3,2,1,0:T(8,128)(2,1)S(1)}, bf16[1,2,96,2048]{3,2,1,0:T(8,128)(2,1)S(1)}, u32[]{:S(2)}, u32[]{:S(2)}) collective-permute-start(bf16[1,2,96,2048]{3,2,1,0:T(8,128)(2,1)S(1)} %get-tuple-element.138), channel_id=1, source_target_pairs={{0,4},{1,5},{2,6},{3,7},{4,0},{5,1},{6,2},{7,3},{8,12},{9,13},{10,... | collective-permute-start | bytes 2359304 | tf_op jit(solution)/shard_map/ppermute | solution.py:32
  432.4 30.8 %all-to-all-start.2 = ((bf16[8,64,1408]{2,1,0:T(8,128)(2,1)}), bf16[8,64,1408]{2,1,0:T(8,128)(2,1)S(1)}, u32[]{:S(2)}, u32[]{:S(2)}) async-start(bf16[8,64,1408]{2,1,0:T(8,128)(2,1)} %bitcast.314), calls=%async_computation.4 | async-start | bytes 2883584 | tf_op jit(solution)/shard_map/all_to_all | solution.py:271
  439.4 82.6 %reduce-scatter.11.cloned.1.call-start = ((), (), s32[]{:S(2)}) async-start(), calls=%async_computation.15 | async-start | bytes 1966080 | tf_op jit(solution)/shard_map/reduce_scatter | solution.py:267
  491.8 20.0 %collective-permute-start.54 = (bf16[2,1,96,2048]{3,2,1,0:T(8,128)(2,1)}, bf16[2,1,96,2048]{3,2,1,0:T(8,128)(2,1)}, u32[]{:S(2)}, u32[]{:S(2)}) collective-permute-start(bf16[2,1,96,2048]{3,2,1,0:T(8,128)(2,1)} %get-tuple-element.154), channel_id=1, source_target_pairs={{0,2},{1,3},{2,0},{3,1},{4,6},{5,7},{6,4},{7,5},{8,10},{9,11},{10,... | collective-permute-start | bytes 2359304 | tf_op jit(solution)/shard_map/ppermute | solution.py:32
  493.5 19.8 %collective-permute-start.55 = (bf16[1,2,96,2048]{3,2,1,0:T(8,128)(2,1)}, bf16[1,2,96,2048]{3,2,1,0:T(8,128)(2,1)}, u32[]{:S(2)}, u32[]{:S(2)}) collective-permute-start(bf16[1,2,96,2048]{3,2,1,0:T(8,128)(2,1)} %get-tuple-element.155), channel_id=1, source_target_pairs={{0,4},{1,5},{2,6},{3,7},{4,0},{5,1},{6,2},{7,3},{8,12},{9,13},{10,... | collective-permute-start | bytes 2359304 | tf_op jit(solution)/shard_map/ppermute | solution.py:32
  (112 other events, 1040.7 us)
Sparse Core Ops, SparseCore 0:
  19.6 43.7 all-gather.4
  65.5 36.5 all-gather.6
  103.7 105.5 all-gather.8
  210.7 57.4 all-gather.10
  270.4 54.8 reduce-scatter.6
  329.0 100.5 reduce-scatter.4
  432.5 27.6 reduce-scatter.8
  480.3 33.8 reduce-scatter.10

commit v6 on v4

--- a/solution.py
+++ b/solution.py
@@ -631,7 +631,7 @@
     inputs = tokens.astype(f32)
     factor_one = row_factor(inputs)
     own_gains = jnp.concatenate([attention_gain, feedforward_gain]).astype(f32)[None]
-    spread, last = double_to(own_gains, seqs)
+    spread, _ = double_to(own_gains, seqs)
     tokens_first = gather_first(tokens)
 
     def split_heads(weight):
@@ -650,7 +650,7 @@
     mix = exchange_ctx(jnp.concatenate([mix, small], axis=1))
     gain_one_row, gain_two_row, seg_row = read_small(mix[:, rows:], spread, segments)
     mix = mix[:, :rows].reshape(ranks * rows, -1)
-    proj_wide = gather_seq(lax.ppermute(after(projection, last), BOTH, head_order()))
+    proj_wide = gather_seq(lax.ppermute(projection, BOTH, head_order()))
     mix_wide = gather_seq(after(mix, proj_wide))
     tokens_second = gather_second(lax.optimization_barrier((tokens_first, mix))[0])
     pair = split_units(after(gate_weight, mix), up_weight, units)

time: 558 us -> 552 us (0.989)
    all_to_all x4, starting transfers between devices: 34.2 us -> 20.5 us  [exchange_ctx(): return lax.all_to_all(value, 'ctx', 0, 0)]
    ppermute x2, starting transfers between devices: 6.12 us -> 17.9 us  [double(): other = lax.ppermute(value, 'seq', [(i, i ^ step) for i in range(seqs)])]
    all_gather x4, waiting for transfers between devices: 21.4 us -> 14.9 us  [gather_seq(): return lax.all_gather(value, 'seq', axis=0, tiled=True)]
    ppermute x51, waiting for transfers between devices: 128 us -> 134 us  [swap(): return lax.ppermute(value, 'ctx', [(i, i ^ step) for i in range(count)])]
    unnamed x159 -> x155, local copies, waits for them, and re-layouts: 17.3 us -> 18 us
  transfers between devices with their start and end apart: 70 -> 70, of which waited for: 29 -> 30; matrix products, arithmetic and copies ran while one was open for 17% -> 17% of each run, Pallas kernels for 24% -> 24%
where the time goes in v6:
time: 552 us; the launch traced here: 541 us
  waiting for transfers between devices  175 us (32%)
  Pallas kernels  137 us (25%)
  starting transfers between devices  94.3 us (17%)
  local copies, waits for them, and re-layouts  44.1 us (8%)
  other arithmetic  41.7 us (8%)
  matrix products  32.8 us (6%)
  between operations  16 us (3%)
    ppermute x51, waiting for transfers between devices, swap(): return lax.ppermute(value, 'ctx', [(i, i ^ step) for i in range(count)])  134 us
    pallas_call x7, Pallas kernels, by_rows(): pl.pallas_call(kernel, grid=(count // block,), in_specs=specs, out_specs=...  72.9 us
    ppermute x51, starting transfers between devices, swap(): return lax.ppermute(value, 'ctx', [(i, i ^ step) for i in range(count)])  47.1 us
    dot_general x7, matrix products, dot(): lax.dot_general(left, right, (contract, ((), ())), preferred_element_type...  32.8 us
    pallas_call x1, Pallas kernels, attention_backward(): pl.pallas_call(functools.partial(backward_kernel, block, heads, count), g...  20.8 us
    all_to_all x4, starting transfers between devices, exchange_ctx(): return lax.all_to_all(value, 'ctx', 0, 0)  20.5 us
    unnamed x155, local copies, waits for them, and re-layouts  18 us
    ppermute x2, starting transfers between devices, double(): other = lax.ppermute(value, 'seq', [(i, i ^ step) for i in range(seqs)])  17.9 us
  transfers between devices with their start and end apart: 70, of which 30 were waited for; matrix products, arithmetic and copies ran while one was open for 17% of the time, Pallas kernels for 24%

profile of v6, /device:TPU:0, one launch (start us, length us, event | category | flops | bytes accessed | tf_op | source)
XLA Modules:
  0.0 541.2 jit_solution(13173939694167841693)
XLA Ops:
  10.3 10.3 %collective-permute-start = (bf16[1,128]{1,0:T(2,128)(2,1)S(1)}, bf16[1,128]{1,0:T(2,128)(2,1)S(1)}, u32[]{:S(2)}, u32[]{:S(2)}) collective-permute-start(bf16[1,128]{1,0:T(2,128)(2,1)S(1)} %maximum_convert_fusion), channel_id=1, source_target_pairs={{0,8},{8,0},{16,24},{24,16},{1,9},{9,1},{17,25},{25,17},{2,10},{10... | collective-permute-start | bytes 776 | tf_op jit(solution)/shard_map/ppermute | solution.py:167
  24.3 7.6 %collective-permute-start.1 = (bf16[2,128]{1,0:T(2,128)(2,1)S(1)}, bf16[2,128]{1,0:T(2,128)(2,1)S(1)}, u32[]{:S(2)}, u32[]{:S(2)}) collective-permute-start(bf16[2,128]{1,0:T(2,128)(2,1)S(1)} %maximum_select_fusion.10), channel_id=1, source_target_pairs={{0,16},{8,24},{16,0},{24,8},{1,17},{9,25},{17,1},{25,9},{2,18},{10... | collective-permute-start | bytes 1544 | tf_op jit(solution)/shard_map/ppermute | solution.py:167
  34.3 6.2 %all-to-all-start = ((bf16[8,80,384]{2,1,0:T(8,128)(2,1)}), bf16[8,80,384]{2,1,0:T(8,128)(2,1)S(1)}, u32[]{:S(2)}, u32[]{:S(2)}) async-start(bf16[8,80,384]{2,1,0:T(8,128)(2,1)} %pad_maximum_fusion.2), calls=%async_computation | async-start | bytes 983040 | tf_op jit(solution)/shard_map/all_to_all | solution.py:269
  44.1 6.2 %all-to-all-done = bf16[8,80,384]{2,1,0:T(8,128)(2,1)S(1)} async-done(((bf16[8,80,384]{2,1,0:T(8,128)(2,1)}), bf16[8,80,384]{2,1,0:T(8,128)(2,1)S(1)}, u32[]{:S(2)}, u32[]{:S(2)}) %all-to-all-start) | async-done | bytes 491552 | tf_op jit(solution)/shard_map/all_to_all | solution.py:269
  69.9 9.9 %collective-permute-done.6 = bf16[1,2,96,2048]{3,2,1,0:T(8,128)(2,1)S(1)} collective-permute-done((bf16[1,2,96,2048]{3,2,1,0:T(8,128)(2,1)}, bf16[1,2,96,2048]{3,2,1,0:T(8,128)(2,1)S(1)}, u32[]{:S(2)}, u32[]{:S(2)}) %collective-permute-start.6) | collective-permute-done | bytes 786464 | tf_op jit(solution)/shard_map/ppermute | solution.py:32
  90.4 5.9 %all-to-all-done.1 = bf16[8,64,1408]{2,1,0:T(8,128)(2,1)} async-done(((bf16[8,64,1408]{2,1,0:T(8,128)(2,1)}), bf16[8,64,1408]{2,1,0:T(8,128)(2,1)}, u32[]{:S(2)}, u32[]{:S(2)}) %all-to-all-start.1) | async-done | bytes 1441824 | tf_op jit(solution)/shard_map/all_to_all | solution.py:269
  101.9 5.8 %fusion.38 = f32[384,1536]{1,0:T(8,128)S(1)} fusion(bf16[2048,384]{1,0:T(8,128)(2,1)} %all-gather.7.cloned.1.call-done.weight_ref, bf16[1536,2048]{1,0:T(8,128)(2,1)} %bitcast.282), kind=kOutput, calls=%fused_computation.165 | convolution fusion | flops 2415919104 | bytes 10223616 | tf_op jit(solution)/shard_map/dot_general | solution.py:24
  112.0 13.7 %attention_forward.1 = (f32[256,1536]{1,0:T(8,128)}, bf16[1536,256]{1,0:T(8,128)(2,1)}, f32[4,1536]{1,0:T(4,128)}) custom-call(bf16[1536,64]{1,0:T(8,128)(2,1)} %copy.130.key_ref, bf16[64,1536]{1,0:T(8,128)(2,1)} %copy.131.value_ref, bf16[256,1536]{1,0:T(8,128)(2,1)} %bitcast.294, s32[1,1536]{1,0:T(1,128)} %reduce_sum.93.start_ref), custom_call_target="tpu_custom_call" | custom-call | tf_op jit(solution)/shard_map/attention_forward/pallas_call | solution.py:474
  125.7 6.9 %collective-permute-done.12 = bf16[192,2048]{1,0:T(8,128)(2,1)S(1)} collective-permute-done((bf16[192,2048]{1,0:T(8,128)(2,1)S(1)}, bf16[192,2048]{1,0:T(8,128)(2,1)S(1)}, u32[]{:S(2)}, u32[]{:S(2)}) %collective-permute-start.12) | collective-permute-done | bytes 786464 | tf_op jit(solution)/shard_map/ppermute | solution.py:32
  149.1 17.4 %collective-permute-done.15 = bf16[2,1,96,2048]{3,2,1,0:T(8,128)(2,1)} collective-permute-done((bf16[2,1,96,2048]{3,2,1,0:T(8,128)(2,1)S(1)}, bf16[2,1,96,2048]{3,2,1,0:T(8,128)(2,1)}, u32[]{:S(2)}, u32[]{:S(2)}) %collective-permute-start.15) | collective-permute-done | bytes 786464 | tf_op jit(solution)/shard_map/ppermute | solution.py:32
  171.2 7.2 %collective-permute-done.16 = bf16[1,1,96,2048]{3,2,1,0:T(8,128)(2,1)S(1)} collective-permute-done((bf16[1,1,96,2048]{3,2,1,0:T(8,128)(2,1)S(1)}, bf16[1,1,96,2048]{3,2,1,0:T(8,128)(2,1)S(1)}, u32[]{:S(2)}, u32[]{:S(2)}) %collective-permute-start.16) | collective-permute-done | bytes 393248 | tf_op jit(solution)/shard_map/ppermute | solution.py:32
  185.6 10.1 %collective-permute-done.23 = bf16[96,2048]{1,0:T(8,128)(2,1)S(1)} collective-permute-done((bf16[96,2048]{1,0:T(8,128)(2,1)S(1)}, bf16[96,2048]{1,0:T(8,128)(2,1)S(1)}, u32[]{:S(2)}, u32[]{:S(2)}) %collective-permute-start.23) | collective-permute-done | bytes 393248 | tf_op jit(solution)/shard_map/ppermute | solution.py:32
  200.2 15.8 %collective-permute-done.25 = bf16[1,2,96,2048]{3,2,1,0:T(8,128)(2,1)S(1)} collective-permute-done((bf16[1,2,96,2048]{3,2,1,0:T(8,128)(2,1)S(1)}, bf16[1,2,96,2048]{3,2,1,0:T(8,128)(2,1)S(1)}, u32[]{:S(2)}, u32[]{:S(2)}) %collective-permute-start.25) | collective-permute-done | bytes 786464 | tf_op jit(solution)/shard_map/ppermute | solution.py:32
  225.9 16.4 %hidden_layer.1 = (bf16[1536,704]{1,0:T(8,128)(2,1)}, bf16[1536,704]{1,0:T(8,128)(2,1)}, bf16[1536,704]{1,0:T(8,128)(2,1)}) custom-call(bf16[1536,2048]{1,0:T(8,128)(2,1)} %bitcast.268, bf16[2048,1408]{1,0:T(8,128)(2,1)} %all-gather.9.cloned.1.call-done.weight_ref), custom_call_target="tpu_custom_call" | custom-call | tf_op jit(solution)/shard_map/hidden_layer/pallas_call | solution.py:394
  242.4 7.8 %convolution_convert_fusion.1 = bf16[704,2048]{1,0:T(8,128)(2,1)} fusion(bf16[1536,704]{1,0:T(8,128)(2,1)} %get-tuple-element.126.row_ref, bf16[1536,2048]{1,0:T(8,128)(2,1)S(1)} %bitcast.274), kind=kOutput, calls=%fused_computation.3 | convolution fusion | flops 4430626816 | bytes 11337728 | tf_op jit(solution)/shard_map/dot_general | solution.py:24
  250.2 11.5 %all-gather.11.cloned.1.call-done.down_ref.weight_ref = bf16[704,2048]{1,0:T(8,128)(2,1)} async-done(((bf16[176,2048]{1,0:T(8,128)(2,1)}), bf16[704,2048]{1,0:T(8,128)(2,1)}) %all-gather.11.cloned.1.call-update) | async-done | bytes 2883600 | tf_op jit(solution)/shard_map/all_gather | solution.py:261
  261.7 15.6 %hidden_back_away.1 = (bf16[768,1408]{1,0:T(8,128)(2,1)}, bf16[768,2048]{1,0:T(8,128)(2,1)}) custom-call(bf16[1536,2048]{1,0:T(8,128)(2,1)} %bitcast.272, bf16[704,2048]{1,0:T(8,128)(2,1)} %all-gather.11.cloned.1.call-done.down_ref.weight_ref, bf16[1536,704]{1,0:T(8,128)(2,1)} %get-tuple-element.112.slope_ref, ...), custom_call_target="tpu_custom_call" | custom-call | tf_op jit(solution)/shard_map/hidden_back_away/pallas_call | solution.py:394
  277.3 5.9 %collective-permute-done.31.refs_0_ = bf16[768,2048]{1,0:T(8,128)(2,1)S(1)} collective-permute-done((bf16[768,2048]{1,0:T(8,128)(2,1)}, bf16[768,2048]{1,0:T(8,128)(2,1)S(1)}, u32[]{:S(2)}, u32[]{:S(2)}) %collective-permute-start.31) | collective-permute-done | bytes 3145760 | tf_op jit(solution)/shard_map/ppermute | solution.py:32
  284.9 15.8 %hidden_back_stay.1 = (bf16[768,1408]{1,0:T(8,128)(2,1)}, bf16[768,2048]{1,0:T(8,128)(2,1)}) custom-call(bf16[1536,2048]{1,0:T(8,128)(2,1)} %bitcast.273, bf16[704,2048]{1,0:T(8,128)(2,1)} %all-gather.11.cloned.1.call-done.down_ref.weight_ref, bf16[1536,704]{1,0:T(8,128)(2,1)} %get-tuple-element.112.slope_ref, ...), custom_call_target="tpu_custom_call" | custom-call | tf_op jit(solution)/shard_map/hidden_back_stay/pallas_call | solution.py:394
  307.8 14.5 %outer.1 = bf16[2048,1408]{1,0:T(8,128)(2,1)} custom-call(bf16[1536,2048]{1,0:T(8,128)(2,1)} %bitcast.269, bf16[768,1408]{1,0:T(8,128)(2,1)} %get-tuple-element.120.refs_0_, bf16[768,1408]{1,0:T(8,128)(2,1)} %get-tuple-element.121.refs_1_), custom_call_target="tpu_custom_call" | custom-call | tf_op jit(solution)/shard_map/outer/pallas_call | solution.py:429
  331.0 5.8 %collective-permute-done.33 = bf16[1,1,96,2048]{3,2,1,0:T(8,128)(2,1)S(1)} collective-permute-done((bf16[1,1,96,2048]{3,2,1,0:T(8,128)(2,1)S(1)}, bf16[1,1,96,2048]{3,2,1,0:T(8,128)(2,1)S(1)}, u32[]{:S(2)}, u32[]{:S(2)}) %collective-permute-start.33) | collective-permute-done | bytes 393248 | tf_op jit(solution)/shard_map/ppermute | solution.py:32
  343.2 6.3 %out_away.1 = bf16[768,2048]{1,0:T(8,128)(2,1)} custom-call(bf16[1536,704]{1,0:T(8,128)(2,1)} %get-tuple-element.126.row_ref, bf16[704,2048]{1,0:T(8,128)(2,1)} %all-gather.11.cloned.1.call-done.down_ref.weight_ref), custom_call_target="tpu_custom_call" | custom-call | flops 7000000000 | tf_op jit(solution)/shard_map/out_away/pallas_call | solution.py:394
  351.3 9.6 %collective-permute-done.38 = bf16[96,2048]{1,0:T(8,128)(2,1)S(1)} collective-permute-done((bf16[96,2048]{1,0:T(8,128)(2,1)S(1)}, bf16[96,2048]{1,0:T(8,128)(2,1)S(1)}, u32[]{:S(2)}, u32[]{:S(2)}) %collective-permute-start.38) | collective-permute-done | bytes 393248 | tf_op jit(solution)/shard_map/ppermute | solution.py:32
  365.6 7.2 %out_stay.1 = bf16[768,2048]{1,0:T(8,128)(2,1)} custom-call(bf16[1536,704]{1,0:T(8,128)(2,1)} %get-tuple-element.126.row_ref, bf16[704,2048]{1,0:T(8,128)(2,1)} %all-gather.11.cloned.1.call-done.down_ref.weight_ref, bf16[768,2048]{1,0:T(8,128)(2,1)} %collective-permute-done.40.refs_0_), custom_call_target="tpu_custom_call" | custom-call | flops 7000000000 | tf_op jit(solution)/shard_map/out_stay/pallas_call | solution.py:394
  372.8 7.6 %collective-permute-done.39 = bf16[2,1,96,2048]{3,2,0,1:T(8,128)(2,1)S(1)} collective-permute-done((bf16[2,1,96,2048]{3,2,0,1:T(8,128)(2,1)S(1)}, bf16[2,1,96,2048]{3,2,0,1:T(8,128)(2,1)S(1)}, u32[]{:S(2)}, u32[]{:S(2)}) %collective-permute-start.39) | collective-permute-done | bytes 786464 | tf_op jit(solution)/shard_map/ppermute | solution.py:32
  411.4 6.3 %collective-permute-start.48 = (bf16[1,1,96,2048]{3,2,1,0:T(8,128)(2,1)S(1)}, bf16[1,1,96,2048]{3,2,1,0:T(8,128)(2,1)S(1)}, u32[]{:S(2)}, u32[]{:S(2)}) collective-permute-start(bf16[1,1,96,2048]{3,2,1,0:T(8,128)(2,1)S(1)} %dynamic-slice_convert_fusion.2), channel_id=1, source_target_pairs={{0,2},{1,3},{2,0},{3,1},{4,6},{5,7},{6,4},{7,5},{8,10},{9,11},{10,... | collective-permute-start | bytes 1179656 | tf_op jit(solution)/shard_map/ppermute | solution.py:32
  418.9 6.3 %collective-permute-done.47 = bf16[1,1,96,2048]{3,2,1,0:T(8,128)(2,1)S(1)} collective-permute-done((bf16[1,1,96,2048]{3,2,1,0:T(8,128)(2,1)S(1)}, bf16[1,1,96,2048]{3,2,1,0:T(8,128)(2,1)S(1)}, u32[]{:S(2)}, u32[]{:S(2)}) %collective-permute-start.47) | collective-permute-done | bytes 393248 | tf_op jit(solution)/shard_map/ppermute | solution.py:32
  425.9 6.3 %all-to-all-start.2 = ((bf16[8,64,1408]{2,1,0:T(8,128)(2,1)}), bf16[8,64,1408]{2,1,0:T(8,128)(2,1)S(1)}, u32[]{:S(2)}, u32[]{:S(2)}) async-start(bf16[8,64,1408]{2,1,0:T(8,128)(2,1)} %bitcast.316), calls=%async_computation.4 | async-start | bytes 2883584 | tf_op jit(solution)/shard_map/all_to_all | solution.py:269
  432.2 20.8 %attention_backward.1 = (f32[256,1536]{1,0:T(8,128)}, f32[64,1536]{1,0:T(8,128)}, f32[64,1536]{1,0:T(8,128)}) custom-call(bf16[1536,64]{1,0:T(8,128)(2,1)} %copy.130.key_ref, bf16[64,1536]{1,0:T(8,128)(2,1)} %bitcast.323, bf16[1536,64]{1,0:T(8,128)(2,1)} %bitcast.302, bf16[256,1536]{1,0:T(8,128)(2,1)} %bitcast.295, bf16[256,1536]{1,0:T(8,128)(2,1)} %fusion.grad_ref, ...), custom_call_target="tpu_custom_call" | custom-call | flops 24999999488 | tf_op jit(solution)/shard_map/attention_backward/pallas_call | solution.py:562
  465.4 7.4 %convolution_convert_fusion.2 = bf16[2048,384]{1,0:T(8,128)(2,1)} fusion(bf16[1536,2048]{1,0:T(8,128)(2,1)} %bitcast.283, bf16[384,1536]{1,0:T(8,128)(2,1)S(1)} %pad_maximum_fusion), kind=kOutput, calls=%fused_computation.4 | convolution fusion | flops 2416705536 | bytes 9043968 | tf_op jit(solution)/shard_map/dot_general | solution.py:24
  473.7 6.5 %mixed_stay.1 = bf16[768,2048]{1,0:T(8,128)(2,1)} custom-call(bf16[768,384]{1,0:T(8,128)(2,1)} %bitcast.298, bf16[2048,384]{1,0:T(8,128)(2,1)} %all-gather.7.cloned.1.call-done.weight_ref, bf16[768,2048]{1,0:T(8,128)(2,1)} %collective-permute-done.53.refs_0_), custom_call_target="tpu_custom_call" | custom-call | tf_op jit(solution)/shard_map/mixed_stay/pallas_call | solution.py:394
  494.1 12.7 %reduce-scatter.11.cloned.1.call-done = bf16[512,384]{1,0:T(8,128)(2,1)} async-done(((bf16[2048,384]{1,0:T(8,128)(2,1)}), bf16[512,384]{1,0:T(8,128)(2,1)}) %reduce-scatter.11.cloned.1.call-update) | async-done | bytes 393232 | tf_op jit(solution)/shard_map/reduce_scatter | solution.py:265
  (433 shorter events, 212.1 us)
Async XLA Ops:
  7.2 47.4 %all-gather.5.cloned.1.call-start = ((), (), s32[]{:S(2)}) async-start(), calls=%async_computation.8 | async-start | bytes 1310720 | tf_op jit(solution)/shard_map/all_gather | solution.py:261
  40.4 61.5 %all-gather.7.cloned.1.call-start = ((), (), s32[]{:S(2)}) async-start(), calls=%async_computation.9 | async-start | bytes 1966080 | tf_op jit(solution)/shard_map/all_gather | solution.py:261
  59.1 20.7 %collective-permute-start.6 = (bf16[1,2,96,2048]{3,2,1,0:T(8,128)(2,1)}, bf16[1,2,96,2048]{3,2,1,0:T(8,128)(2,1)S(1)}, u32[]{:S(2)}, u32[]{:S(2)}) collective-permute-start(bf16[1,2,96,2048]{3,2,1,0:T(8,128)(2,1)} %maximum_select_fusion.1), channel_id=1, source_target_pairs={{0,4},{1,5},{2,6},{3,7},{4,0},{5,1},{6,2},{7,3},{8,12},{9,13},{10,... | collective-permute-start | bytes 2359304 | tf_op jit(solution)/shard_map/ppermute | solution.py:32
  61.6 20.7 %collective-permute-start.9 = (bf16[2,1,96,2048]{3,2,1,0:T(8,128)(2,1)}, bf16[2,1,96,2048]{3,2,1,0:T(8,128)(2,1)S(1)}, u32[]{:S(2)}, u32[]{:S(2)}) collective-permute-start(bf16[2,1,96,2048]{3,2,1,0:T(8,128)(2,1)} %maximum_select_fusion.3), channel_id=1, source_target_pairs={{0,2},{1,3},{2,0},{3,1},{4,6},{5,7},{6,4},{7,5},{8,10},{9,11},{10,... | collective-permute-start | bytes 2359304 | tf_op jit(solution)/shard_map/ppermute | solution.py:32
  62.1 23.8 %collective-permute-start.5 = (bf16[1,2,96,2048]{3,2,1,0:T(8,128)(2,1)}, bf16[1,2,96,2048]{3,2,1,0:T(8,128)(2,1)}, u32[]{:S(2)}, u32[]{:S(2)}) collective-permute-start(bf16[1,2,96,2048]{3,2,1,0:T(8,128)(2,1)} %maximum_select_fusion.1), channel_id=1, source_target_pairs={{0,1},{1,0},{2,3},{3,2},{4,5},{5,4},{6,7},{7,6},{8,9},{9,8},{10,11... | collective-permute-start | bytes 2359304 | tf_op jit(solution)/shard_map/ppermute | solution.py:32
  62.1 23.8 %collective-permute-start.8 = (bf16[2,1,96,2048]{3,2,1,0:T(8,128)(2,1)}, bf16[2,1,96,2048]{3,2,1,0:T(8,128)(2,1)}, u32[]{:S(2)}, u32[]{:S(2)}) collective-permute-start(bf16[2,1,96,2048]{3,2,1,0:T(8,128)(2,1)} %maximum_select_fusion.3), channel_id=1, source_target_pairs={{0,1},{1,0},{2,3},{3,2},{4,5},{5,4},{6,7},{7,6},{8,9},{9,8},{10,11... | collective-permute-start | bytes 2359304 | tf_op jit(solution)/shard_map/ppermute | solution.py:32
  64.5 31.8 %all-to-all-start.1 = ((bf16[8,64,1408]{2,1,0:T(8,128)(2,1)}), bf16[8,64,1408]{2,1,0:T(8,128)(2,1)}, u32[]{:S(2)}, u32[]{:S(2)}) async-start(bf16[8,64,1408]{2,1,0:T(8,128)(2,1)} %split_units.1), calls=%async_computation.1 | async-start | bytes 2883584 | tf_op jit(solution)/shard_map/all_to_all | solution.py:269
  68.9 157.0 %all-gather.9.cloned.1.call-start = ((), (), s32[]{:S(2)}) async-start(), calls=%async_computation.10 | async-start | bytes 7208960 | tf_op jit(solution)/shard_map/all_gather | solution.py:261
  96.3 165.3 %all-gather.11.cloned.1.call-start = ((), (), s32[]{:S(2)}) async-start(), calls=%async_computation.11 | async-start | bytes 3604480 | tf_op jit(solution)/shard_map/all_gather | solution.py:261
  98.4 27.3 %collective-permute-start.13 = (bf16[192,2048]{1,0:T(8,128)(2,1)S(1)}, bf16[192,2048]{1,0:T(8,128)(2,1)S(1)}, u32[]{:S(2)}, u32[]{:S(2)}) collective-permute-start(bf16[192,2048]{1,0:T(8,128)(2,1)S(1)} %copy-done.17), channel_id=1, source_target_pairs={{0,6},{1,7},{2,4},{3,5},{4,2},{5,3},{6,0},{7,1},{8,14},{9,15},{10,... | collective-permute-start | bytes 2359304 | tf_op jit(solution)/shard_map/ppermute | solution.py:32
  100.3 32.3 %collective-permute-start.12 = (bf16[192,2048]{1,0:T(8,128)(2,1)S(1)}, bf16[192,2048]{1,0:T(8,128)(2,1)S(1)}, u32[]{:S(2)}, u32[]{:S(2)}) collective-permute-start(bf16[192,2048]{1,0:T(8,128)(2,1)S(1)} %copy-done.17), channel_id=1, source_target_pairs={{0,4},{1,5},{2,6},{3,7},{4,0},{5,1},{6,2},{7,3},{8,12},{9,13},{10,... | collective-permute-start | bytes 2359304 | tf_op jit(solution)/shard_map/ppermute | solution.py:32
  100.6 32.5 %collective-permute-start.11 = (bf16[192,2048]{1,0:T(8,128)(2,1)S(1)}, bf16[192,2048]{1,0:T(8,128)(2,1)}, u32[]{:S(2)}, u32[]{:S(2)}) collective-permute-start(bf16[192,2048]{1,0:T(8,128)(2,1)S(1)} %copy-done.17), channel_id=1, source_target_pairs={{0,2},{1,3},{2,0},{3,1},{4,6},{5,7},{6,4},{7,5},{8,10},{9,11},{10,... | collective-permute-start | bytes 2359304 | tf_op jit(solution)/shard_map/ppermute | solution.py:32
  146.8 19.7 %collective-permute-start.15 = (bf16[2,1,96,2048]{3,2,1,0:T(8,128)(2,1)S(1)}, bf16[2,1,96,2048]{3,2,1,0:T(8,128)(2,1)}, u32[]{:S(2)}, u32[]{:S(2)}) collective-permute-start(bf16[2,1,96,2048]{3,2,1,0:T(8,128)(2,1)S(1)} %dynamic-slice_bitcast_fusion.7), channel_id=1, source_target_pairs={{0,2},{1,3},{2,0},{3,1},{4,6},{5,7},{6,4},{7,5},{8,10},{9,11},{10,... | collective-permute-start | bytes 2359304 | tf_op jit(solution)/shard_map/ppermute | solution.py:32
  147.8 21.5 %collective-permute-start.17 = (bf16[1,2,96,2048]{3,2,1,0:T(8,128)(2,1)S(1)}, bf16[1,2,96,2048]{3,2,1,0:T(8,128)(2,1)}, u32[]{:S(2)}, u32[]{:S(2)}) collective-permute-start(bf16[1,2,96,2048]{3,2,1,0:T(8,128)(2,1)S(1)} %dynamic-slice_bitcast_fusion.6), channel_id=1, source_target_pairs={{0,4},{1,5},{2,6},{3,7},{4,0},{5,1},{6,2},{7,3},{8,12},{9,13},{10,... | collective-permute-start | bytes 2359304 | tf_op jit(solution)/shard_map/ppermute | solution.py:32
  149.1 214.2 %reduce-scatter.7.cloned.1.call-start = ((), (), s32[]{:S(2)}) async-start(), calls=%async_computation.13 | async-start | bytes 3604480 | tf_op jit(solution)/shard_map/reduce_scatter | solution.py:265
  195.7 23.5 %collective-permute-start.22 = (bf16[192,2048]{1,0:T(8,128)(2,1)S(1)}, bf16[192,2048]{1,0:T(8,128)(2,1)S(1)}, u32[]{:S(2)}, u32[]{:S(2)}) collective-permute-start(bf16[192,2048]{1,0:T(8,128)(2,1)S(1)} %copy-done.52), channel_id=1, source_target_pairs={{0,1},{1,0},{2,3},{3,2},{4,5},{5,4},{6,7},{7,6},{8,9},{9,8},{10,11... | collective-permute-start | bytes 2359304 | tf_op jit(solution)/shard_map/ppermute | solution.py:32
  195.9 20.0 %collective-permute-start.25 = (bf16[1,2,96,2048]{3,2,1,0:T(8,128)(2,1)S(1)}, bf16[1,2,96,2048]{3,2,1,0:T(8,128)(2,1)S(1)}, u32[]{:S(2)}, u32[]{:S(2)}) collective-permute-start(bf16[1,2,96,2048]{3,2,1,0:T(8,128)(2,1)S(1)} %maximum_select_fusion.5), channel_id=1, source_target_pairs={{0,4},{1,5},{2,6},{3,7},{4,0},{5,1},{6,2},{7,3},{8,12},{9,13},{10,... | collective-permute-start | bytes 2359304 | tf_op jit(solution)/shard_map/ppermute | solution.py:32
  197.7 21.6 %collective-permute-start.24 = (bf16[1,2,96,2048]{3,2,1,0:T(8,128)(2,1)S(1)}, bf16[1,2,96,2048]{3,2,1,0:T(8,128)(2,1)S(1)}, u32[]{:S(2)}, u32[]{:S(2)}) collective-permute-start(bf16[1,2,96,2048]{3,2,1,0:T(8,128)(2,1)S(1)} %maximum_select_fusion.5), channel_id=1, source_target_pairs={{0,1},{1,0},{2,3},{3,2},{4,5},{5,4},{6,7},{7,6},{8,9},{9,8},{10,11... | collective-permute-start | bytes 2359304 | tf_op jit(solution)/shard_map/ppermute | solution.py:32
  199.3 19.8 %collective-permute-start.29 = (bf16[2,1,96,2048]{3,2,1,0:T(8,128)(2,1)S(1)}, bf16[2,1,96,2048]{3,2,1,0:T(8,128)(2,1)S(1)}, u32[]{:S(2)}, u32[]{:S(2)}) collective-permute-start(bf16[2,1,96,2048]{3,2,1,0:T(8,128)(2,1)S(1)} %maximum_select_fusion.7), channel_id=1, source_target_pairs={{0,2},{1,3},{2,0},{3,1},{4,6},{5,7},{6,4},{7,5},{8,10},{9,11},{10,... | collective-permute-start | bytes 2359304 | tf_op jit(solution)/shard_map/ppermute | solution.py:32
  200.0 19.3 %collective-permute-start.28 = (bf16[2,1,96,2048]{3,2,1,0:T(8,128)(2,1)S(1)}, bf16[2,1,96,2048]{3,2,1,0:T(8,128)(2,1)S(1)}, u32[]{:S(2)}, u32[]{:S(2)}) collective-permute-start(bf16[2,1,96,2048]{3,2,1,0:T(8,128)(2,1)S(1)} %maximum_select_fusion.7), channel_id=1, source_target_pairs={{0,1},{1,0},{2,3},{3,2},{4,5},{5,4},{6,7},{7,6},{8,9},{9,8},{10,11... | collective-permute-start | bytes 2359304 | tf_op jit(solution)/shard_map/ppermute | solution.py:32
  250.2 175.0 %reduce-scatter.5.cloned.1.call-start = ((), (), s32[]{:S(2)}) async-start(), calls=%async_computation.12 | async-start | bytes 7208960 | tf_op jit(solution)/shard_map/reduce_scatter | solution.py:265
  304.9 19.9 %collective-permute-start.32 = (bf16[2,1,96,2048]{3,2,1,0:T(8,128)(2,1)}, bf16[2,1,96,2048]{3,2,1,0:T(8,128)(2,1)}, u32[]{:S(2)}, u32[]{:S(2)}) collective-permute-start(bf16[2,1,96,2048]{3,2,1,0:T(8,128)(2,1)} %dynamic-slice_bitcast_fusion.5), channel_id=1, source_target_pairs={{0,2},{1,3},{2,0},{3,1},{4,6},{5,7},{6,4},{7,5},{8,10},{9,11},{10,... | collective-permute-start | bytes 2359304 | tf_op jit(solution)/shard_map/ppermute | solution.py:32
  306.4 21.6 %collective-permute-start.34 = (bf16[1,2,96,2048]{3,2,1,0:T(8,128)(2,1)S(1)}, bf16[1,2,96,2048]{3,2,1,0:T(8,128)(2,1)}, u32[]{:S(2)}, u32[]{:S(2)}) collective-permute-start(bf16[1,2,96,2048]{3,2,1,0:T(8,128)(2,1)S(1)} %dynamic-slice_bitcast_fusion.4), channel_id=1, source_target_pairs={{0,4},{1,5},{2,6},{3,7},{4,0},{5,1},{6,2},{7,3},{8,12},{9,13},{10,... | collective-permute-start | bytes 2359304 | tf_op jit(solution)/shard_map/ppermute | solution.py:32
  322.3 133.7 %reduce-scatter.9.cloned.1.call-start = ((), (), s32[]{:S(2)}) async-start(), calls=%async_computation.14 | async-start | bytes 1310720 | tf_op jit(solution)/shard_map/reduce_scatter | solution.py:265
  361.1 19.3 %collective-permute-start.39 = (bf16[2,1,96,2048]{3,2,0,1:T(8,128)(2,1)S(1)}, bf16[2,1,96,2048]{3,2,0,1:T(8,128)(2,1)S(1)}, u32[]{:S(2)}, u32[]{:S(2)}) collective-permute-start(bf16[2,1,96,2048]{3,2,0,1:T(8,128)(2,1)S(1)} %bitcast_select_fusion), channel_id=1, source_target_pairs={{0,2},{1,3},{2,0},{3,1},{4,6},{5,7},{6,4},{7,5},{8,10},{9,11},{10,... | collective-permute-start | bytes 2359304 | tf_op jit(solution)/shard_map/ppermute | solution.py:32
  362.7 19.1 %collective-permute-start.37 = (bf16[1,2,96,2048]{3,2,1,0:T(8,128)(2,1)S(1)}, bf16[1,2,96,2048]{3,2,1,0:T(8,128)(2,1)S(1)}, u32[]{:S(2)}, u32[]{:S(2)}) collective-permute-start(bf16[1,2,96,2048]{3,2,1,0:T(8,128)(2,1)S(1)} %maximum_select_fusion.8), channel_id=1, source_target_pairs={{0,4},{1,5},{2,6},{3,7},{4,0},{5,1},{6,2},{7,3},{8,12},{9,13},{10,... | collective-permute-start | bytes 2359304 | tf_op jit(solution)/shard_map/ppermute | solution.py:32
  385.6 19.8 %collective-permute-start.45 = (bf16[2,1,96,2048]{3,2,1,0:T(8,128)(2,1)S(1)}, bf16[2,1,96,2048]{3,2,1,0:T(8,128)(2,1)S(1)}, u32[]{:S(2)}, u32[]{:S(2)}) collective-permute-start(bf16[2,1,96,2048]{3,2,1,0:T(8,128)(2,1)S(1)} %get-tuple-element.133), channel_id=1, source_target_pairs={{0,2},{1,3},{2,0},{3,1},{4,6},{5,7},{6,4},{7,5},{8,10},{9,11},{10,... | collective-permute-start | bytes 2359304 | tf_op jit(solution)/shard_map/ppermute | solution.py:32
  386.3 19.8 %collective-permute-start.46 = (bf16[1,2,96,2048]{3,2,1,0:T(8,128)(2,1)S(1)}, bf16[1,2,96,2048]{3,2,1,0:T(8,128)(2,1)S(1)}, u32[]{:S(2)}, u32[]{:S(2)}) collective-permute-start(bf16[1,2,96,2048]{3,2,1,0:T(8,128)(2,1)S(1)} %get-tuple-element.134), channel_id=1, source_target_pairs={{0,4},{1,5},{2,6},{3,7},{4,0},{5,1},{6,2},{7,3},{8,12},{9,13},{10,... | collective-permute-start | bytes 2359304 | tf_op jit(solution)/shard_map/ppermute | solution.py:32
  425.9 30.2 %all-to-all-start.2 = ((bf16[8,64,1408]{2,1,0:T(8,128)(2,1)}), bf16[8,64,1408]{2,1,0:T(8,128)(2,1)S(1)}, u32[]{:S(2)}, u32[]{:S(2)}) async-start(bf16[8,64,1408]{2,1,0:T(8,128)(2,1)} %bitcast.316), calls=%async_computation.4 | async-start | bytes 2883584 | tf_op jit(solution)/shard_map/all_to_all | solution.py:269
  432.2 74.7 %reduce-scatter.11.cloned.1.call-start = ((), (), s32[]{:S(2)}) async-start(), calls=%async_computation.15 | async-start | bytes 1966080 | tf_op jit(solution)/shard_map/reduce_scatter | solution.py:265
  485.2 21.6 %collective-permute-start.54 = (bf16[2,1,96,2048]{3,2,1,0:T(8,128)(2,1)}, bf16[2,1,96,2048]{3,2,1,0:T(8,128)(2,1)}, u32[]{:S(2)}, u32[]{:S(2)}) collective-permute-start(bf16[2,1,96,2048]{3,2,1,0:T(8,128)(2,1)} %get-tuple-element.150), channel_id=1, source_target_pairs={{0,2},{1,3},{2,0},{3,1},{4,6},{5,7},{6,4},{7,5},{8,10},{9,11},{10,... | collective-permute-start | bytes 2359304 | tf_op jit(solution)/shard_map/ppermute | solution.py:32
  486.9 19.9 %collective-permute-start.55 = (bf16[1,2,96,2048]{3,2,1,0:T(8,128)(2,1)}, bf16[1,2,96,2048]{3,2,1,0:T(8,128)(2,1)}, u32[]{:S(2)}, u32[]{:S(2)}) collective-permute-start(bf16[1,2,96,2048]{3,2,1,0:T(8,128)(2,1)} %get-tuple-element.151), channel_id=1, source_target_pairs={{0,4},{1,5},{2,6},{3,7},{4,0},{5,1},{6,2},{7,3},{8,12},{9,13},{10,... | collective-permute-start | bytes 2359304 | tf_op jit(solution)/shard_map/ppermute | solution.py:32
  (114 other events, 1009.8 us)
Sparse Core Ops, SparseCore 0:
  10.2 44.3 all-gather.4
  56.7 36.5 all-gather.6
  96.4 106.2 all-gather.8
  204.2 57.4 all-gather.10
  263.8 54.8 reduce-scatter.6
  322.5 100.5 reduce-scatter.4
  425.9 27.6 reduce-scatter.8
  473.0 33.7 reduce-scatter.10
